TPU v7x, 32 devices: a whole 2x2x4 slice. The times are simulated.
32 devices in a mesh: section: 2 (over y), wide: 16 (over z, x, core).
Axes of the slice: x: 2, y: 2, z: 4, core: 2. Of those that a mesh axis runs over, the one named last changes fastest.
Arguments:
- features: bfloat16 [32, 512, 256], P('wide')
- masked: int32 [32, 512], P('wide'), may hold values 0 or 1
- valid: int32 [32, 512], P('wide'), may hold values from 0 to 1, as said below
- kinds: int32 [32], P('wide'), may hold values from 0 to 1, as said below
- embed_weight: bfloat16 [2, 256, 768], replicated, may hold values from -0.375 to 0.375
- embed_vectors: float32 [3, 768], replicated, may hold values from -3 to 3
- pos_embed: float32 [512, 768], replicated, may hold values from -3 to 3
- norm_gains: float32 [2, 2, 768], P('section'), may hold values from 0.5 to 1.5
- vectors: float32 [2, 6, 768], P('section'), may hold values from -2 to 2
- qkv_weight: bfloat16 [2, 768, 2304], P('section'), may hold values from -0.21875 to 0.21875
- out_weight: bfloat16 [2, 768, 768], P('section'), may hold values from -1.75 to 1.75
- up_weight: bfloat16 [2, 768, 3072], P('section'), may hold values from -0.21875 to 0.21875
- up_bias: float32 [2, 3072], P('section'), may hold values from -2 to 2
- down_weight: bfloat16 [2, 3072, 768], P('section'), may hold values from -0.109375 to 0.109375
- cotangent: bfloat16 [32, 512, 768], P('wide'), may hold values from -6 to 6
Outputs:
- output: bfloat16 [32, 512, 768], P('wide', None, 'section')
- feature_grad: bfloat16 [32, 512, 256], P('wide', None, 'section')
- embed_weight_grad: float32 [2, 256, 768], replicated
- embed_vectors_grad: float32 [3, 768], replicated
- pos_grad: float32 [512, 768], replicated
- norm_gains_grad: float32 [2, 2, 768], P('section')
- vectors_grad: float32 [2, 6, 768], P('section')
- qkv_grad: float32 [2, 768, 2304], P('section')
- out_grad: float32 [2, 768, 768], P('section')
- up_grad: float32 [2, 768, 3072], P('section')
- up_bias_grad: float32 [2, 3072], P('section')
- down_grad: float32 [2, 3072, 768], P('section')
- rms: float32 [2, 3], P('section')
Inputs may be any that keep to these rules, and one draw needn't show every extreme that they name: In each clip the valid tokens are its first ones, at least 256 of them and never all. `kinds`: exactly half of the clips are of each kind.
All inputs are finite; a program needn't handle non-finite values. No bound on the sum of `masked` on one device may be relied on, other than what follows from the above.
Results may differ from a plain program's by a relative error of at most 0.015.
Values may be sent and summed in bfloat16 or wider, within the bound.
A program may use at most 320 MiB of HBM per device.

v0:
```python
import jax
import jax.numpy as jnp
from jax import lax
from jax.sharding import PartitionSpec as P

H = 12
HD = 64
MB = 2


EPS = 1e-06
NEG = -1000000000.0


def from_partner(block, axis, apart):
    count = lax.axis_size(axis)
    route = []
    for low in range(count):
        high = low | 1 << apart
        if high != low and high < count:
            route += [(low, high), (high, low)]
    return lax.ppermute(block, axis, route)


def layer_norm(values, gain, shift):
    center = jnp.mean(values, axis=-1, keepdims=True)
    offset = values - center
    spread = jnp.mean(offset * offset, axis=-1, keepdims=True)
    return offset * lax.rsqrt(spread + EPS) * gain + shift


def matmul_plain(left, right):
    return jnp.dot(left, right, preferred_element_type=jnp.float32)


def matmul_left_t(left, right):
    return lax.dot_general(
        left, right, (((0,), (0,)), ((), ())), preferred_element_type=jnp.float32
    )


def matmul_right_t(left, right):
    return lax.dot_general(
        left, right, (((1,), (1,)), ((), ())), preferred_element_type=jnp.float32
    )


def gelu_exact(values):
    return jax.nn.gelu(values, approximate=False)


def head_scores(packed, live_keys):
    length = packed.shape[0]
    heads_view = packed.reshape(length, 3, H, HD)
    scores = jnp.einsum(
        "qhe,khe->hqk", heads_view[:, 0], heads_view[:, 1], preferred_element_type=jnp.float32
    ) * HD ** (-0.5)
    return (heads_view, jnp.where(live_keys[None, None, :] > 0, scores, NEG))


def attend_clip(clip_item):
    packed, live_keys = clip_item
    heads_view, scores = head_scores(packed, live_keys)
    row_top = jnp.max(scores, axis=-1, keepdims=True)
    exp_scores = jnp.exp(scores - row_top)
    row_total = jnp.sum(exp_scores, axis=-1, keepdims=True)
    soft_low = (exp_scores / row_total).astype(jnp.bfloat16)
    context = jnp.einsum(
        "hqk,khe->qhe", soft_low, heads_view[:, 2], preferred_element_type=jnp.float32
    )
    return (context.reshape(packed.shape[0], H * HD), (row_top + jnp.log(row_total))[:, :, 0])


def attend_back_clip(clip_item):
    packed, live_keys, log_total, context_grad = clip_item
    length = packed.shape[0]
    heads_view, scores = head_scores(packed, live_keys)
    soft_weights = jnp.exp(scores - log_total[:, :, None])
    grad_view = context_grad.reshape(length, H, HD)
    weight_grad = jnp.einsum(
        "qhe,khe->hqk", grad_view, heads_view[:, 2], preferred_element_type=jnp.float32
    )
    value_grad = jnp.einsum(
        "hqk,qhe->khe",
        soft_weights.astype(jnp.bfloat16),
        grad_view,
        preferred_element_type=jnp.float32,
    )
    row_delta = jnp.sum(weight_grad * soft_weights, axis=-1, keepdims=True)
    score_grad = (soft_weights * (weight_grad - row_delta)).astype(jnp.bfloat16)
    query_grad = jnp.einsum(
        "hqk,khe->qhe", score_grad, heads_view[:, 1], preferred_element_type=jnp.float32
    ) * HD ** (-0.5)
    key_grad = jnp.einsum(
        "hqk,qhe->khe", score_grad, heads_view[:, 0], preferred_element_type=jnp.float32
    ) * HD ** (-0.5)
    return jnp.concatenate(
        [
            query_grad.reshape(length, H * HD),
            key_grad.reshape(length, H * HD),
            value_grad.reshape(length, H * HD),
        ],
        axis=1,
    )


def layer_forward(layer_in, live_keys, weights):
    gain_rows, vector_rows, attend_weight, project_weight, up_matrix, up_offset, down_matrix = (
        weights
    )
    block_clips, length, model_width = layer_in.shape
    flat_rows = layer_in.reshape(block_clips * length, model_width)
    normed = layer_norm(flat_rows, gain_rows[0], vector_rows[0]).astype(jnp.bfloat16)
    in_offset = jnp.concatenate(
        [vector_rows[1], jnp.zeros((model_width,), jnp.float32), vector_rows[2]]
    )
    packed = (matmul_plain(normed, attend_weight) + in_offset).astype(jnp.bfloat16)
    context, log_total = lax.map(
        attend_clip, (packed.reshape(block_clips, length, 3 * model_width), live_keys)
    )
    context = context.reshape(block_clips * length, model_width).astype(jnp.bfloat16)
    branch = matmul_plain(context, project_weight) + vector_rows[3]
    middle = flat_rows + branch
    hidden_in = layer_norm(middle, gain_rows[1], vector_rows[4]).astype(jnp.bfloat16)
    hidden = matmul_plain(hidden_in, up_matrix) + up_offset
    active = gelu_exact(hidden).astype(jnp.bfloat16)
    mixer = matmul_plain(active, down_matrix) + vector_rows[5]
    layer_out = middle + mixer
    kept_state = (
        flat_rows,
        normed,
        packed,
        log_total,
        context,
        middle,
        hidden_in,
        hidden,
        active,
        live_keys,
    )
    return (layer_out, branch, mixer, kept_state)


def ffn_back(out_grad_rows, kept_state, weights):
    gain_rows, vector_rows, attend_weight, project_weight, up_matrix, up_offset, down_matrix = (
        weights
    )
    flat_rows, normed, packed, log_total, context, middle, hidden_in, hidden, active, live_keys = (
        kept_state
    )
    mix_grad = out_grad_rows.astype(jnp.bfloat16)
    down_part = matmul_left_t(active, mix_grad)
    down_offset_part = jnp.sum(mix_grad.astype(jnp.float32), axis=0)
    active_grad = matmul_right_t(mix_grad, down_matrix)
    gelu_value, gelu_pull = jax.vjp(gelu_exact, hidden)
    hidden_grad = gelu_pull(active_grad)[0].astype(jnp.bfloat16)
    up_part = matmul_left_t(hidden_in, hidden_grad)
    up_offset_part = jnp.sum(hidden_grad.astype(jnp.float32), axis=0)
    hidden_in_grad = matmul_right_t(hidden_grad, up_matrix)
    norm_value, norm_pull = jax.vjp(layer_norm, middle, gain_rows[1], vector_rows[4])
    middle_part, gain_part, shift_part = norm_pull(hidden_in_grad)
    middle_grad = out_grad_rows + middle_part
    return (
        middle_grad,
        (gain_part, jnp.stack([shift_part, down_offset_part]), up_part, up_offset_part, down_part),
    )


def attn_back(middle_grad, kept_state, weights):
    gain_rows, vector_rows, attend_weight, project_weight, up_matrix, up_offset, down_matrix = (
        weights
    )
    flat_rows, normed, packed, log_total, context, middle, hidden_in, hidden, active, live_keys = (
        kept_state
    )
    block_clips = live_keys.shape[0]
    length = live_keys.shape[1]
    model_width = flat_rows.shape[1]
    branch_grad = middle_grad.astype(jnp.bfloat16)
    project_part = matmul_left_t(context, branch_grad)
    project_offset_part = jnp.sum(branch_grad.astype(jnp.float32), axis=0)
    context_grad = matmul_right_t(branch_grad, project_weight).astype(jnp.bfloat16)
    packed_grad = lax.map(
        attend_back_clip,
        (
            packed.reshape(block_clips, length, 3 * model_width),
            live_keys,
            log_total,
            context_grad.reshape(block_clips, length, model_width),
        ),
    )
    packed_grad = packed_grad.reshape(block_clips * length, 3 * model_width).astype(jnp.bfloat16)
    attend_part = matmul_left_t(normed, packed_grad)
    column_sums = jnp.sum(packed_grad.astype(jnp.float32), axis=0)
    normed_grad = matmul_right_t(packed_grad, attend_weight)
    norm_value, norm_pull = jax.vjp(layer_norm, flat_rows, gain_rows[0], vector_rows[0])
    row_part, gain_part, shift_part = norm_pull(normed_grad)
    input_grad = middle_grad + row_part
    vector_part = jnp.stack(
        [shift_part, column_sums[:model_width], column_sums[2 * model_width :], project_offset_part]
    )
    return (input_grad, (gain_part, vector_part, attend_part, project_part))


def embed_forward(feature_rows, mask_rows, kind_rows, embed_weight, embed_vectors, pos_embed):
    chosen = jnp.where(kind_rows[:, None, None] == 0, embed_weight[0], embed_weight[1])
    kind_offset = jnp.where(kind_rows[:, None] == 0, embed_vectors[0], embed_vectors[1])
    lifted = (
        jnp.einsum("ctf,cfd->ctd", feature_rows, chosen, preferred_element_type=jnp.float32)
        + kind_offset[:, None, :]
    )
    start = jnp.where(mask_rows[:, :, None] > 0, embed_vectors[2], lifted) + pos_embed
    return (start, chosen)


def embed_feature_grad(grad_low, mask_rows, chosen):
    lifted_grad = jnp.where(mask_rows[:, :, None] > 0, jnp.zeros_like(grad_low), grad_low)
    return jnp.einsum(
        "ctd,cfd->ctf", lifted_grad, chosen, preferred_element_type=jnp.float32
    ).astype(jnp.bfloat16)


def embed_parts(grad_low, feature_rows, mask_rows, kind_rows, position_keep):
    kept_grad = grad_low.astype(jnp.float32) * position_keep[None, :, None]
    lifted_grad = jnp.where(mask_rows[:, :, None] > 0, 0.0, kept_grad).astype(jnp.bfloat16)
    chosen_grad = jnp.einsum(
        "ctf,ctd->cfd", feature_rows, lifted_grad, preferred_element_type=jnp.float32
    )
    offset_grad = jnp.sum(lifted_grad.astype(jnp.float32), axis=1)
    kind_zero = kind_rows == 0
    weight_part = jnp.stack(
        [
            jnp.sum(jnp.where(kind_zero[:, None, None], chosen_grad, 0.0), axis=0),
            jnp.sum(jnp.where(kind_zero[:, None, None], 0.0, chosen_grad), axis=0),
        ]
    )
    mask_part = jnp.sum(jnp.where(mask_rows[:, :, None] > 0, kept_grad, 0.0), axis=(0, 1))
    vector_part = jnp.stack(
        [
            jnp.sum(jnp.where(kind_zero[:, None], offset_grad, 0.0), axis=0),
            jnp.sum(jnp.where(kind_zero[:, None], 0.0, offset_grad), axis=0),
            mask_part,
        ]
    )
    pos_part = jnp.sum(kept_grad, axis=0)
    return (weight_part, vector_part, pos_part)


def local(
    features,
    masked,
    valid,
    kinds,
    embed_weight,
    embed_vectors,
    pos_embed,
    norm_gains,
    vectors,
    qkv_weight,
    out_weight,
    up_weight,
    up_bias,
    down_weight,
    cotangent,
):
    section_index = lax.axis_index("section")
    is_first = section_index == 0
    clip_total, length, feat_width = features.shape
    model_width = pos_embed.shape[1]
    half_width = model_width // 2
    half_feat = feat_width // 2
    block_clips = clip_total // MB
    weights = (
        norm_gains[0],
        vectors[0],
        qkv_weight[0],
        out_weight[0],
        up_weight[0],
        up_bias[0],
        down_weight[0],
    )
    live_all = valid.astype(jnp.float32)
    position_keep = (jnp.arange(length, dtype=jnp.int32) // (length // 2) == section_index).astype(
        jnp.float32
    )

    def block_rows(source, block_index):
        return lax.dynamic_slice_in_dim(source, block_index * block_clips, block_clips, 0)

    received = jnp.zeros((block_clips, length, model_width), jnp.bfloat16)
    kept_ticks = []
    output_blocks = []
    square_sums = jnp.zeros((3,), jnp.float32)
    for forward_tick in range(MB + 1):
        offset_tick = forward_tick - section_index
        block_index = jnp.clip(offset_tick, 0, MB - 1)
        tick_flag = ((offset_tick >= 0) & (offset_tick < MB)).astype(jnp.float32)
        feature_rows = block_rows(features, block_index)
        mask_rows = block_rows(masked, block_index)
        kind_rows = block_rows(kinds, block_index)
        live_keys = block_rows(live_all, block_index)
        start, chosen = embed_forward(
            feature_rows, mask_rows, kind_rows, embed_weight, embed_vectors, pos_embed
        )
        layer_in = jnp.where(is_first, start, received.astype(jnp.float32))
        layer_out, branch, mixer, kept_state = layer_forward(layer_in, live_keys, weights)
        token_flags = live_keys.reshape(-1, 1) * tick_flag
        square_sums = square_sums + jnp.stack(
            [
                jnp.sum(token_flags * layer_out * layer_out),
                jnp.sum(token_flags * branch * branch),
                jnp.sum(token_flags * mixer * mixer),
            ]
        )
        sent_rows = layer_out.astype(jnp.bfloat16).reshape(block_clips, length, model_width)
        received = from_partner(sent_rows, "section", 0)
        if forward_tick >= 1:
            full_out = jnp.where(is_first, received, sent_rows)
            output_blocks.append(
                lax.dynamic_slice_in_dim(full_out, section_index * half_width, half_width, 2)
            )
        kept_ticks.append((kept_state, mask_rows, chosen))
    valid_count = jnp.sum(live_all)
    ffn_accum = (
        jnp.zeros((model_width,), jnp.float32),
        jnp.zeros((2, model_width), jnp.float32),
        jnp.zeros(up_weight.shape[1:], jnp.float32),
        jnp.zeros(up_bias.shape[1:], jnp.float32),
        jnp.zeros(down_weight.shape[1:], jnp.float32),
    )
    attn_accum = (
        jnp.zeros((model_width,), jnp.float32),
        jnp.zeros((4, model_width), jnp.float32),
        jnp.zeros(qkv_weight.shape[1:], jnp.float32),
        jnp.zeros(out_weight.shape[1:], jnp.float32),
    )
    embed_accum = (
        jnp.zeros(embed_weight.shape, jnp.float32),
        jnp.zeros(embed_vectors.shape, jnp.float32),
        jnp.zeros(pos_embed.shape, jnp.float32),
    )
    back_in = jnp.zeros((block_clips, length, model_width), jnp.bfloat16)
    feature_blocks = []
    for back_tick in range(MB + 1):
        kept_state, mask_rows, chosen = kept_ticks[MB - back_tick]
        offset_tick = MB - back_tick - section_index
        block_index = jnp.clip(offset_tick, 0, MB - 1)
        tick_flag = ((offset_tick >= 0) & (offset_tick < MB)).astype(jnp.float32)
        cot_rows = block_rows(cotangent, block_index)
        out_grad_rows = jnp.where(
            is_first, back_in.astype(jnp.float32), cot_rows.astype(jnp.float32)
        ).reshape(block_clips * length, model_width)
        middle_grad, ffn_part = ffn_back(out_grad_rows, kept_state, weights)
        ffn_accum = tuple((accum + tick_flag * part for accum, part in zip(ffn_accum, ffn_part)))
        input_grad, attn_part = attn_back(middle_grad, kept_state, weights)
        attn_accum = tuple((accum + tick_flag * part for accum, part in zip(attn_accum, attn_part)))
        own_low = input_grad.astype(jnp.bfloat16).reshape(block_clips, length, model_width)
        feature_grad = embed_feature_grad(own_low, mask_rows, chosen)
        joined_send = jnp.concatenate([own_low, feature_grad[:, :, half_feat:]], axis=2)
        joined_back = from_partner(joined_send, "section", 0)
        back_in = joined_back[:, :, :model_width]
        if back_tick >= 1:
            feature_blocks.append(
                jnp.where(is_first, feature_grad[:, :, :half_feat], joined_back[:, :, model_width:])
            )
            part_index = MB - back_tick
            grad_low = jnp.where(is_first, own_low, back_in)
            embed_part = embed_parts(
                grad_low,
                block_rows(features, part_index),
                block_rows(masked, part_index),
                block_rows(kinds, part_index),
                position_keep,
            )
            embed_accum = tuple((accum + part for accum, part in zip(embed_accum, embed_part)))
    layer_total = lax.psum(
        (
            attn_accum[0],
            attn_accum[1],
            attn_accum[2],
            attn_accum[3],
            ffn_accum[0],
            ffn_accum[1],
            ffn_accum[2],
            ffn_accum[3],
            ffn_accum[4],
            square_sums,
            valid_count,
        ),
        "wide",
    )
    (
        gain_one,
        attn_vectors,
        attend_total,
        project_total,
        gain_two,
        ffn_vectors,
        up_total,
        up_offset_total,
        down_total,
        square_total,
        count_total,
    ) = layer_total
    embed_total = lax.psum((embed_accum[0], embed_accum[1], embed_accum[2]), ("section", "wide"))
    output = jnp.concatenate(output_blocks, axis=0)
    feature_out = jnp.concatenate(feature_blocks[::-1], axis=0)
    gains_out = jnp.stack([gain_one, gain_two])[None]
    vectors_out = jnp.stack(
        [
            attn_vectors[0],
            attn_vectors[1],
            attn_vectors[2],
            attn_vectors[3],
            ffn_vectors[0],
            ffn_vectors[1],
        ]
    )[None]
    rms_out = jnp.sqrt(square_total / (count_total * model_width))[None]
    return (
        output,
        feature_out,
        embed_total[0],
        embed_total[1],
        embed_total[2],
        gains_out,
        vectors_out,
        attend_total[None],
        project_total[None],
        up_total[None],
        up_offset_total[None],
        down_total[None],
        rms_out,
    )


def solution(mesh):
    return jax.shard_map(
        local,
        mesh=mesh,
        in_specs=(
            P("wide", None, None),
            P("wide", None),
            P("wide", None),
            P("wide"),
            P(),
            P(),
            P(),
            P("section", None, None),
            P("section", None, None),
            P("section", None, None),
            P("section", None, None),
            P("section", None, None),
            P("section", None),
            P("section", None, None),
            P("wide", None, None),
        ),
        out_specs=(
            P("wide", None, "section"),
            P("wide", None, "section"),
            P(),
            P(),
            P(),
            P("section", None, None),
            P("section", None, None),
            P("section", None, None),
            P("section", None, None),
            P("section", None, None),
            P("section", None),
            P("section", None, None),
            P("section", None),
        ),
        check_vma=False,
    )
```

profile of v0, /device:TPU:0, one launch (start us, length us, event | category | flops | bytes accessed | tf_op | source)
XLA Modules:
  0.0 1127.2 jit_solution(17980174379610667172)
XLA Ops:
  24.4 4.6 copy.59
  29.0 4.0 fusion.228
  37.7 3.8 fusion.99
  44.7 20.0 %multiply_convert_fusion.5 = (bf16[512,3072]{1,0:T(8,128)(2,1)S(1)}, f32[512,3072]{1,0:T(8,128)}, f32[512,3072]{1,0:T(8,128)}) fusion(f32[3072]{0:T(1024)S(1)} %bitcast.497, bf16[1,768,3072]{2,1,0:T(8,128)(2,1)} %param.26, f32[512,768]{1,0:T(8,128)S(1)} %get-tuple-element.244, f32[768]{0:T(1024)S(1)} %copy-done.147, f32[768]{0:T(1024)S(1)} %get-tuple-element.185, ...), kind=kOutput, calls=%fused_computation.71 | convolution fusion | flops 2521694208 | bytes 22042624 | tf_op jit(solution)/shard_map/dot_general | solution.py:33
  70.8 17.5 %collective-permute-done = bf16[1,512,768]{2,1,0:T(8,128)(2,1)S(1)} collective-permute-done((bf16[1,512,768]{2,1,0:T(8,128)(2,1)S(1)}, bf16[1,512,768]{2,1,0:T(8,128)(2,1)S(1)}, u32[]{:S(2)}, u32[]{:S(2)}) %collective-permute-start) | collective-permute-done | bytes 786464 | tf_op jit(solution)/shard_map/ppermute | solution.py:22
  94.4 4.3 copy.61
  98.7 4.0 fusion.230
  107.4 3.9 fusion.98
  114.6 19.5 %multiply_convert_fusion.4 = (bf16[512,3072]{1,0:T(8,128)(2,1)S(1)}, f32[512,3072]{1,0:T(8,128)}, f32[512,3072]{1,0:T(8,128)}) fusion(f32[3072]{0:T(1024)S(1)} %bitcast.498, bf16[1,768,3072]{2,1,0:T(8,128)(2,1)} %param.26, f32[512,768]{1,0:T(8,128)S(1)} %get-tuple-element.240, f32[512]{0:T(512)S(1)} %fusion.188, f32[512]{0:T(512)S(1)} %broadcast_multiply_fusion.5, ...), kind=kOutput, calls=%fused_computation.58 | convolution fusion | flops 2521694208 | bytes 22042624 | tf_op jit(solution)/shard_map/dot_general | solution.py:33
  145.2 12.0 %collective-permute-done.1 = bf16[1,512,768]{2,1,0:T(8,128)(2,1)} collective-permute-done((bf16[1,512,768]{2,1,0:T(8,128)(2,1)}, bf16[1,512,768]{2,1,0:T(8,128)(2,1)}, u32[]{:S(2)}, u32[]{:S(2)}) %collective-permute-start.1) | collective-permute-done | bytes 786464 | tf_op jit(solution)/shard_map/ppermute | solution.py:22
  165.1 4.5 copy.63
  169.6 4.0 fusion.232
  184.1 20.0 %multiply_convert_fusion.3 = (bf16[512,3072]{1,0:T(8,128)(2,1)S(1)}, f32[512,3072]{1,0:T(8,128)}, f32[512,3072]{1,0:T(8,128)}) fusion(f32[3072]{0:T(1024)S(1)} %bitcast.499, bf16[1,768,3072]{2,1,0:T(8,128)(2,1)} %param.26, f32[512,768]{1,0:T(8,128)S(1)} %get-tuple-element.236, f32[512]{0:T(512)S(1)} %fusion.190, f32[512]{0:T(512)S(1)} %broadcast_multiply_fusion.3, ...), kind=kOutput, calls=%fused_computation.45 | convolution fusion | flops 2521694208 | bytes 22042624 | tf_op jit(solution)/shard_map/dot_general | solution.py:33
  204.0 10.6 convert_reduce_fusion.2
  214.6 5.9 fusion.52
  220.6 4.9 fusion.84
  232.2 6.9 fusion.88
  239.2 9.4 multiply_reduce_fusion.2
  248.6 7.0 multiply_convert_fusion.2
  262.4 5.3 fusion.203
  267.6 5.2 fusion.137
  279.1 5.8 fusion.209
  284.9 11.2 collective-permute-done.3
  296.1 9.5 convert_reduce_fusion.1
  305.6 7.3 fusion.81
  319.7 6.9 fusion.91
  326.6 9.4 multiply_reduce_fusion.1
  336.1 7.2 multiply_convert_fusion.1
  350.1 5.3 fusion.202
  359.8 5.1 fusion.163
  367.1 5.8 fusion.208
  372.8 5.3 collective-permute-done.4
  378.2 9.5 convert_reduce_fusion
  387.7 7.5 fusion.78
  402.4 6.9 fusion.94
  409.4 9.4 multiply_reduce_fusion
  418.8 7.0 multiply_convert_fusion
  437.4 8.6 add_bitcast_fusion
  446.1 10.8 add_bitcast_fusion.2
  464.2 5.5 add_bitcast_fusion.3
  469.7 11.0 add_bitcast_fusion.1
  487.0 12.6 %collective-permute-done.2 = bf16[1,512,768]{2,1,0:T(8,128)(2,1)} collective-permute-done((bf16[1,512,768]{2,1,0:T(8,128)(2,1)}, bf16[1,512,768]{2,1,0:T(8,128)(2,1)}, u32[]{:S(2)}, u32[]{:S(2)}) %collective-permute-start.2) | collective-permute-done | bytes 786464 | tf_op jit(solution)/shard_map/ppermute | solution.py:22
  503.9 6.4 fusion.191
  511.6 59.0 %all-reduce.1 = (f32[1,768]{1,0:T(1,128)}, f32[1,768]{1,0:T(1,128)}, f32[2,768]{1,0:T(2,128)}, f32[4,768]{1,0:T(4,128)}, f32[1,3072]{1,0:T(1,128)}, /*index=5*/f32[3]{0:T(128)}, f32[]{:T(128)}) all-reduce(f32[1,768]{1,0:T(1,128)} %stack.142, f32[1,768]{1,0:T(1,128)} %stack.141, ...), channel_id=1, replica_groups=mesh['section'=2,'wide'=16] {'wide'}, use_global_device_ids=true, to_apply=%region_47.48 | all-reduce | flops 9220 | bytes 73760 | tf_op jit(solution)/shard_map/psum | solution.py:376
  578.9 37.2 %psum.99 = f32[3,768]{1,0:T(4,128)} all-reduce(f32[3,768]{1,0:T(4,128)S(1)} %maximum_add_fusion.1), channel_id=1, replica_groups=mesh['section'=2,'wide'=16] {'section','wide'}, use_global_device_ids=true, to_apply=%region_38.39 | all-reduce | flops 2304 | bytes 18432 | tf_op jit(solution)/shard_map/psum | solution.py:405
  621.7 474.4 %all-reduce.8.cloned.1.call-done = (f32[1,768,2304]{2,1,0:T(8,128)}, f32[1,768,768]{2,1,0:T(8,128)}, f32[1,768,3072]{2,1,0:T(8,128)}, f32[1,3072,768]{2,1,0:T(8,128)}) async-done(((f32[1,768,2304]{2,1,0:T(8,128)}, f32[1,768,768]{2,1,0:T(8,128)}, f32[1,768,3072]{2,1,0:T(8,128)}, f32[1,3072,768]{2,1,0:T(8,128)}), (f32[1,768,2304]{2,1,0:T(8,128)}, f32[1,768,768]{2,1,0:T(8,128)}, f32[1,768,3072]{2,1,0:T(8,128)}, ...) | async-done | bytes 28311568 | tf_op jit(solution)/shard_map/psum | solution.py:376
  1098.8 6.6 copy.103
  1106.8 9.3 copy.105
  (629 shorter events, 168.8 us)
Async XLA Ops:
  7.2 611.5 %all-reduce.6.cloned.1.call-start = ((), (), s32[]{:S(2)}) async-start(), calls=%async_computation | async-start | bytes 6291456 | tf_op jit(solution)/shard_map/psum | solution.py:405
  41.5 23.2 %slice-start.15 = ((s8[4718592]{0:T(1024)(128)(4,1)}), s8[4194304]{0:T(1024)(128)(4,1)S(1)}, s32[]{:S(2)}) async-start(s8[4718592]{0:T(1024)(128)(4,1)} %bitcast.489), calls=%async_computation.17 | async-start | bytes 8388608
  43.6 24.0 %copy-start.4 = (f32[512,768]{1,0:T(8,128)}, f32[512,768]{1,0:T(8,128)S(1)}, u32[]{:S(2)}) copy-start(f32[512,768]{1,0:T(8,128)S(1)} %get-tuple-element.244) | copy-start | bytes 4718596
  43.6 21.2 %copy-start.112 = (f32[512]{0:T(512)}, f32[512]{0:T(512)S(1)}, u32[]{:S(2)}) copy-start(f32[512]{0:T(512)S(1)} %broadcast_multiply_fusion.7) | copy-start | bytes 6148
  43.9 20.9 %copy-start.118 = (f32[512]{0:T(512)}, f32[512]{0:T(512)S(1)}, u32[]{:S(2)}) copy-start(f32[512]{0:T(512)S(1)} %fusion.186) | copy-start | bytes 6148
  44.7 20.1 %slice-start.16 = ((s8[4718592]{0:T(1024)(128)(4,1)}), s8[524288]{0:T(1024)(128)(4,1)S(1)}, s32[]{:S(2)}) async-start(s8[4718592]{0:T(1024)(128)(4,1)} %bitcast.489), calls=%async_computation.18 | async-start | bytes 1048576
  67.5 21.6 %copy-start.79 = (f32[512,768]{1,0:T(8,128)}, f32[512,768]{1,0:T(8,128)S(1)}, u32[]{:S(2)}) copy-start(f32[512,768]{1,0:T(8,128)S(1)} %fusion.46) | copy-start | bytes 4718596
  67.5 20.9 %copy-start.58 = (f32[512,768]{1,0:T(8,128)S(1)}, f32[512,768]{1,0:T(8,128)}, u32[]{:S(2)}) copy-start(f32[512,768]{1,0:T(8,128)} %param.21) | copy-start | bytes 4718596
  67.5 20.9 %copy-start.85 = (bf16[2,256,768]{2,1,0:T(8,128)(2,1)S(1)}, bf16[2,256,768]{2,1,0:T(8,128)(2,1)}, u32[]{:S(2)}) copy-start(bf16[2,256,768]{2,1,0:T(8,128)(2,1)} %param.19) | copy-start | bytes 2359300
  67.5 20.9 %copy-start.89 = (bf16[2,512,256]{2,1,0:T(8,128)(2,1)S(1)}, bf16[2,512,256]{2,1,0:T(8,128)(2,1)}, u32[]{:S(2)}) copy-start(bf16[2,512,256]{2,1,0:T(8,128)(2,1)} %param.15) | copy-start | bytes 1572868
  67.5 20.9 %copy-start.111 = (f32[768]{0:T(1024)S(1)}, f32[768]{0:T(1024)}, u32[]{:S(2)}) copy-start(f32[768]{0:T(1024)} %copy-done.110) | copy-start | bytes 9220
  67.5 20.9 %copy-start.155 = (f32[768]{0:T(1024)S(1)}, f32[768]{0:T(1024)}, u32[]{:S(2)}) copy-start(f32[768]{0:T(1024)} %get-tuple-element.183) | copy-start | bytes 9220
  67.5 20.9 %copy-start.188 = (pred[512]{0:T(512)(128)(4,1)S(1)}, pred[512]{0:T(512)(128)(4,1)}, u32[]{:S(2)}) copy-start(pred[512]{0:T(512)(128)(4,1)} %get-tuple-element.190) | copy-start | bytes 1540
  67.8 23.0 %copy-start.157 = (f32[2304]{0:T(1024)S(1)}, f32[2304]{0:T(1024)}, u32[]{:S(2)}) copy-start(f32[2304]{0:T(1024)} %copy-done.156) | copy-start | bytes 27652
  67.8 20.6 %collective-permute-start = (bf16[1,512,768]{2,1,0:T(8,128)(2,1)S(1)}, bf16[1,512,768]{2,1,0:T(8,128)(2,1)S(1)}, u32[]{:S(2)}, u32[]{:S(2)}) collective-permute-start(bf16[1,512,768]{2,1,0:T(8,128)(2,1)S(1)} %convert_bitcast_fusion.2), channel_id=1, source_target_pairs={{0,16},{16,0},{1,17},{17,1},{2,18},{18,2},{3,19},{19,3},{4,20},{20... | collective-permute-start | bytes 2359304 | tf_op jit(solution)/shard_map/ppermute | solution.py:22
  111.4 22.7 %slice-start.17 = ((s8[4718592]{0:T(1024)(128)(4,1)}), s8[4194304]{0:T(1024)(128)(4,1)S(1)}, s32[]{:S(2)}) async-start(s8[4718592]{0:T(1024)(128)(4,1)} %bitcast.491), calls=%async_computation.19 | async-start | bytes 8388608
  113.5 23.3 %copy-start.14 = (f32[512,768]{1,0:T(8,128)}, f32[512,768]{1,0:T(8,128)S(1)}, u32[]{:S(2)}) copy-start(f32[512,768]{1,0:T(8,128)S(1)} %get-tuple-element.240) | copy-start | bytes 4718596
  113.5 20.6 %copy-start.121 = (f32[512]{0:T(512)}, f32[512]{0:T(512)S(1)}, u32[]{:S(2)}) copy-start(f32[512]{0:T(512)S(1)} %broadcast_multiply_fusion.5) | copy-start | bytes 6148
  114.6 19.5 %copy-start.162 = (f32[512]{0:T(512)}, f32[512]{0:T(512)S(1)}, u32[]{:S(2)}) copy-start(f32[512]{0:T(512)S(1)} %fusion.188) | copy-start | bytes 6148
  114.6 19.5 %slice-start.18 = ((s8[4718592]{0:T(1024)(128)(4,1)}), s8[524288]{0:T(1024)(128)(4,1)S(1)}, s32[]{:S(2)}) async-start(s8[4718592]{0:T(1024)(128)(4,1)} %bitcast.491), calls=%async_computation.20 | async-start | bytes 1048576
  138.2 19.1 %collective-permute-start.1 = (bf16[1,512,768]{2,1,0:T(8,128)(2,1)}, bf16[1,512,768]{2,1,0:T(8,128)(2,1)}, u32[]{:S(2)}, u32[]{:S(2)}) collective-permute-start(bf16[1,512,768]{2,1,0:T(8,128)(2,1)} %convert_bitcast_fusion.1), channel_id=1, source_target_pairs={{0,16},{16,0},{1,17},{17,1},{2,18},{18,2},{3,19},{19,3},{4,20},{20... | collective-permute-start | bytes 2359304 | tf_op jit(solution)/shard_map/ppermute | solution.py:22
  182.7 21.3 %slice-start.19 = ((s8[4718592]{0:T(1024)(128)(4,1)}), s8[4194304]{0:T(1024)(128)(4,1)S(1)}, s32[]{:S(2)}) async-start(s8[4718592]{0:T(1024)(128)(4,1)} %bitcast.493), calls=%async_computation.21 | async-start | bytes 8388608
  183.7 41.9 %copy-start.31 = (f32[512,768]{1,0:T(8,128)}, f32[512,768]{1,0:T(8,128)S(1)}, u32[]{:S(2)}) copy-start(f32[512,768]{1,0:T(8,128)S(1)} %get-tuple-element.236) | copy-start | bytes 4718596
  183.7 41.8 %copy-start.126 = (f32[512]{0:T(512)}, f32[512]{0:T(512)S(1)}, u32[]{:S(2)}) copy-start(f32[512]{0:T(512)S(1)} %broadcast_multiply_fusion.3) | copy-start | bytes 6148
  184.0 41.5 %copy-start.167 = (f32[512]{0:T(512)}, f32[512]{0:T(512)S(1)}, u32[]{:S(2)}) copy-start(f32[512]{0:T(512)S(1)} %fusion.190) | copy-start | bytes 6148
  184.0 20.0 %copy-start.10 = (bf16[2,512,768]{2,1,0:T(8,128)(2,1)S(1)}, bf16[2,512,768]{2,1,0:T(8,128)(2,1)}, u32[]{:S(2)}) copy-start(bf16[2,512,768]{2,1,0:T(8,128)(2,1)} %param.29) | copy-start | bytes 4718596
  184.0 20.0 %slice-start.20 = ((s8[4718592]{0:T(1024)(128)(4,1)}), s8[524288]{0:T(1024)(128)(4,1)S(1)}, s32[]{:S(2)}) async-start(s8[4718592]{0:T(1024)(128)(4,1)} %bitcast.493), calls=%async_computation.22 | async-start | bytes 1048576
  239.1 23.2 %copy-start.65 = (bf16[12,64,512]{2,1,0:T(8,128)(2,1)}, bf16[12,64,512]{2,1,0:T(8,128)(2,1)S(1)}, u32[]{:S(2)}) copy-start(bf16[12,64,512]{2,1,0:T(8,128)(2,1)S(1)} %fusion.88) | copy-start | bytes 2359300
  275.2 20.8 %slice-start.21 = ((s8[4718592]{0:T(1024)(128)(4,1)}), s8[4194304]{0:T(1024)(128)(4,1)S(1)}, s32[]{:S(2)}) async-start(s8[4718592]{0:T(1024)(128)(4,1)} %bitcast.495), calls=%async_computation.23 | async-start | bytes 8388608
  275.3 20.7 %collective-permute-start.3 = (bf16[1,512,896]{2,1,0:T(8,128)(2,1)S(1)}, bf16[1,512,896]{2,1,0:T(8,128)(2,1)S(1)}, u32[]{:S(2)}, u32[]{:S(2)}) collective-permute-start(bf16[1,512,896]{2,1,0:T(8,128)(2,1)S(1)} %pad_maximum_fusion.3), channel_id=1, source_target_pairs={{0,16},{16,0},{1,17},{17,1},{2,18},{18,2},{3,19},{19,3},{4,20},{20... | collective-permute-start | bytes 2752520 | tf_op jit(solution)/shard_map/ppermute | solution.py:22
  326.6 23.4 %copy-start.66 = (bf16[12,64,512]{2,1,0:T(8,128)(2,1)}, bf16[12,64,512]{2,1,0:T(8,128)(2,1)S(1)}, u32[]{:S(2)}) copy-start(bf16[12,64,512]{2,1,0:T(8,128)(2,1)S(1)} %fusion.91) | copy-start | bytes 2359300
  358.4 19.7 %collective-permute-start.4 = (bf16[1,512,896]{2,1,0:T(8,128)(2,1)S(1)}, bf16[1,512,896]{2,1,0:T(8,128)(2,1)S(1)}, u32[]{:S(2)}, u32[]{:S(2)}) collective-permute-start(bf16[1,512,896]{2,1,0:T(8,128)(2,1)S(1)} %pad_maximum_fusion.4), channel_id=1, source_target_pairs={{0,16},{16,0},{1,17},{17,1},{2,18},{18,2},{3,19},{19,3},{4,20},{20... | collective-permute-start | bytes 2752520 | tf_op jit(solution)/shard_map/ppermute | solution.py:22
  409.4 36.7 %copy-start.49 = (bf16[12,64,512]{2,1,0:T(8,128)(2,1)}, bf16[12,64,512]{2,1,0:T(8,128)(2,1)S(1)}, u32[]{:S(2)}) copy-start(bf16[12,64,512]{2,1,0:T(8,128)(2,1)S(1)} %fusion.94) | copy-start | bytes 2359300
  436.1 20.8 %collective-permute-start.5 = (bf16[1,512,896]{2,1,0:T(8,128)(2,1)}, bf16[1,512,896]{2,1,0:T(8,128)(2,1)}, u32[]{:S(2)}, u32[]{:S(2)}) collective-permute-start(bf16[1,512,896]{2,1,0:T(8,128)(2,1)} %pad_maximum_fusion.5), channel_id=1, source_target_pairs={{0,16},{16,0},{1,17},{17,1},{2,18},{18,2},{3,19},{19,3},{4,20},{20... | collective-permute-start | bytes 2752520 | tf_op jit(solution)/shard_map/ppermute | solution.py:22
  464.1 632.0 %all-reduce.8.cloned.1.call-start = ((), (), s32[]{:S(2)}) async-start(), calls=%async_computation.1 | async-start | bytes 56623104 | tf_op jit(solution)/shard_map/psum | solution.py:376
  480.7 18.8 %collective-permute-start.2 = (bf16[1,512,768]{2,1,0:T(8,128)(2,1)}, bf16[1,512,768]{2,1,0:T(8,128)(2,1)}, u32[]{:S(2)}, u32[]{:S(2)}) collective-permute-start(bf16[1,512,768]{2,1,0:T(8,128)(2,1)} %get-tuple-element.245), channel_id=1, source_target_pairs={{0,16},{16,0},{1,17},{17,1},{2,18},{18,2},{3,19},{19,3},{4,20},{20... | collective-permute-start | bytes 2359304 | tf_op jit(solution)/shard_map/ppermute | solution.py:22
  482.5 19.2 %copy-start.172 = (f32[768]{0:T(1024)S(1)}, f32[768]{0:T(1024)}, u32[]{:S(2)}) copy-start(f32[768]{0:T(1024)} %get-tuple-element.161) | copy-start | bytes 9220
  482.5 19.2 %copy-start.154 = (f32[768]{0:T(1024)S(1)}, f32[768]{0:T(1024)}, u32[]{:S(2)}) copy-start(f32[768]{0:T(1024)} %get-tuple-element.215) | copy-start | bytes 9220
  482.5 19.2 %copy-start.57 = (bf16[12,64,512]{2,1,0:T(8,128)(2,1)S(1)}, bf16[12,64,512]{2,1,0:T(8,128)(2,1)}, u32[]{:S(2)}) copy-start(bf16[12,64,512]{2,1,0:T(8,128)(2,1)} %copy-done.56) | copy-start | bytes 2359300
  482.5 19.2 %copy-start.67 = (bf16[12,64,512]{2,1,0:T(8,128)(2,1)S(1)}, bf16[12,64,512]{2,1,0:T(8,128)(2,1)}, u32[]{:S(2)}) copy-start(bf16[12,64,512]{2,1,0:T(8,128)(2,1)} %copy-done.66) | copy-start | bytes 2359300
  482.5 19.2 %copy-start.77 = (bf16[12,64,512]{2,1,0:T(8,128)(2,1)S(1)}, bf16[12,64,512]{2,1,0:T(8,128)(2,1)}, u32[]{:S(2)}) copy-start(bf16[12,64,512]{2,1,0:T(8,128)(2,1)} %copy-done.76) | copy-start | bytes 2359300
  485.5 17.9 %copy-start.146 = (f32[768]{0:T(1024)S(1)}, f32[768]{0:T(1024)}, u32[]{:S(2)}) copy-start(f32[768]{0:T(1024)} %get-tuple-element.169) | copy-start | bytes 9220
  485.5 17.9 %copy-start.144 = (f32[768]{0:T(1024)S(1)}, f32[768]{0:T(1024)}, u32[]{:S(2)}) copy-start(f32[768]{0:T(1024)} %get-tuple-element.168) | copy-start | bytes 9220
  485.5 17.9 %copy-start.174 = (f32[768]{0:T(1024)S(1)}, f32[768]{0:T(1024)}, u32[]{:S(2)}) copy-start(f32[768]{0:T(1024)} %get-tuple-element.164) | copy-start | bytes 9220
  485.5 17.9 %copy-start.143 = (f32[768]{0:T(1024)S(1)}, f32[768]{0:T(1024)}, u32[]{:S(2)}) copy-start(f32[768]{0:T(1024)} %get-tuple-element.246) | copy-start | bytes 9220
  485.6 17.9 %copy-start.36 = (bf16[12,64,512]{2,1,0:T(8,128)(2,1)S(1)}, bf16[12,64,512]{2,1,0:T(8,128)(2,1)}, u32[]{:S(2)}) copy-start(bf16[12,64,512]{2,1,0:T(8,128)(2,1)} %copy-done.35) | copy-start | bytes 2359300
  485.6 17.9 %copy-start.50 = (bf16[12,64,512]{2,1,0:T(8,128)(2,1)S(1)}, bf16[12,64,512]{2,1,0:T(8,128)(2,1)}, u32[]{:S(2)}) copy-start(bf16[12,64,512]{2,1,0:T(8,128)(2,1)} %copy-done.49) | copy-start | bytes 2359300
  485.6 17.9 %copy-start.52 = (bf16[12,64,512]{2,1,0:T(8,128)(2,1)S(1)}, bf16[12,64,512]{2,1,0:T(8,128)(2,1)}, u32[]{:S(2)}) copy-start(bf16[12,64,512]{2,1,0:T(8,128)(2,1)} %copy-done.51) | copy-start | bytes 2359300
  (185 other events, 1112.5 us)
Sparse Core Ops, SparseCore 0:
  464.2 138.5 all-reduce.5
  609.5 486.6 all-reduce.7
where the time goes:
time: 1130 us
  waiting for transfers between devices  533 us (47%)
  matrix products  312 us (28%)
  blocking collectives  96.2 us (9%)
  local copies, waits for them, and re-layouts  78.8 us (7%)
  other arithmetic  77 us (7%)
  between operations  21 us (2%)
    psum x1, waiting for transfers between devices, local(): lax.psum((attn_accum[0], attn_accum[1], attn_accum[2], attn_accum[3], ffn...  474 us
    dot_general x12, matrix products, matmul_plain(): return jnp.dot(left, right, preferred_element_type=jnp.float32)  85.3 us
    dot_general x12, matrix products, matmul_left_t(): lax.dot_general(left, right, (((0,), (0,)), ((), ())), preferred_element_...  72.5 us
    dot_general x12, matrix products, matmul_right_t(): lax.dot_general(left, right, (((1,), (1,)), ((), ())), preferred_element_...  64.4 us
    psum x1, blocking collectives, local(): lax.psum((attn_accum[0], attn_accum[1], attn_accum[2], attn_accum[3], ffn...  59 us
    ppermute x6, waiting for transfers between devices, from_partner(): return lax.ppermute(block, axis, route)  58.6 us
    unnamed x456, local copies, waits for them, and re-layouts  50.9 us
    psum x1, blocking collectives, local(): lax.psum((embed_accum[0], embed_accum[1], embed_accum[2]), ('section', 'w...  37.2 us
  transfers between devices with their start and end apart: 8, of which 6 were waited for; matrix products, arithmetic and copies ran while one was open for 8% of the time, Pallas kernels for 0%

commit v1 on v0

--- a/solution.py
+++ b/solution.py
@@ -1,6 +1,10 @@
+import functools
+
 import jax
 import jax.numpy as jnp
 from jax import lax
+from jax.experimental import pallas as pl
+from jax.experimental.pallas import tpu as pltpu
 from jax.sharding import PartitionSpec as P
 
 H = 12
@@ -10,6 +14,202 @@
 
 EPS = 1e-06
 NEG = -1000000000.0
+
+
+MESH = pl.DeviceIdType.MESH
+SMALL = 16
+
+
+def ring_kernel(n, rows, tail, g_ref, o_ref, e_ref, own, part, ring, sems):
+    (own_sem, part_send, part_recv, ring_send, ring_recv, gather_send, gather_recv,
+     pair_send, pair_recv, keep_sem, cross_send, cross_recv) = sems
+    columns = g_ref.shape[2] // 2
+    me = lax.axis_index("wide")
+    section = lax.axis_index("section")
+    chip, core = me // 2, me % 2
+    place = jnp.where(chip % 2 == 0, chip // 2, n - 1 - chip // 2)
+
+    def member(position):
+        position = lax.rem(position + 2 * n, n)
+        return jnp.where(2 * position < n, 2 * position, 2 * (n - 1 - position) + 1) * 2 + core
+
+    right, left = member(place + 1), member(place - 1)
+    other = chip * 2 + 1 - core
+    target = (right, left)
+
+    barrier = pltpu.get_barrier_semaphore()
+    for peer in (right, left, other):
+        pl.semaphore_signal(barrier, inc=1, device_id={"wide": peer}, device_id_type=MESH)
+    pl.semaphore_signal(barrier, inc=1, device_id={"section": 1 - section}, device_id_type=MESH)
+    pl.semaphore_wait(barrier, 4)
+
+    half = -(-rows // 32) * 16
+    spans = ((0, half), (half, rows - half))
+    streams = [(q, d) for q in range(2) for d in range(2)]
+
+    def turn(position):
+        return lax.rem(position + 2 * n, n)
+
+    def reduce_at(d, step):
+        return turn(place - step) if d == 0 else turn(place + step)
+
+    def gather_at(d, index):
+        return turn(place + 1 - index) if d == 0 else turn(place - 1 + index)
+
+    def span(q):
+        return pl.ds(*spans[q])
+
+    def cols(d):
+        return pl.ds(d * columns, columns)
+
+    def remote(src, dst, send, recv, device):
+        return pltpu.make_async_remote_copy(
+            src_ref=src, dst_ref=dst, send_sem=send, recv_sem=recv,
+            device_id=device, device_id_type=MESH)
+
+    def own_copy(q, d, s):
+        return pltpu.make_async_copy(
+            g_ref.at[reduce_at(d, s) * 2 + core, span(q), cols(d)],
+            own.at[d, s, span(q)], own_sem.at[d, q, s])
+
+    def part_copy(q, d, s):
+        return remote(
+            g_ref.at[reduce_at(d, s) * 2 + 1 - core, span(q), cols(d)],
+            part.at[d, s, span(q)], part_send.at[d, q, s], part_recv.at[d, q, s],
+            {"wide": other})
+
+    def ring_copy(q, d, s):
+        return remote(
+            own.at[d, s, span(q)], ring.at[d, s, span(q)],
+            ring_send.at[d, q, s], ring_recv.at[d, q, s], {"wide": target[d]})
+
+    def spot(q, d, index, which):
+        return o_ref.at[gather_at(d, index) * 2 + which, span(q), cols(d)]
+
+    def source(q, d, index):
+        return own.at[d, n - 1, span(q)] if index == 0 else spot(q, d, index, core)
+
+    def gather_copy(q, d, index):
+        return remote(
+            source(q, d, index), spot(q, d, index, core),
+            gather_send.at[d, q, index], gather_recv.at[d, q, index], {"wide": target[d]})
+
+    def gather_landed(q, d, index):
+        return remote(
+            source(q, d, 0), spot(q, d, index + 1, core),
+            gather_send.at[d, q, index], gather_recv.at[d, q, index], {"wide": target[d]})
+
+    def pair_copy(q, d, index):
+        return remote(
+            source(q, d, index), spot(q, d, index, core),
+            pair_send.at[d, q, index], pair_recv.at[d, q, index], {"wide": other})
+
+    def pair_landed(q, d, index):
+        return remote(
+            source(q, d, 0), spot(q, d, index, 1 - core),
+            pair_send.at[d, q, index], pair_recv.at[d, q, index], {"wide": other})
+
+    def keep_copy(q, d):
+        return pltpu.make_async_copy(
+            own.at[d, n - 1, span(q)], spot(q, d, 0, core), keep_sem.at[d, q])
+
+    def cross_copy(d, index, mine):
+        which = core if mine else 1 - core
+        at = gather_at(d, index) * 2 + which
+        if mine and index == 0:
+            src = own.at[d, n - 1, pl.ds(rows - tail, tail)]
+        else:
+            src = o_ref.at[at, pl.ds(rows - tail, tail), cols(d)]
+        lane = 0 if mine else 1
+        return remote(
+            src, e_ref.at[at, :, cols(d)],
+            cross_send.at[d, lane, index], cross_recv.at[d, lane, index],
+            {"section": 1 - section})
+
+    for s in range(n):
+        for q, d in streams:
+            own_copy(q, d, s).start()
+            part_copy(q, d, s).start()
+
+    for s in range(n):
+        for q, d in streams:
+            own_copy(q, d, s).wait()
+            part_copy(q, d, s).wait_recv()
+            if s:
+                ring_copy(q, d, s - 1).wait_recv()
+
+            def add(tile, carry, q=q, d=d, s=s):
+                at = pl.ds(pl.multiple_of(spans[q][0] + tile * 16, 16), 16)
+                total = own[d, s, at].astype(jnp.float32) + part[d, s, at].astype(jnp.float32)
+                if s:
+                    total = total + ring[d, s - 1, at].astype(jnp.float32)
+                own[d, s, at] = total.astype(own.dtype)
+                return carry
+
+            lax.fori_loop(0, spans[q][1] // 16, add, 0)
+            if s < n - 1:
+                ring_copy(q, d, s).start()
+            else:
+                gather_copy(q, d, 0).start()
+                pair_copy(q, d, 0).start()
+                keep_copy(q, d).start()
+                if q == 1:
+                    cross_copy(d, 0, True).start()
+
+    for t in range(n - 1):
+        for q, d in streams:
+            gather_landed(q, d, t).wait_recv()
+            if t < n - 2:
+                gather_copy(q, d, t + 1).start()
+            pair_copy(q, d, t + 1).start()
+            if q == 1:
+                cross_copy(d, t + 1, True).start()
+        for q, d in streams:
+            pair_landed(q, d, t).wait_recv()
+            if q == 1:
+                cross_copy(d, t, False).start()
+    for q, d in streams:
+        pair_landed(q, d, n - 1).wait_recv()
+        if q == 1:
+            cross_copy(d, n - 1, False).start()
+
+    for q, d in streams:
+        keep_copy(q, d).wait()
+        for s in range(n):
+            part_copy(q, d, s).wait_send()
+            pair_copy(q, d, s).wait_send()
+            if s < n - 1:
+                ring_copy(q, d, s).wait_send()
+                gather_copy(q, d, s).wait_send()
+            if q == 1:
+                for mine in (True, False):
+                    cross_copy(d, s, mine).wait()
+
+
+def ring_sum(stacked, tail):
+    members, rows, width = stacked.shape
+    n = members // 2
+    dma = pltpu.SemaphoreType.DMA
+    half = width // 2
+    sems = [dma((2, 2, n)) for _ in range(9)] + [dma((2, 2)), dma((2, 2, n)), dma((2, 2, n))]
+    return pl.pallas_call(
+        functools.partial(ring_kernel, n, rows, tail),
+        out_shape=(
+            jax.ShapeDtypeStruct((members, rows, width), jnp.bfloat16),
+            jax.ShapeDtypeStruct((members, tail, width), jnp.bfloat16),
+        ),
+        in_specs=[pl.BlockSpec(memory_space=pl.ANY)],
+        out_specs=(pl.BlockSpec(memory_space=pl.ANY), pl.BlockSpec(memory_space=pl.ANY)),
+        scratch_shapes=[
+            pltpu.VMEM((2, n, rows, half), jnp.bfloat16),
+            pltpu.VMEM((2, n, rows, half), jnp.bfloat16),
+            pltpu.VMEM((2, n - 1, rows, half), jnp.bfloat16),
+            sems,
+        ],
+        compiler_params=pltpu.CompilerParams(
+            collective_id=0, has_side_effects=True, vmem_limit_bytes=48 * 2**20
+        ),
+    )(stacked)
 
 
 def from_partner(block, axis, apart):
@@ -373,56 +573,77 @@
                 position_keep,
             )
             embed_accum = tuple((accum + part for accum, part in zip(embed_accum, embed_part)))
-    layer_total = lax.psum(
-        (
-            attn_accum[0],
+    low = jnp.bfloat16
+    members = lax.axis_size("wide")
+    feed_width = up_weight.shape[2]
+    blocks = feed_width // model_width
+
+    def side_by_side(matrix):
+        height, width = matrix.shape
+        pieces = matrix.reshape(height, width // model_width, model_width)
+        return pieces.transpose(1, 0, 2).reshape(-1, model_width)
+
+    weight_rows = jnp.concatenate(
+        [
+            side_by_side(attn_accum[2].astype(low)),
+            attn_accum[3].astype(low),
+            side_by_side(ffn_accum[2].astype(low)),
+            ffn_accum[4].astype(low),
+        ]
+    ).reshape(members, -1, model_width)
+    embed_rows = jnp.concatenate(
+        [embed_accum[0].reshape(-1, model_width), embed_accum[2]]
+    ).astype(low).reshape(members, -1, model_width)
+    stats = jnp.zeros((1, model_width), jnp.float32)
+    stats = stats.at[0, 0:3].set(square_sums).at[0, 3].set(valid_count)
+    small_rows = jnp.concatenate(
+        [
+            attn_accum[0][None],
+            ffn_accum[0][None],
             attn_accum[1],
-            attn_accum[2],
-            attn_accum[3],
-            ffn_accum[0],
             ffn_accum[1],
-            ffn_accum[2],
-            ffn_accum[3],
-            ffn_accum[4],
-            square_sums,
-            valid_count,
-        ),
-        "wide",
-    )
-    (
-        gain_one,
-        attn_vectors,
-        attend_total,
-        project_total,
-        gain_two,
-        ffn_vectors,
-        up_total,
-        up_offset_total,
-        down_total,
-        square_total,
-        count_total,
-    ) = layer_total
-    embed_total = lax.psum((embed_accum[0], embed_accum[1], embed_accum[2]), ("section", "wide"))
+            ffn_accum[3].reshape(blocks, model_width),
+            embed_accum[1],
+            stats,
+        ]
+    ).astype(low)
+    small_rows = jnp.pad(small_rows, ((0, members * SMALL - small_rows.shape[0]), (0, 0)))
+    stacked = jnp.concatenate(
+        [weight_rows, embed_rows, small_rows.reshape(members, SMALL, model_width)], axis=1
+    )
+    weight_count, embed_count = weight_rows.shape[1], embed_rows.shape[1]
+    total, cross = ring_sum(stacked, embed_count + SMALL)
+    cross = cross.astype(jnp.float32)
+    weight_total = total[:, :weight_count].reshape(-1, model_width).astype(jnp.float32)
+    embed_total = (total[:, weight_count : weight_count + embed_count].astype(jnp.float32)
+                   + cross[:, :embed_count]).reshape(-1, model_width)
+    small_total = total[0, weight_count + embed_count :].astype(jnp.float32)
+    small_cross = cross[0, embed_count:]
+    width = model_width
+    edges = [3 * width, 4 * width, 4 * width + blocks * width]
+
+    def joined(rows, count):
+        return rows.reshape(count, width, width).transpose(1, 0, 2).reshape(width, count * width)
+
+    attend_total = joined(weight_total[: edges[0]], 3)
+    project_total = weight_total[edges[0] : edges[1]]
+    up_total = joined(weight_total[edges[1] : edges[2]], blocks)
+    down_total = weight_total[edges[2] :]
+    gains_out = small_total[None, 0:2]
+    vectors_out = small_total[None, 2:8]
+    up_offset_total = small_total[8 : 8 + blocks].reshape(-1)
+    embed_vectors_total = (small_total + small_cross)[8 + blocks : 11 + blocks]
+    stat_row = small_total[11 + blocks]
     output = jnp.concatenate(output_blocks, axis=0)
     feature_out = jnp.concatenate(feature_blocks[::-1], axis=0)
-    gains_out = jnp.stack([gain_one, gain_two])[None]
-    vectors_out = jnp.stack(
-        [
-            attn_vectors[0],
-            attn_vectors[1],
-            attn_vectors[2],
-            attn_vectors[3],
-            ffn_vectors[0],
-            ffn_vectors[1],
-        ]
-    )[None]
-    rms_out = jnp.sqrt(square_total / (count_total * model_width))[None]
+    rms_out = jnp.sqrt(stat_row[0:3] / (stat_row[3] * model_width))[None]
+    embed_weight_rows = 2 * feat_width
     return (
         output,
         feature_out,
-        embed_total[0],
-        embed_total[1],
-        embed_total[2],
+        embed_total[:embed_weight_rows].reshape(2, feat_width, width),
+        embed_vectors_total,
+        embed_total[embed_weight_rows:],
         gains_out,
         vectors_out,
         attend_total[None],

time: 1130 us -> 888 us (0.79)
  waiting for transfers between devices: 533 us -> 54.2 us
  Pallas kernels: 0 us -> 170 us
  blocking collectives: 96.2 us -> 0 us
  other arithmetic: 77 us -> 163 us
  local copies, waits for them, and re-layouts: 78.8 us -> 164 us
  between operations: 21 us -> 7.41 us
    psum x2 -> x0, waiting for transfers between devices: 474 us -> none  [the longest x1 474 us: local(): lax.psum((attn_accum[0], attn_accum[1], attn_accum[2], attn_accum[3], ffn...]
    pallas_call x0 -> x1, Pallas kernels: none -> 170 us  [ring_sum(): pl.pallas_call(functools.partial(ring_kernel, n, rows, tail), out_shape=(...]
    psum x2 -> x0, blocking collectives: 96.2 us -> none  [the longest x1 59 us: local(): lax.psum((attn_accum[0], attn_accum[1], attn_accum[2], attn_accum[3], ffn...]
    concatenate x0 -> x3, other arithmetic: none -> 72.8 us  [the longest x1 60.1 us: local(): jnp.concatenate([side_by_side(attn_accum[2].astype(low)), attn_accum[3].a...]
    transpose x0 -> x3, local copies, waits for them, and re-layouts: none -> 24.8 us  [the longest x1 13.4 us: joined(): rows.reshape(count, width, width).transpose(1, 0, 2)]
    unnamed x456 -> x466, local copies, waits for them, and re-layouts: 50.9 us -> 32.5 us
    reshape x0 -> x2, local copies, waits for them, and re-layouts: none -> 18 us  [the longest x1 9.93 us: side_by_side(): pieces = matrix.reshape(height, width // model_width, model_width)]
    convert_element_type x0 -> x3, other arithmetic: none -> 16.7 us  [the longest x1 15.5 us: local(): total[:, :weight_count].reshape(-1, model_width).astype(jnp.float32)]
  transfers between devices with their start and end apart: 8 -> 6, of which waited for: 6 -> 5; matrix products, arithmetic and copies ran while one was open for 8% -> 20% of each run, Pallas kernels for 0% -> 0%
where the time goes in v1:
time: 888 us; the launch traced here: 883 us
  matrix products  316 us (36%)
  Pallas kernels  170 us (19%)
  local copies, waits for them, and re-layouts  164 us (18%)
  other arithmetic  163 us (18%)
  waiting for transfers between devices  54.2 us (6%)
    pallas_call x1, Pallas kernels, ring_sum(): pl.pallas_call(functools.partial(ring_kernel, n, rows, tail), out_shape=(...  170 us
    dot_general x12, matrix products, matmul_plain(): return jnp.dot(left, right, preferred_element_type=jnp.float32)  85.2 us
    dot_general x12, matrix products, matmul_left_t(): lax.dot_general(left, right, (((0,), (0,)), ((), ())), preferred_element_...  75.7 us
    dot_general x12, matrix products, matmul_right_t(): lax.dot_general(left, right, (((1,), (1,)), ((), ())), preferred_element_...  63.8 us
    concatenate x1, other arithmetic, local(): jnp.concatenate([side_by_side(attn_accum[2].astype(low)), attn_accum[3].a...  60.1 us
    ppermute x6, waiting for transfers between devices, from_partner(): return lax.ppermute(block, axis, route)  54.2 us
    unnamed x466, local copies, waits for them, and re-layouts  32.5 us
    dot_general x3, matrix products, attend_back_clip(): jnp.einsum('qhe,khe->hqk', grad_view, heads_view[:, 2], preferred_element...  27.6 us
  transfers between devices with their start and end apart: 6, of which 5 were waited for; matrix products, arithmetic and copies ran while one was open for 20% of the time, Pallas kernels for 0%

profile of v1, /device:TPU:0, one launch (start us, length us, event | category | flops | bytes accessed | tf_op | source)
XLA Modules:
  0.0 882.7 jit_solution(12087712244424687338)
XLA Ops:
  18.4 4.5 copy.63
  38.6 19.8 %multiply_convert_fusion.5 = (bf16[512,3072]{1,0:T(8,128)(2,1)S(1)}, f32[512,3072]{1,0:T(8,128)}, f32[512,3072]{1,0:T(8,128)}) fusion(f32[3072]{0:T(1024)S(1)} %bitcast.532, bf16[1,768,3072]{2,1,0:T(8,128)(2,1)} %param.30, f32[512,768]{1,0:T(8,128)S(1)} %get-tuple-element.260, f32[768]{0:T(1024)S(1)} %copy-done.142, f32[768]{0:T(1024)S(1)} %get-tuple-element.213, ...), kind=kOutput, calls=%fused_computation.75 | convolution fusion | flops 2521694208 | bytes 22042624 | tf_op jit(solution)/shard_map/dot_general | solution.py:233
  68.0 15.3 %collective-permute-done = bf16[1,512,768]{2,1,0:T(8,128)(2,1)} collective-permute-done((bf16[1,512,768]{2,1,0:T(8,128)(2,1)}, bf16[1,512,768]{2,1,0:T(8,128)(2,1)}, u32[]{:S(2)}, u32[]{:S(2)}) %collective-permute-start) | collective-permute-done | bytes 786464 | tf_op jit(solution)/shard_map/ppermute | solution.py:222
  110.9 19.7 %multiply_convert_fusion.4 = (bf16[512,3072]{1,0:T(8,128)(2,1)S(1)}, f32[512,3072]{1,0:T(8,128)}, f32[512,3072]{1,0:T(8,128)}) fusion(f32[3072]{0:T(1024)S(1)} %bitcast.533, bf16[1,768,3072]{2,1,0:T(8,128)(2,1)} %param.30, f32[512,768]{1,0:T(8,128)S(1)} %get-tuple-element.256, f32[512]{0:T(512)S(1)} %fusion.194, f32[512]{0:T(512)S(1)} %broadcast_multiply_fusion.5, ...), kind=kOutput, calls=%fused_computation.62 | convolution fusion | flops 2521694208 | bytes 22042624 | tf_op jit(solution)/shard_map/dot_general | solution.py:233
  138.5 13.9 %collective-permute-done.1 = bf16[1,512,768]{2,1,0:T(8,128)(2,1)S(1)} collective-permute-done((bf16[1,512,768]{2,1,0:T(8,128)(2,1)S(1)}, bf16[1,512,768]{2,1,0:T(8,128)(2,1)S(1)}, u32[]{:S(2)}, u32[]{:S(2)}) %collective-permute-start.1) | collective-permute-done | bytes 786464 | tf_op jit(solution)/shard_map/ppermute | solution.py:222
  177.4 20.0 %multiply_convert_fusion.3 = (bf16[512,3072]{1,0:T(8,128)(2,1)S(1)}, f32[512,3072]{1,0:T(8,128)}, f32[512,3072]{1,0:T(8,128)}) fusion(f32[3072]{0:T(1024)S(1)} %bitcast.534, bf16[1,768,3072]{2,1,0:T(8,128)(2,1)} %param.30, f32[512,768]{1,0:T(8,128)S(1)} %get-tuple-element.252, f32[512]{0:T(512)S(1)} %fusion.196, f32[512]{0:T(512)S(1)} %broadcast_multiply_fusion.3, ...), kind=kOutput, calls=%fused_computation.49 | convolution fusion | flops 2521694208 | bytes 22042624 | tf_op jit(solution)/shard_map/dot_general | solution.py:233
  197.4 10.6 %convert_reduce_fusion.2 = (f32[3072]{0:T(1024)}, bf16[512,3072]{1,0:T(8,128)(2,1)}) fusion(f32[512,3072]{1,0:T(8,128)} %get-tuple-element.250, bf16[1,3072,768]{2,1,0:T(8,128)(2,1)S(1)} %bitcast.529, pred[]{:T(512)S(6)} %eq.37, bf16[2,512,768]{2,1,0:T(8,128)(2,1)S(1)} %copy-done.10, s32[]{:T(128)S(6)} %min.15, f32[512,3072]{1,0:T(8,128)} %get-tuple-element.309, ...), kind=kOutput, calls=%fused_computation.42 | convolution fusion | flops 2443834368 | bytes 21258244 | tf_op jit(solution)/shard_map/dot_general | solution.py:243
  208.0 5.9 fusion.52
  214.0 4.9 fusion.84
  225.6 6.9 fusion.89
  232.5 9.1 %multiply_reduce_fusion.2 = (f32[12,512]{1,0:T(8,128)S(1)}, f32[12,512,512]{1,2,0:T(8,128)}) fusion(f32[12,512,512]{1,2,0:T(8,128)} %copy-done.3, f32[12,512]{1,0:T(8,128)S(1)} %copy-done.87, bf16[512,12,64]{0,2,1:T(8,128)(2,1)S(1)} %bitcast.480, bf16[512,3,12,64]{0,3,2,1:T(8,128)(2,1)S(1)} %bitcast.464), kind=kOutput, calls=%fused_computation.10 | convolution fusion | flops 412084224 | bytes 26796032 | tf_op jit(solution)/shard_map/while/body/eval_jaxpr/qhe,khe->hqk/dot_general | solution.py:280
  241.7 7.2 multiply_convert_fusion.2
  255.8 5.2 fusion.139
  263.3 5.3 fusion.210
  276.4 5.8 fusion.216
  282.2 6.9 collective-permute-done.2
  290.1 15.9 %collective-permute-done.3 = bf16[1,512,896]{2,1,0:T(8,128)(2,1)S(1)} collective-permute-done((bf16[1,512,896]{2,1,0:T(8,128)(2,1)S(1)}, bf16[1,512,896]{2,1,0:T(8,128)(2,1)S(1)}, u32[]{:S(2)}, u32[]{:S(2)}) %collective-permute-start.3) | collective-permute-done | bytes 917536 | tf_op jit(solution)/shard_map/ppermute | solution.py:222
  306.1 9.3 %convert_reduce_fusion.1 = (f32[3072]{0:T(1024)}, bf16[512,3072]{1,0:T(8,128)(2,1)}) fusion(f32[512,3072]{1,0:T(8,128)} %get-tuple-element.254, bf16[1,3072,768]{2,1,0:T(8,128)(2,1)S(1)} %bitcast.531, pred[]{:T(512)S(6)} %eq.37, bf16[1,512,896]{2,1,0:T(8,128)(2,1)S(1)} %collective-permute-done.3, bf16[2,512,768]{2,1,0:T(8,128)(2,1)S(1)} %copy-done.11, ...), kind=kOutput, calls=%fused_computation.41 | convolution fusion | flops 2444227584 | bytes 22044676 | tf_op jit(solution)/shard_map/dot_general | solution.py:243
  315.5 7.3 fusion.81
  329.6 6.9 fusion.92
  336.5 9.1 %multiply_reduce_fusion.1 = (f32[12,512]{1,0:T(8,128)S(1)}, f32[12,512,512]{1,2,0:T(8,128)}) fusion(f32[12,512,512]{1,2,0:T(8,128)} %copy-done.2, f32[12,512]{1,0:T(8,128)S(1)} %copy-done.86, bf16[512,12,64]{0,2,1:T(8,128)(2,1)S(1)} %bitcast.482, bf16[512,3,12,64]{0,3,2,1:T(8,128)(2,1)S(1)} %bitcast.459), kind=kOutput, calls=%fused_computation.7 | convolution fusion | flops 412084224 | bytes 26796032 | tf_op jit(solution)/shard_map/while/body/eval_jaxpr/qhe,khe->hqk/dot_general | solution.py:280
  345.6 7.0 multiply_convert_fusion.1
  359.5 5.3 fusion.209
  371.9 5.2 fusion.165
  379.4 5.9 fusion.215
  387.6 9.5 %convert_reduce_fusion = (f32[3072]{0:T(1024)}, bf16[512,3072]{1,0:T(8,128)(2,1)S(1)}) fusion(f32[512,3072]{1,0:T(8,128)} %get-tuple-element.258, bf16[1,3072,768]{2,1,0:T(8,128)(2,1)} %param.32, pred[]{:T(512)S(6)} %eq.37, bf16[2,512,768]{2,1,0:T(8,128)(2,1)S(1)} %copy-done.12, s32[]{:T(128)S(6)} %min.14, ...), kind=kOutput, calls=%fused_computation.40 | convolution fusion | flops 2444227584 | bytes 22044676 | tf_op jit(solution)/shard_map/dot_general | solution.py:243
  397.1 7.5 fusion.78
  411.8 6.9 fusion.95
  418.8 9.4 %multiply_reduce_fusion = (f32[12,512]{1,0:T(8,128)S(1)}, f32[12,512,512]{1,2,0:T(8,128)}) fusion(f32[12,512,512]{1,2,0:T(8,128)} %copy-done.1, f32[12,512]{1,0:T(8,128)S(1)} %copy-done.85, bf16[512,12,64]{0,2,1:T(8,128)(2,1)S(1)} %bitcast.484, bf16[512,3,12,64]{0,3,2,1:T(8,128)(2,1)S(1)} %bitcast.454), kind=kOutput, calls=%fused_computation.4 | convolution fusion | flops 412084224 | bytes 26796032 | tf_op jit(solution)/shard_map/while/body/eval_jaxpr/qhe,khe->hqk/dot_general | solution.py:280
  428.2 7.0 multiply_convert_fusion
  454.3 6.5 broadcast_select_fusion.17
  461.8 13.7 %add_convert_fusion.1 = bf16[768,3072]{1,0:T(8,128)(2,1)} fusion(f32[768,3072]{1,0:T(8,128)} %fusion.215, f32[768,3072]{1,0:T(8,128)} %fusion.216, bf16[512,3072]{1,0:T(8,128)(2,1)} %copy-done.66, f32[]{:T(128)S(6)} %convert_element_type.419, f32[]{:T(128)S(6)} %convert_element_type.418, f32[]{:T(128)S(6)} %convert_element_type.417, ...), kind=kOutput, calls=%fused_computation.32 | convolution fusion | flops 2432040960 | bytes 28321804 | tf_op jit(solution)/shard_map/dot_general | solution.py:237
  475.6 9.9 %reshape.1265 = bf16[768,4,768]{2,1,0:T(4,128)(2,1)} reshape(bf16[768,3072]{1,0:T(8,128)(2,1)} %add_convert_fusion.1) | data formatting | bytes 9437184 | tf_op jit(solution)/shard_map/reshape | solution.py:583
  485.5 5.3 copy.86
  490.8 9.8 %add_convert_fusion.2 = bf16[768,2304]{1,0:T(8,128)(2,1)} fusion(f32[768,2304]{1,0:T(8,128)} %fusion.209, f32[768,2304]{1,0:T(8,128)} %fusion.210, f32[]{:T(128)S(6)} %convert_element_type.419, f32[]{:T(128)S(6)} %convert_element_type.418, f32[]{:T(128)S(6)} %convert_element_type.417, bf16[512,768]{0,1:T(8,128)(2,1)S(1)} %bitcast.478, ...), kind=kOutput, calls=%fused_computation.33 | convolution fusion | flops 1831600128 | bytes 21637132 | tf_op jit(solution)/shard_map/dot_general | solution.py:237
  500.6 5.7 copy.84
  506.4 6.1 copy.85
  523.6 10.9 %add_convert_fusion = bf16[3072,768]{1,0:T(8,128)(2,1)S(1)} fusion(f32[3072,768]{1,0:T(8,128)} %fusion.165, f32[3072,768]{1,0:T(8,128)} %fusion.139, bf16[512,3072]{1,0:T(8,128)(2,1)} %copy-done.65, f32[]{:T(128)S(6)} %convert_element_type.419, f32[]{:T(128)S(6)} %convert_element_type.418, f32[]{:T(128)S(6)} %convert_element_type.417, pred[]{:T(512)S(6)} %eq.37, ...), kind=kOutput, calls=%fused_computation.31 | convolution fusion | flops 2431647744 | bytes 28311568 | tf_op jit(solution)/shard_map/dot_general | solution.py:237
  534.5 60.1 %pad_maximum_fusion.1 = bf16[9216,768]{1,0:T(8,128)(2,1)} fusion(bf16[3072,768]{1,0:T(8,128)(2,1)S(1)} %add_convert_fusion, bf16[3072,768]{1,0:T(8,128)(2,1)S(1)} %bitcast.469, bf16[768,768]{1,0:T(8,128)(2,1)S(1)} %add_convert_fusion.6, bf16[2304,768]{1,0:T(8,128)(2,1)} %bitcast.471), kind=kLoop, calls=%fused_computation.1 | loop fusion | flops 56623104 | bytes 28311552 | tf_op jit(solution)/shard_map/concatenate | solution.py:586
  607.2 12.6 %pad_maximum_fusion.g_ref = bf16[16,656,768]{2,1,0:T(8,128)(2,1)} fusion(bf16[16,16,768]{2,1,0:T(8,128)(2,1)S(1)} %bitcast.517, bf16[16,64,768]{2,1,0:T(8,128)(2,1)S(1)} %bitcast.496, bf16[16,576,768]{2,1,0:T(8,128)(2,1)} %bitcast.448), kind=kLoop, calls=%fused_computation | loop fusion | flops 48365568 | bytes 32243712 | tf_op jit(solution)/shard_map/concatenate | solution.py:611
  619.8 169.7 %shard_map.246 = (bf16[16,656,768]{2,1,0:T(8,128)(2,1)}, bf16[16,80,768]{2,1,0:T(8,128)(2,1)S(1)}) custom-call(bf16[16,656,768]{2,1,0:T(8,128)(2,1)} %pad_maximum_fusion.g_ref), custom_call_target="tpu_custom_call" | custom-call | tf_op jit(solution)/shard_map/pallas_call | solution.py:195
  793.2 15.5 %slice_convert_fusion = f32[16,576,768]{2,1,0:T(8,128)} fusion(bf16[16,656,768]{2,1,0:T(8,128)(2,1)} %get-tuple-element.138), kind=kLoop, calls=%fused_computation.2 | loop fusion | flops 7077888 | bytes 42467328 | tf_op jit(solution)/shard_map/convert_element_type | solution.py:617
  808.7 6.4 slice.377
  818.3 13.3 %slice_bitcast_fusion = (f32[1,3072,768]{2,1,0:T(8,128)}, f32[3072,768]{1,0:T(8,128)}) fusion(f32[9216,768]{1,0:T(8,128)} %bitcast.447), kind=kLoop, calls=%fused_computation.30 | loop fusion | bytes 37748736 | tf_op jit(solution)/shard_map/broadcast_in_dim | solution.py:653
  835.4 8.1 copy.87
  843.5 8.2 copy.90
  851.7 13.4 %copy.88 = f32[768,4,768]{2,1,0:T(4,128)} copy(f32[768,4,768]{2,0,1:T(8,128)} %bitcast.449) | data formatting | bytes 18874368 | tf_op jit(solution)/shard_map/transpose | solution.py:626
  865.1 12.3 %broadcast_in_dim_reshape.10 = f32[1,768,3072]{2,1,0:T(8,128)} reshape(f32[768,4,768]{2,1,0:T(4,128)} %copy.88) | data formatting | bytes 18874368 | tf_op jit(solution)/shard_map/broadcast_in_dim;reshape | solution.py:651
  (660 shorter events, 214.4 us)
Async XLA Ops:
  1.5 16.8 %copy-start.97 = (f32[2,512]{1,0:T(2,128)}, f32[2,512]{1,0:T(2,128)S(1)}, u32[]{:S(2)}) copy-start(f32[2,512]{1,0:T(2,128)S(1)} %convert_element_type.352) | copy-start | bytes 12292
  35.5 23.0 %slice-start.11 = ((s8[4718592]{0:T(1024)(128)(4,1)}), s8[4194304]{0:T(1024)(128)(4,1)S(1)}, s32[]{:S(2)}) async-start(s8[4718592]{0:T(1024)(128)(4,1)} %bitcast.524), calls=%async_computation.11 | async-start | bytes 8388608
  37.5 23.7 %copy-start.4 = (f32[512,768]{1,0:T(8,128)}, f32[512,768]{1,0:T(8,128)S(1)}, u32[]{:S(2)}) copy-start(f32[512,768]{1,0:T(8,128)S(1)} %get-tuple-element.260) | copy-start | bytes 4718596
  37.5 20.9 %copy-start.104 = (f32[512]{0:T(512)}, f32[512]{0:T(512)S(1)}, u32[]{:S(2)}) copy-start(f32[512]{0:T(512)S(1)} %broadcast_multiply_fusion.7) | copy-start | bytes 6148
  37.8 20.6 %copy-start.111 = (f32[512]{0:T(512)}, f32[512]{0:T(512)S(1)}, u32[]{:S(2)}) copy-start(f32[512]{0:T(512)S(1)} %fusion.192) | copy-start | bytes 6148
  38.6 19.8 %slice-start.12 = ((s8[4718592]{0:T(1024)(128)(4,1)}), s8[524288]{0:T(1024)(128)(4,1)S(1)}, s32[]{:S(2)}) async-start(s8[4718592]{0:T(1024)(128)(4,1)} %bitcast.524), calls=%async_computation.12 | async-start | bytes 1048576
  62.5 20.8 %collective-permute-start = (bf16[1,512,768]{2,1,0:T(8,128)(2,1)}, bf16[1,512,768]{2,1,0:T(8,128)(2,1)}, u32[]{:S(2)}, u32[]{:S(2)}) collective-permute-start(bf16[1,512,768]{2,1,0:T(8,128)(2,1)} %convert_bitcast_fusion.2), channel_id=1, source_target_pairs={{0,16},{16,0},{1,17},{17,1},{2,18},{18,2},{3,19},{19,3},{4,20},{20... | collective-permute-start | bytes 2359304 | tf_op jit(solution)/shard_map/ppermute | solution.py:222
  67.4 20.4 %copy-start.137 = (f32[768]{0:T(1024)S(1)}, f32[768]{0:T(1024)}, u32[]{:S(2)}) copy-start(f32[768]{0:T(1024)} %copy-done.136) | copy-start | bytes 9220
  67.4 20.4 %copy-start.163 = (f32[2304]{0:T(1024)S(1)}, f32[2304]{0:T(1024)}, u32[]{:S(2)}) copy-start(f32[2304]{0:T(1024)} %copy-done.162) | copy-start | bytes 27652
  108.4 22.1 %slice-start.13 = ((s8[4718592]{0:T(1024)(128)(4,1)}), s8[4194304]{0:T(1024)(128)(4,1)S(1)}, s32[]{:S(2)}) async-start(s8[4718592]{0:T(1024)(128)(4,1)} %bitcast.526), calls=%async_computation.13 | async-start | bytes 8388608
  110.5 22.8 %copy-start.14 = (f32[512,768]{1,0:T(8,128)}, f32[512,768]{1,0:T(8,128)S(1)}, u32[]{:S(2)}) copy-start(f32[512,768]{1,0:T(8,128)S(1)} %get-tuple-element.256) | copy-start | bytes 4718596
  110.5 20.1 %copy-start.113 = (f32[512]{0:T(512)}, f32[512]{0:T(512)S(1)}, u32[]{:S(2)}) copy-start(f32[512]{0:T(512)S(1)} %broadcast_multiply_fusion.5) | copy-start | bytes 6148
  110.8 19.8 %copy-start.127 = (f32[512]{0:T(512)}, f32[512]{0:T(512)S(1)}, u32[]{:S(2)}) copy-start(f32[512]{0:T(512)S(1)} %multiply_reduce_fusion.17) | copy-start | bytes 6148
  110.8 19.7 %copy-start.174 = (f32[512]{0:T(512)}, f32[512]{0:T(512)S(1)}, u32[]{:S(2)}) copy-start(f32[512]{0:T(512)S(1)} %fusion.194) | copy-start | bytes 6148
  110.9 19.8 %slice-start.14 = ((s8[4718592]{0:T(1024)(128)(4,1)}), s8[524288]{0:T(1024)(128)(4,1)S(1)}, s32[]{:S(2)}) async-start(s8[4718592]{0:T(1024)(128)(4,1)} %bitcast.526), calls=%async_computation.14 | async-start | bytes 1048576
  133.3 19.9 %copy-start.75 = (f32[512,768]{1,0:T(8,128)}, f32[512,768]{1,0:T(8,128)S(1)}, u32[]{:S(2)}) copy-start(f32[512,768]{1,0:T(8,128)S(1)} %fusion.44) | copy-start | bytes 4718596
  133.3 19.1 %copy-start.54 = (f32[512,768]{1,0:T(8,128)S(1)}, f32[512,768]{1,0:T(8,128)}, u32[]{:S(2)}) copy-start(f32[512,768]{1,0:T(8,128)} %param.25) | copy-start | bytes 4718596
  133.3 19.1 %copy-start.79 = (bf16[2,256,768]{2,1,0:T(8,128)(2,1)S(1)}, bf16[2,256,768]{2,1,0:T(8,128)(2,1)}, u32[]{:S(2)}) copy-start(bf16[2,256,768]{2,1,0:T(8,128)(2,1)} %param.23) | copy-start | bytes 2359300
  133.3 19.1 %copy-start.83 = (bf16[2,512,256]{2,1,0:T(8,128)(2,1)S(1)}, bf16[2,512,256]{2,1,0:T(8,128)(2,1)}, u32[]{:S(2)}) copy-start(bf16[2,512,256]{2,1,0:T(8,128)(2,1)} %param.19) | copy-start | bytes 1572868
  133.4 19.1 %copy-start.101 = (f32[768]{0:T(1024)S(1)}, f32[768]{0:T(1024)}, u32[]{:S(2)}) copy-start(f32[768]{0:T(1024)} %copy-done.100) | copy-start | bytes 9220
  133.4 19.1 %copy-start.149 = (f32[768]{0:T(1024)S(1)}, f32[768]{0:T(1024)}, u32[]{:S(2)}) copy-start(f32[768]{0:T(1024)} %get-tuple-element.209) | copy-start | bytes 9220
  133.4 19.1 %copy-start.199 = (pred[512]{0:T(512)(128)(4,1)S(1)}, pred[512]{0:T(512)(128)(4,1)}, u32[]{:S(2)}) copy-start(pred[512]{0:T(512)(128)(4,1)} %get-tuple-element.216) | copy-start | bytes 1540
  133.6 20.0 %copy-start.69 = (bf16[1,512,768]{2,1,0:T(8,128)(2,1)}, bf16[1,512,768]{2,1,0:T(8,128)(2,1)S(1)}, u32[]{:S(2)}) copy-start(bf16[1,512,768]{2,1,0:T(8,128)(2,1)S(1)} %convert_bitcast_fusion.1) | copy-start | bytes 2359300
  133.6 18.8 %collective-permute-start.1 = (bf16[1,512,768]{2,1,0:T(8,128)(2,1)S(1)}, bf16[1,512,768]{2,1,0:T(8,128)(2,1)S(1)}, u32[]{:S(2)}, u32[]{:S(2)}) collective-permute-start(bf16[1,512,768]{2,1,0:T(8,128)(2,1)S(1)} %convert_bitcast_fusion.1), channel_id=1, source_target_pairs={{0,16},{16,0},{1,17},{17,1},{2,18},{18,2},{3,19},{19,3},{4,20},{20... | collective-permute-start | bytes 2359304 | tf_op jit(solution)/shard_map/ppermute | solution.py:222
  137.9 17.1 %copy-start.138 = (f32[768]{0:T(1024)S(1)}, f32[768]{0:T(1024)}, u32[]{:S(2)}) copy-start(f32[768]{0:T(1024)} %copy-done.136) | copy-start | bytes 9220
  137.9 17.1 %copy-start.164 = (f32[2304]{0:T(1024)S(1)}, f32[2304]{0:T(1024)}, u32[]{:S(2)}) copy-start(f32[2304]{0:T(1024)} %copy-done.162) | copy-start | bytes 27652
  176.1 21.3 %slice-start.15 = ((s8[4718592]{0:T(1024)(128)(4,1)}), s8[4194304]{0:T(1024)(128)(4,1)S(1)}, s32[]{:S(2)}) async-start(s8[4718592]{0:T(1024)(128)(4,1)} %bitcast.528), calls=%async_computation.15 | async-start | bytes 8388608
  177.0 41.9 %copy-start.30 = (f32[512,768]{1,0:T(8,128)}, f32[512,768]{1,0:T(8,128)S(1)}, u32[]{:S(2)}) copy-start(f32[512,768]{1,0:T(8,128)S(1)} %get-tuple-element.252) | copy-start | bytes 4718596
  177.4 41.5 %copy-start.179 = (f32[512]{0:T(512)}, f32[512]{0:T(512)S(1)}, u32[]{:S(2)}) copy-start(f32[512]{0:T(512)S(1)} %fusion.196) | copy-start | bytes 6148
  177.4 20.0 %copy-start.10 = (bf16[2,512,768]{2,1,0:T(8,128)(2,1)S(1)}, bf16[2,512,768]{2,1,0:T(8,128)(2,1)}, u32[]{:S(2)}) copy-start(bf16[2,512,768]{2,1,0:T(8,128)(2,1)} %param.33) | copy-start | bytes 4718596
  177.4 20.0 %slice-start.16 = ((s8[4718592]{0:T(1024)(128)(4,1)}), s8[524288]{0:T(1024)(128)(4,1)S(1)}, s32[]{:S(2)}) async-start(s8[4718592]{0:T(1024)(128)(4,1)} %bitcast.528), calls=%async_computation.16 | async-start | bytes 1048576
  197.4 16.6 %copy-start.208 = (bf16[512,3072]{1,0:T(8,128)(2,1)}, bf16[512,3072]{1,0:T(8,128)(2,1)S(1)}, u32[]{:S(2)}) copy-start(bf16[512,3072]{1,0:T(8,128)(2,1)S(1)} %get-tuple-element.249) | copy-start | bytes 9437188
  268.6 20.5 %collective-permute-start.2 = (bf16[1,512,768]{2,1,0:T(8,128)(2,1)S(1)}, bf16[1,512,768]{2,1,0:T(8,128)(2,1)S(1)}, u32[]{:S(2)}, u32[]{:S(2)}) collective-permute-start(bf16[1,512,768]{2,1,0:T(8,128)(2,1)S(1)} %copy-done.93), channel_id=1, source_target_pairs={{0,16},{16,0},{1,17},{17,1},{2,18},{18,2},{3,19},{19,3},{4,20},{20... | collective-permute-start | bytes 2359304 | tf_op jit(solution)/shard_map/ppermute | solution.py:222
  271.9 34.2 %slice-start.17 = ((s8[4718592]{0:T(1024)(128)(4,1)}), s8[4194304]{0:T(1024)(128)(4,1)S(1)}, s32[]{:S(2)}) async-start(s8[4718592]{0:T(1024)(128)(4,1)} %bitcast.530), calls=%async_computation.17 | async-start | bytes 8388608
  272.4 33.6 %collective-permute-start.3 = (bf16[1,512,896]{2,1,0:T(8,128)(2,1)S(1)}, bf16[1,512,896]{2,1,0:T(8,128)(2,1)S(1)}, u32[]{:S(2)}, u32[]{:S(2)}) collective-permute-start(bf16[1,512,896]{2,1,0:T(8,128)(2,1)S(1)} %pad_maximum_fusion.6), channel_id=1, source_target_pairs={{0,16},{16,0},{1,17},{17,1},{2,18},{18,2},{3,19},{19,3},{4,20},{20... | collective-permute-start | bytes 2752520 | tf_op jit(solution)/shard_map/ppermute | solution.py:222
  276.4 29.7 %slice-start.18 = ((s8[4718592]{0:T(1024)(128)(4,1)}), s8[524288]{0:T(1024)(128)(4,1)S(1)}, s32[]{:S(2)}) async-start(s8[4718592]{0:T(1024)(128)(4,1)} %bitcast.530), calls=%async_computation.18 | async-start | bytes 1048576
  276.4 29.7 %copy-start.206 = (f32[1,3072]{1,0:T(1,128)S(1)}, f32[1,3072]{1,0:T(1,128)}, u32[]{:S(2)}) copy-start(f32[1,3072]{1,0:T(1,128)} %param.31) | copy-start | bytes 36868
  306.1 17.4 %copy-start.55 = (bf16[1,512,896]{2,1,0:T(8,128)(2,1)}, bf16[1,512,896]{2,1,0:T(8,128)(2,1)S(1)}, u32[]{:S(2)}) copy-start(bf16[1,512,896]{2,1,0:T(8,128)(2,1)S(1)} %collective-permute-done.3) | copy-start | bytes 2752516
  367.7 19.8 %collective-permute-start.4 = (bf16[1,512,896]{2,1,0:T(8,128)(2,1)S(1)}, bf16[1,512,896]{2,1,0:T(8,128)(2,1)S(1)}, u32[]{:S(2)}, u32[]{:S(2)}) collective-permute-start(bf16[1,512,896]{2,1,0:T(8,128)(2,1)S(1)} %pad_maximum_fusion.7), channel_id=1, source_target_pairs={{0,16},{16,0},{1,17},{17,1},{2,18},{18,2},{3,19},{19,3},{4,20},{20... | collective-permute-start | bytes 2752520 | tf_op jit(solution)/shard_map/ppermute | solution.py:222
  387.5 17.7 %copy-start.52 = (bf16[1,512,896]{2,1,0:T(8,128)(2,1)}, bf16[1,512,896]{2,1,0:T(8,128)(2,1)S(1)}, u32[]{:S(2)}) copy-start(bf16[1,512,896]{2,1,0:T(8,128)(2,1)S(1)} %collective-permute-done.4) | copy-start | bytes 2752516
  411.8 16.4 %slice-start = ((s8[12582912]{0:T(1024)(128)(4,1)}), s8[4194304]{0:T(1024)(128)(4,1)S(1)}, s32[]{:S(2)}) async-start(s8[12582912]{0:T(1024)(128)(4,1)} %bitcast.440), calls=%async_computation | async-start | bytes 8388608
  411.8 16.4 %slice-start.1 = ((s8[12582912]{0:T(1024)(128)(4,1)}), s8[4194304]{0:T(1024)(128)(4,1)S(1)}, s32[]{:S(2)}) async-start(s8[12582912]{0:T(1024)(128)(4,1)} %bitcast.440), calls=%async_computation.1 | async-start | bytes 8388608
  418.8 22.7 %copy-start.41 = (bf16[12,64,512]{2,1,0:T(8,128)(2,1)}, bf16[12,64,512]{2,1,0:T(8,128)(2,1)S(1)}, u32[]{:S(2)}) copy-start(bf16[12,64,512]{2,1,0:T(8,128)(2,1)S(1)} %fusion.95) | copy-start | bytes 2359300
  445.7 149.0 %collective-permute-start.5 = (bf16[1,512,896]{2,1,0:T(8,128)(2,1)}, bf16[1,512,896]{2,1,0:T(8,128)(2,1)}, u32[]{:S(2)}, u32[]{:S(2)}) collective-permute-start(bf16[1,512,896]{2,1,0:T(8,128)(2,1)} %pad_maximum_fusion.8), channel_id=1, source_target_pairs={{0,16},{16,0},{1,17},{17,1},{2,18},{18,2},{3,19},{19,3},{4,20},{20... | collective-permute-start | bytes 2752520 | tf_op jit(solution)/shard_map/ppermute | solution.py:222
  534.5 60.1 %copy-start.49 = (bf16[512,768]{1,0:T(8,128)(2,1)S(1)}, bf16[512,768]{1,0:T(8,128)(2,1)}, u32[]{:S(2)}) copy-start(bf16[512,768]{1,0:T(8,128)(2,1)} %copy-done.48) | copy-start | bytes 2359300
  534.5 60.1 %copy-start.51 = (bf16[512,768]{1,0:T(8,128)(2,1)S(1)}, bf16[512,768]{1,0:T(8,128)(2,1)}, u32[]{:S(2)}) copy-start(bf16[512,768]{1,0:T(8,128)(2,1)} %copy-done.50) | copy-start | bytes 2359300
  534.5 60.1 %copy-start.107 = (f32[512]{0:T(512)S(1)}, f32[512]{0:T(512)}, u32[]{:S(2)}) copy-start(f32[512]{0:T(512)} %fusion.189) | copy-start | bytes 6148
  792.5 41.6 %copy-start.96 = (f32[16,768]{1,0:T(8,128)}, f32[16,768]{1,0:T(8,128)S(1)}, u32[]{:S(2)}) copy-start(f32[16,768]{1,0:T(8,128)S(1)} %get-tuple-element.264) | copy-start | bytes 147460
  (189 other events, 850.9 us)

commit v2 on v1

v2 whole, which is shorter than its diff:
```python
import functools
import math

import jax
import jax.numpy as jnp
from jax import lax
from jax.experimental import pallas as pl
from jax.experimental.pallas import tpu as pltpu
from jax.sharding import PartitionSpec as P

H = 12
HD = 64
EPS = 1e-06
NEG = -1000000000.0
MESH = pl.DeviceIdType.MESH
SMALL = 16


def ring_kernel(n, rows, tail, g_ref, f_ref, o_ref, e_ref, h_ref, own, part, ring, sems):
    (own_sem, part_send, part_recv, ring_send, ring_recv, gather_send, gather_recv,
     pair_send, pair_recv, keep_sem, cross_send, cross_recv, feat_sem) = sems
    columns = g_ref.shape[2] // 2
    me = lax.axis_index("wide")
    section = lax.axis_index("section")
    chip, core = me // 2, me % 2
    place = jnp.where(chip % 2 == 0, chip // 2, n - 1 - chip // 2)

    def member(position):
        position = lax.rem(position + 2 * n, n)
        return jnp.where(2 * position < n, 2 * position, 2 * (n - 1 - position) + 1) * 2 + core

    right, left = member(place + 1), member(place - 1)
    other = chip * 2 + 1 - core
    target = (right, left)

    barrier = pltpu.get_barrier_semaphore()
    for peer in (right, left, other):
        pl.semaphore_signal(barrier, inc=1, device_id={"wide": peer}, device_id_type=MESH)
    pl.semaphore_signal(barrier, inc=1, device_id={"section": 1 - section}, device_id_type=MESH)
    pl.semaphore_wait(barrier, 4)

    half = -(-rows // 32) * 16
    spans = ((0, half), (half, rows - half))
    streams = [(q, d) for q in range(2) for d in range(2)]

    def turn(position):
        return lax.rem(position + 2 * n, n)

    def reduce_at(d, step):
        return turn(place - step) if d == 0 else turn(place + step)

    def gather_at(d, index):
        return turn(place + 1 - index) if d == 0 else turn(place - 1 + index)

    def span(q):
        return pl.ds(*spans[q])

    def cols(d):
        return pl.ds(d * columns, columns)

    def remote(src, dst, send, recv, device):
        return pltpu.make_async_remote_copy(
            src_ref=src, dst_ref=dst, send_sem=send, recv_sem=recv,
            device_id=device, device_id_type=MESH)

    def own_copy(q, d, s):
        return pltpu.make_async_copy(
            g_ref.at[reduce_at(d, s) * 2 + core, span(q), cols(d)],
            own.at[d, s, span(q)], own_sem.at[d, q, s])

    def part_copy(q, d, s):
        return remote(
            g_ref.at[reduce_at(d, s) * 2 + 1 - core, span(q), cols(d)],
            part.at[d, s, span(q)], part_send.at[d, q, s], part_recv.at[d, q, s],
            {"wide": other})

    def ring_copy(q, d, s):
        return remote(
            own.at[d, s, span(q)], ring.at[d, s, span(q)],
            ring_send.at[d, q, s], ring_recv.at[d, q, s], {"wide": target[d]})

    def spot(q, d, index, which):
        return o_ref.at[gather_at(d, index) * 2 + which, span(q), cols(d)]

    def source(q, d, index):
        return own.at[d, n - 1, span(q)] if index == 0 else spot(q, d, index, core)

    def gather_copy(q, d, index):
        return remote(
            source(q, d, index), spot(q, d, index, core),
            gather_send.at[d, q, index], gather_recv.at[d, q, index], {"wide": target[d]})

    def gather_landed(q, d, index):
        return remote(
            source(q, d, 0), spot(q, d, index + 1, core),
            gather_send.at[d, q, index], gather_recv.at[d, q, index], {"wide": target[d]})

    def pair_copy(q, d, index):
        return remote(
            source(q, d, index), spot(q, d, index, core),
            pair_send.at[d, q, index], pair_recv.at[d, q, index], {"wide": other})

    def pair_landed(q, d, index):
        return remote(
            source(q, d, 0), spot(q, d, index, 1 - core),
            pair_send.at[d, q, index], pair_recv.at[d, q, index], {"wide": other})

    def keep_copy(q, d):
        return pltpu.make_async_copy(
            own.at[d, n - 1, span(q)], spot(q, d, 0, core), keep_sem.at[d, q])

    def cross_copy(d, index, mine):
        which = core if mine else 1 - core
        at = gather_at(d, index) * 2 + which
        if mine and index == 0:
            src = own.at[d, n - 1, pl.ds(rows - tail, tail)]
        else:
            src = o_ref.at[at, pl.ds(rows - tail, tail), cols(d)]
        lane = 0 if mine else 1
        return remote(
            src, e_ref.at[at, :, cols(d)],
            cross_send.at[d, lane, index], cross_recv.at[d, lane, index],
            {"section": 1 - section})

    feat_half = h_ref.shape[2]
    feat_keep = pltpu.make_async_copy(
        f_ref.at[:, :, pl.ds(0, feat_half)], h_ref, feat_sem.at[0])
    feat_send = remote(
        f_ref.at[:, :, pl.ds(feat_half, feat_half)], h_ref, feat_sem.at[1], feat_sem.at[2],
        {"section": 1 - section})

    @pl.when(section == 0)
    def _():
        feat_keep.start()
        feat_send.start()

    for s in range(n):
        for q, d in streams:
            own_copy(q, d, s).start()
            part_copy(q, d, s).start()

    for s in range(n):
        for q, d in streams:
            own_copy(q, d, s).wait()
            part_copy(q, d, s).wait_recv()
            if s:
                ring_copy(q, d, s - 1).wait_recv()

            def add(tile, carry, q=q, d=d, s=s):
                at = pl.ds(pl.multiple_of(spans[q][0] + tile * 16, 16), 16)
                total = own[d, s, at].astype(jnp.float32) + part[d, s, at].astype(jnp.float32)
                if s:
                    total = total + ring[d, s - 1, at].astype(jnp.float32)
                own[d, s, at] = total.astype(own.dtype)
                return carry

            lax.fori_loop(0, spans[q][1] // 16, add, 0)
            if s < n - 1:
                ring_copy(q, d, s).start()
            else:
                gather_copy(q, d, 0).start()
                pair_copy(q, d, 0).start()
                keep_copy(q, d).start()
                if q == 1:
                    cross_copy(d, 0, True).start()

    for t in range(n - 1):
        for q, d in streams:
            gather_landed(q, d, t).wait_recv()
            if t < n - 2:
                gather_copy(q, d, t + 1).start()
            pair_copy(q, d, t + 1).start()
            if q == 1:
                cross_copy(d, t + 1, True).start()
        for q, d in streams:
            pair_landed(q, d, t).wait_recv()
            if q == 1:
                cross_copy(d, t, False).start()
    for q, d in streams:
        pair_landed(q, d, n - 1).wait_recv()
        if q == 1:
            cross_copy(d, n - 1, False).start()

    @pl.when(section == 0)
    def _():
        feat_keep.wait()
        feat_send.wait_send()

    @pl.when(section == 1)
    def _():
        feat_send.wait_recv()

    for q, d in streams:
        keep_copy(q, d).wait()
        for s in range(n):
            part_copy(q, d, s).wait_send()
            pair_copy(q, d, s).wait_send()
            if s < n - 1:
                ring_copy(q, d, s).wait_send()
                gather_copy(q, d, s).wait_send()
            if q == 1:
                for mine in (True, False):
                    cross_copy(d, s, mine).wait()


def dot_nn(left, right):
    return jnp.dot(left, right, preferred_element_type=jnp.float32)


def dot_nt(left, right):
    return lax.dot_general(
        left, right, (((1,), (1,)), ((), ())), preferred_element_type=jnp.float32
    )


def tile_of(index, size):
    return pl.ds(pl.multiple_of(index * size, size), size)


def column_sum(values):
    return jnp.sum(values, axis=0, keepdims=True)


def row_mean(values):
    return jnp.mean(values, axis=-1, keepdims=True)


def gelu_pair(hidden):
    decay = jnp.exp(-0.5 * hidden * hidden)
    t = 1.0 / (1.0 + (0.3275911 * 0.5**0.5) * jnp.abs(hidden))
    poly = 1.061405429 * 0.5
    for term in (-1.453152027, 1.421413741, -0.284496736, 0.254829592):
        poly = poly * t + 0.5 * term
    upper = poly * t * decay
    cdf = jnp.where(hidden > 0.0, 1.0 - upper, upper)
    return hidden * cdf, cdf + hidden * decay * 0.3989422804014327


def fetch(pairs, sems):
    copies = [pltpu.make_async_copy(src, dst, sems.at[i]) for i, (src, dst) in enumerate(pairs)]
    for copy in copies:
        copy.start()
    return copies


def greet_partner():
    barrier = pltpu.get_barrier_semaphore()
    pl.semaphore_signal(
        barrier, inc=1, device_id={"section": 1 - lax.axis_index("section")}, device_id_type=MESH
    )
    pl.semaphore_wait(barrier, 1)


def to_partner(src, dst, send, recv):
    return pltpu.make_async_remote_copy(
        src_ref=src, dst_ref=dst, send_sem=send, recv_sem=recv,
        device_id={"section": 1 - lax.axis_index("section")}, device_id_type=MESH)


def forward_kernel(
    feat_h, chosen_h, pos_h, wqkv_h, wout_h, wup_h, wdown_h,
    cols, kind_offset, mask_row, bias_row, live_row, gains, vectors, up_bias,
    left_h, x_h, qkv_h, probs_h, middle_h, slope_h, out_h, stats,
    feat, chosen, pos, wqkv, wout, wup, wdown,
    x, normed, qkv, probs, context, middle, hidden_in, active, slope, y, landed,
    load_sem, save_sem, probs_sem, send_sem, recv_sem, back_send, back_recv, keep_sem,
):
    low = jnp.bfloat16
    section = lax.axis_index("section")
    clips, length, width = landed.shape
    half = length // 2
    feed = wup.shape[1]
    heads2 = width // 128
    blocks = feed // width
    greet_partner()
    loads = fetch(
        [(feat_h, feat), (chosen_h, chosen), (pos_h, pos), (wqkv_h, wqkv), (wout_h, wout),
         (wup_h, wup), (wdown_h, wdown)], load_sem)
    stats[...] = jnp.zeros_like(stats)
    low_lanes = lax.broadcasted_iota(jnp.int32, (1, 128), 1) < HD

    def save(index, src, dst):
        return pltpu.make_async_copy(src, dst, save_sem.at[index])

    def saves(c):
        rows = pl.ds(pl.multiple_of(c * length, length), length)
        pairs = [
            (x, x_h.at[c]), (normed, left_h.at[0, rows]), (qkv, qkv_h.at[c]),
            (context, left_h.at[1, rows]), (middle, middle_h.at[c]),
            (hidden_in, left_h.at[2, rows]), (slope, slope_h.at[c]),
        ] + [
            (active.at[:, pl.ds(b * width, width)], left_h.at[3 + b, rows]) for b in range(blocks)
        ]
        return [save(i, src, dst) for i, (src, dst) in enumerate(pairs)]

    def probs_save(c, pair):
        slot = lax.rem(pair, 2)
        return pltpu.make_async_copy(
            probs.at[slot], probs_h.at[c, pl.ds(pair * 2, 2)], probs_sem.at[slot])

    def send_half(c, h):
        rows = pl.ds(h * half, half)
        return to_partner(
            y.at[c, rows], landed.at[c, rows], send_sem.at[c, h], recv_sem.at[c, h])

    def back_half(c, h):
        rows = pl.ds(h * half, half)
        return to_partner(
            y.at[c, rows, pl.ds(0, width // 2)], out_h.at[c, rows],
            back_send.at[c, h], back_recv.at[c, h])

    def keep_half(c, h):
        rows = pl.ds(h * half, half)
        return pltpu.make_async_copy(
            y.at[c, rows, pl.ds(width // 2, width // 2)], out_h.at[c, rows], keep_sem.at[c, h])

    def clip(c, carry):
        def after_first(index):
            @pl.when(c > 0)
            def _():
                saves(c - 1)[index].wait()

        after_first(0)
        after_first(1)

        @pl.when(section == 0)
        def _():
            @pl.when(c == 0)
            def _():
                for copy in loads[:3]:
                    copy.wait()

            def tile(i, carry):
                rows = tile_of(i, 128)
                lifted = dot_nn(feat[c, rows, :], chosen[c]) + kind_offset[c]
                hidden = cols[c, rows, :][:, 0:1]
                x[rows, :] = jnp.where(hidden > 0.0, mask_row[...], lifted) + pos[rows, :]
                return carry

            lax.fori_loop(0, length // 128, tile, 0)

        @pl.when(section == 1)
        def _():
            @pl.when(c == 0)
            def _():
                for copy in loads[:3]:
                    copy.wait()

            for h in range(2):
                send_half(c, h).wait_recv()

            def tile(i, carry):
                rows = tile_of(i, 64)
                x[rows, :] = landed[c, rows, :].astype(jnp.float32)
                return carry

            lax.fori_loop(0, length // 64, tile, 0)

        own = saves(c)
        own[0].start()

        def norm_rows(source, target, which, shift, first, count):
            gain, offset = gains[which : which + 1, :], vectors[shift : shift + 1, :]

            def tile(i, carry):
                rows = tile_of(i, 64)
                values = source[rows, :]
                values = values - row_mean(values)
                scale = lax.rsqrt(row_mean(values * values) + EPS)
                target[rows, :] = (values * scale * gain + offset).astype(low)
                return carry

            lax.fori_loop(first, first + count, tile, 0)

        norm_rows(x, normed, 0, 0, 0, length // 64)
        own[1].start()
        after_first(2)

        @pl.when(c == 0)
        def _():
            loads[3].wait()

        def qkv_tile(j, carry):
            at = tile_of(j, 256)
            qkv[:, at] = (dot_nn(normed[...], wqkv[:, at]) + bias_row[:, at]).astype(low)
            return carry

        lax.fori_loop(0, 3 * width // 256, qkv_tile, 0)
        own[2].start()
        after_first(3)

        def attend(pair, carry):
            @pl.when((pair > 1) | (c > 0))
            def _():
                probs_save(c, pair).wait()

            at = tile_of(pair, 128)
            queries = qkv[:, at]
            keys_in = qkv[:, tile_of(pair + heads2, 128)]
            values_in = qkv[:, tile_of(pair + 2 * heads2, 128)]
            outs = []
            for h in range(2):
                pick = jnp.where(low_lanes == (h == 0), HD**-0.5, 0.0).astype(low)
                scores = dot_nt(queries * pick, keys_in) + live_row[c]
                top = jnp.max(scores, axis=-1, keepdims=True)
                scores = jnp.exp(scores - top)
                total = jnp.sum(scores, axis=-1, keepdims=True)
                soft = (scores * (1.0 / total)).astype(low)
                probs[lax.rem(pair, 2), h] = soft
                outs.append(dot_nn(soft, values_in))
            context[:, at] = jnp.where(low_lanes, outs[0], outs[1]).astype(low)
            probs_save(c, pair).start()
            return carry

        lax.fori_loop(0, heads2, attend, 0)
        own[3].start()
        after_first(4)

        @pl.when(c == 0)
        def _():
            loads[4].wait()

        live = cols[c][:, 1:2]

        def out_tile(j, carry):
            at = tile_of(j, 256)
            branch = dot_nn(context[...], wout[:, at]) + vectors[3:4, at]
            middle[:, at] = x[:, at] + branch
            stats[1:2, at] += column_sum(branch * branch * live)
            return carry

        lax.fori_loop(0, width // 256, out_tile, 0)
        own[4].start()
        for index in range(5, 7 + blocks):
            after_first(index)

        @pl.when(c == 0)
        def _():
            loads[5].wait()
            loads[6].wait()

        for h in range(2):
            rows = pl.ds(h * half, half)
            norm_rows(middle, hidden_in, 1, 4, h * (half // 64), half // 64)
            if h == 1:
                own[5].start()

            def up_tile(j, carry):
                at = tile_of(j, 256)
                hidden = dot_nn(hidden_in[rows, :], wup[:, at]) + up_bias[:, at]
                value, steep = gelu_pair(hidden)
                active[rows, at] = value.astype(low)
                slope[rows, at] = steep.astype(low)
                return carry

            lax.fori_loop(0, feed // 256, up_tile, 0)
            if h == 1:
                for copy in own[6:]:
                    copy.start()

            def down_tile(j, carry):
                at = tile_of(j, 256)
                mixer = dot_nn(active[rows, :], wdown[:, at]) + vectors[5:6, at]
                total = middle[rows, at] + mixer
                flags = cols[c, rows, :][:, 1:2]
                stats[0:1, at] += column_sum(total * total * flags)
                stats[2:3, at] += column_sum(mixer * mixer * flags)
                y[c, rows, at] = total.astype(low)
                return carry

            lax.fori_loop(0, width // 256, down_tile, 0)

            @pl.when(section == 0)
            def _():
                send_half(c, h).start()

            @pl.when(section == 1)
            def _():
                back_half(c, h).start()
                keep_half(c, h).start()
        return carry

    lax.fori_loop(0, clips, clip, 0)
    for pair in (heads2 - 2, heads2 - 1):
        probs_save(clips - 1, pair).wait()
    for copy in saves(clips - 1):
        copy.wait()
    for c in range(clips):
        for h in range(2):
            @pl.when(section == 0)
            def _():
                send_half(c, h).wait_send()
                back_half(c, h).wait_recv()

            @pl.when(section == 1)
            def _():
                back_half(c, h).wait_send()
                keep_half(c, h).wait()


def backward_kernel(
    cot_h, wqkv_h, wout_h, wup_h, wdown_h, x_h, qkv_h, probs_h, middle_h, slope_h, gains,
    right_h, dx_h, small, up_sums,
    wqkv, wout, wup, wdown, x, qkv, probs, middle, slope, g,
    d_hidden, wide_grad, d_middle, d_branch, d_context, d_qkv, d_low,
    load_sem, state_sem, probs_sem, save_sem, dx_sem, send_sem, recv_sem,
):
    low = jnp.bfloat16
    f32 = jnp.float32
    section = lax.axis_index("section")
    clips, length, width = g.shape
    half = length // 2
    feed = wup.shape[1]
    heads2 = width // 128
    blocks = feed // width
    greet_partner()

    def cot_load(c):
        return pltpu.make_async_copy(cot_h.at[c], g.at[c], state_sem.at[c, 0])

    def state_loads(c):
        pairs = [(slope_h, slope), (middle_h, middle), (qkv_h, qkv), (x_h, x)]
        return [
            pltpu.make_async_copy(src.at[c], dst.at[c], state_sem.at[c, 1 + i])
            for i, (src, dst) in enumerate(pairs)
        ]

    @pl.when(section == 1)
    def _():
        cot_load(0).start()

    loads = fetch([(wdown_h, wdown), (wup_h, wup), (wout_h, wout), (wqkv_h, wqkv)], load_sem)
    for c in range(clips):
        for copy in state_loads(c):
            copy.start()

    @pl.when(section == 1)
    def _():
        for c in range(1, clips):
            cot_load(c).start()

    small[...] = jnp.zeros_like(small)
    up_sums[...] = jnp.zeros_like(up_sums)
    low_lanes = lax.broadcasted_iota(jnp.int32, (1, 128), 1) < HD
    slots = probs.shape[0]
    pairs_total = clips * heads2

    def probs_load(step):
        slot = lax.rem(step, slots)
        return pltpu.make_async_copy(
            probs_h.at[step // heads2, pl.ds(lax.rem(step, heads2) * 2, 2)],
            probs.at[slot], probs_sem.at[slot])

    for step in range(slots):
        probs_load(step).start()

    def saves(c):
        rows = pl.ds(pl.multiple_of(c * length, length), length)
        pairs = [(d_qkv.at[:, pl.ds(b * width, width)], right_h.at[b, rows]) for b in range(3)]
        pairs += [(d_branch, right_h.at[3, rows])]
        pairs += [
            (d_hidden.at[:, pl.ds(b * width, width)], right_h.at[4 + b, rows])
            for b in range(blocks)
        ]
        pairs += [(g.at[c], right_h.at[4 + blocks, rows])]
        return [pltpu.make_async_copy(s, d, save_sem.at[i]) for i, (s, d) in enumerate(pairs)]

    def send_half(c, h):
        rows = pl.ds(h * half, half)
        return to_partner(
            d_low.at[c, rows], g.at[c, rows], send_sem.at[c, h], recv_sem.at[c, h])

    def dx_save(c):
        return pltpu.make_async_copy(d_low.at[c], dx_h.at[c], dx_sem.at[c])

    def norm_back(source, carried, which, shift_row, rows, take):
        gain = gains[which : which + 1, :]
        values = source[rows, :]
        values = values - row_mean(values)
        scale = lax.rsqrt(row_mean(values * values) + EPS)
        values = values * scale
        grad = wide_grad[rows, :]
        small[which : which + 1, :] += column_sum(grad * values)
        small[shift_row : shift_row + 1, :] += column_sum(grad)
        grad = grad * gain
        return carried + scale * (grad - row_mean(grad) - values * row_mean(grad * values))

    def clip(c, carry):
        def after_first(lo, hi):
            @pl.when(c > 0)
            def _():
                for copy in saves(c - 1)[lo:hi]:
                    copy.wait()

        after_first(4, 5 + blocks)

        @pl.when(section == 1)
        def _():
            cot_load(c).wait()

        state = state_loads(c)
        own = saves(c)

        @pl.when(c == 0)
        def _():
            loads[0].wait()
            loads[1].wait()

        state[0].wait()
        state[1].wait()
        for h in range(2):
            rows = pl.ds(h * half, half)

            @pl.when(section == 0)
            def _():
                send_half(c, h).wait_recv()

            if h == 1:
                own[-1].start()

            def feed_tile(j, carry):
                at = tile_of(j, 256)
                d_active = dot_nt(g[c, rows, :], wdown[at, :])
                grad = (slope[c, rows, at].astype(f32) * d_active).astype(low)
                d_hidden[rows, at] = grad
                up_sums[:, at] += column_sum(grad.astype(f32))
                return carry

            lax.fori_loop(0, feed // 256, feed_tile, 0)

            def in_tile(j, carry):
                at = tile_of(j, 256)
                wide_grad[rows, at] = dot_nt(d_hidden[rows, :], wup[at, :])
                return carry

            lax.fori_loop(0, width // 256, in_tile, 0)

        after_first(3, 4)
        for copy in own[4:-1]:
            copy.start()

        def middle_tile(i, carry):
            rows = tile_of(i, 64)
            grad_in = g[c, rows, :].astype(f32)
            total = norm_back(middle.at[c], grad_in, 1, 6, rows, None)
            d_middle[rows, :] = total
            rounded = total.astype(low)
            d_branch[rows, :] = rounded
            small[5:6, :] += column_sum(rounded.astype(f32))
            small[7:8, :] += column_sum(grad_in)
            return carry

        lax.fori_loop(0, length // 64, middle_tile, 0)
        own[3].start()

        @pl.when(c == 0)
        def _():
            loads[2].wait()

        def context_tile(j, carry):
            at = tile_of(j, 256)
            d_context[:, at] = dot_nt(d_branch[...], wout[at, :]).astype(low)
            return carry

        lax.fori_loop(0, width // 256, context_tile, 0)
        state[2].wait()
        after_first(0, 3)

        def attend(pair, carry):
            step = c * heads2 + pair
            slot = lax.rem(step, slots)
            probs_load(step).wait()
            at, key_at = tile_of(pair, 128), tile_of(pair + heads2, 128)
            value_at = tile_of(pair + 2 * heads2, 128)
            queries, keys_in, values_in = qkv[c, :, at], qkv[c, :, key_at], qkv[c, :, value_at]
            grad = d_context[:, at]
            queries_t, grad_t = queries.T, grad.T
            d_queries, keys_t, values_t = [], [], []
            for h in range(2):
                pick = jnp.where(low_lanes == (h == 0), 1.0, 0.0).astype(low)
                soft = probs[slot, h]
                soft_wide = soft.astype(f32)
                d_soft = dot_nt(grad * pick, values_in)
                delta = jnp.sum(soft_wide * d_soft, axis=-1, keepdims=True)
                d_scores = (soft_wide * (d_soft - delta)).astype(low)
                part = slice(h * HD, (h + 1) * HD)
                values_t.append(dot_nn(grad_t[part], soft))
                keys_t.append(dot_nn(queries_t[part], d_scores))
                d_queries.append(dot_nn(d_scores, keys_in))
            scale = HD**-0.5
            query_grad = (jnp.where(low_lanes, d_queries[0], d_queries[1]) * scale).astype(low)
            value_grad = jnp.concatenate(values_t, axis=0).T.astype(low)
            d_qkv[:, at] = query_grad
            d_qkv[:, key_at] = (jnp.concatenate(keys_t, axis=0) * scale).T.astype(low)
            d_qkv[:, value_at] = value_grad
            small[3:4, at] += column_sum(query_grad.astype(f32))
            small[4:5, at] += column_sum(value_grad.astype(f32))

            @pl.when(step + slots < pairs_total)
            def _():
                probs_load(step + slots).start()

            return carry

        lax.fori_loop(0, heads2, attend, 0)
        for copy in own[:3]:
            copy.start()

        @pl.when(c == 0)
        def _():
            loads[3].wait()

        state[3].wait()
        for h in range(2):
            rows = pl.ds(h * half, half)

            def in_tile(j, carry):
                at = tile_of(j, 256)
                wide_grad[rows, at] = dot_nt(d_qkv[rows, :], wqkv[at, :])
                return carry

            lax.fori_loop(0, width // 256, in_tile, 0)

            def last_tile(i, carry):
                part = tile_of(i, 64)
                total = norm_back(x.at[c], d_middle[part, :], 0, 2, part, None)
                d_low[c, part, :] = total.astype(low)
                return carry

            lax.fori_loop(h * (half // 64), (h + 1) * (half // 64), last_tile, 0)

            @pl.when(section == 1)
            def _():
                send_half(c, h).start()

        dx_save(c).start()
        return carry

    lax.fori_loop(0, clips, clip, 0)
    for copy in saves(clips - 1):
        copy.wait()
    for c in range(clips):
        dx_save(c).wait()
        for h in range(2):
            @pl.when(section == 1)
            def _():
                send_half(c, h).wait_send()


def unit_rows(members, width, stack_rows):
    return math.gcd(stack_rows // members, width)


def grads_kernel(
    members, info, left, right, dx, feat, chosen, cols, small_in, up_sums, stats, stack_h, feat_grad,
    turned, result, embed, small, blank, unit_sem, embed_sem, small_sem,
):
    low = jnp.bfloat16
    f32 = jnp.float32
    b = pl.program_id(0)
    width = left.shape[2]
    total_rows = 12 * width
    unit = unit_rows(members, width, total_rows)
    share = total_rows // members
    per_block, per_member = width // unit, share // unit
    embed_share = embed.shape[0] // members

    def unit_copy(block, u):
        spot = block * per_block + u
        slot = lax.rem(block, 2)
        return pltpu.make_async_copy(
            result.at[slot, pl.ds(u * unit, unit)],
            stack_h.at[spot // per_member, pl.ds(pl.multiple_of(
                lax.rem(spot, per_member) * unit, 16), unit)],
            unit_sem.at[slot, u])

    @pl.when((b == 0) | (b == 3) | (b == 4) | ((b > 7) & (b < 12)))
    def _():
        def turn(i, carry):
            at = tile_of(i, 128)
            turned[at, :] = left[0, :, at].T
            return carry

        lax.fori_loop(0, width // 128, turn, 0)

    @pl.when(b < 12)
    def _():
        @pl.when(b > 1)
        def _():
            for u in range(per_block):
                unit_copy(b - 2, u).wait()

        def part(i, carry):
            at = tile_of(i, 128)
            result[lax.rem(b, 2), at, :] = dot_nn(turned[at, :], right[0]).astype(low)
            return carry

        lax.fori_loop(0, width // 128, part, 0)
        for u in range(per_block):
            unit_copy(b, u).start()

    @pl.when(b == 12)
    def _():
        for block in (10, 11):
            for u in range(per_block):
                unit_copy(block, u).wait()
        feat_width = feat.shape[2]
        first = info[2].astype(f32)
        clips = feat.shape[0]
        blank[...] = jnp.zeros_like(blank)
        small[...] = jnp.zeros_like(small)
        small[0:8, :] = small_in[...]
        for i in range(up_sums.shape[1] // width):
            small[8 + i : 9 + i, :] = up_sums[:, i * width : (i + 1) * width]
        lane = lax.broadcasted_iota(jnp.int32, (1, width), 1)
        row = jnp.zeros((1, width), f32)
        for i in range(3):
            row = jnp.where(lane == i, jnp.sum(stats[i : i + 1, :], axis=1, keepdims=True), row)
        count = jnp.zeros((1, 1), f32)
        for c in range(clips):
            count = count + jnp.sum(cols[c][:, 1:2], axis=0, keepdims=True)
        small[15:16, :] = jnp.where(lane == 3, count, row)
        weight_sum = [jnp.zeros((feat_width, width), f32)] * 2
        place_sum = jnp.zeros(dx.shape[1:], f32)
        for c in range(clips):
            grad = dx[c]
            kept = jnp.where(cols[c][:, 0:1] > 0.0, jnp.zeros_like(grad), grad)
            feat_grad[c] = dot_nt(kept, chosen[c]).astype(low)
            second = info[c].astype(f32)
            flags = ((1.0 - second) * first, second * first)
            wide = dot_nn(feat[c].T, kept)
            sums = column_sum(kept.astype(f32))
            for kind in range(2):
                weight_sum[kind] = weight_sum[kind] + flags[kind] * wide
                small[12 + kind : 13 + kind, :] += flags[kind] * sums
            small[14:15, :] += first * (column_sum(grad.astype(f32)) - sums)
            place_sum = place_sum + grad.astype(f32)
        embed[0:feat_width, :] = weight_sum[0].astype(low)
        embed[feat_width : 2 * feat_width, :] = weight_sum[1].astype(low)
        embed[2 * feat_width :, :] = (place_sum * first).astype(low)
        blank[0] = small[...].astype(low)
        copies = []
        for w in range(members):
            copies.append(pltpu.make_async_copy(
                embed.at[pl.ds(w * embed_share, embed_share)],
                stack_h.at[w, pl.ds(share, embed_share)], embed_sem.at[w]))
            copies.append(pltpu.make_async_copy(
                blank.at[min(w, 1)],
                stack_h.at[w, pl.ds(share + embed_share, SMALL)], small_sem.at[w]))
        for copy in copies:
            copy.start()
        for copy in copies:
            copy.wait()


def unpack_kernel(per_block, blocks, total, attend, project, up, down):
    b = pl.program_id(0) // per_block
    values = total[0].astype(jnp.float32)

    @pl.when(b < 3)
    def _():
        attend[...] = values

    @pl.when(b == 3)
    def _():
        project[...] = values

    @pl.when((b > 3) & (b < 4 + blocks))
    def _():
        up[...] = values

    @pl.when(b > 3 + blocks)
    def _():
        down[...] = values


ANY = pl.BlockSpec(memory_space=pl.ANY)
VMEM = pl.BlockSpec(memory_space=pltpu.VMEM)
SMEM = pl.BlockSpec(memory_space=pltpu.SMEM)
LOW = jnp.bfloat16
WIDE = jnp.float32


def shaped(kind, *dims):
    return jax.ShapeDtypeStruct(dims, kind)


def run_forward(features, chosen, pos_embed, weights, cols, kind_offset, mask_row, bias_row,
                live_row, gains, vectors, up_bias):
    clips, length, feat_width = features.shape
    width, feed = weights[2].shape
    blocks = feed // width
    dma = pltpu.SemaphoreType.DMA
    vm = pltpu.VMEM
    return pl.pallas_call(
        forward_kernel,
        out_shape=(
            shaped(LOW, 3 + blocks, clips * length, width),
            shaped(WIDE, clips, length, width),
            shaped(LOW, clips, length, 3 * width),
            shaped(LOW, clips, H, length, length),
            shaped(WIDE, clips, length, width),
            shaped(LOW, clips, length, feed),
            shaped(LOW, clips, length, width // 2),
            shaped(WIDE, 8, width),
        ),
        in_specs=[ANY] * 7 + [VMEM] * 8,
        out_specs=(ANY,) * 7 + (VMEM,),
        scratch_shapes=[
            vm(features.shape, LOW), vm(chosen.shape, LOW), vm(pos_embed.shape, WIDE),
            vm((width, 3 * width), LOW), vm((width, width), LOW), vm((width, feed), LOW),
            vm((feed, width), LOW),
            vm((length, width), WIDE), vm((length, width), LOW), vm((length, 3 * width), LOW),
            vm((2, 2, length, length), LOW), vm((length, width), LOW), vm((length, width), WIDE),
            vm((length, width), LOW), vm((length, feed), LOW), vm((length, feed), LOW),
            vm((clips, length, width), LOW), vm((clips, length, width), LOW),
            dma((7,)), dma((7 + blocks,)), dma((2,)), dma((clips, 2)), dma((clips, 2)),
            dma((clips, 2)), dma((clips, 2)), dma((clips, 2)),
        ],
        compiler_params=pltpu.CompilerParams(
            collective_id=1, has_side_effects=True, vmem_limit_bytes=56 * 2**20
        ),
    )(features, chosen, pos_embed, *weights, cols, kind_offset, mask_row, bias_row, live_row,
      gains, vectors, up_bias)


def run_backward(cotangent, weights, x, qkv, probs, middle, slope, gains):
    clips, length, width = cotangent.shape
    feed = weights[2].shape[1]
    blocks = feed // width
    dma = pltpu.SemaphoreType.DMA
    vm = pltpu.VMEM
    return pl.pallas_call(
        backward_kernel,
        out_shape=(
            shaped(LOW, 5 + blocks, clips * length, width),
            shaped(LOW, clips, length, width),
            shaped(WIDE, 8, width),
            shaped(WIDE, 1, feed),
        ),
        in_specs=[ANY] * 10 + [VMEM],
        out_specs=(ANY, ANY, VMEM, VMEM),
        scratch_shapes=[
            vm((width, 3 * width), LOW), vm((width, width), LOW), vm((width, feed), LOW),
            vm((feed, width), LOW),
            vm((clips, length, width), WIDE), vm((clips, length, 3 * width), LOW),
            vm((3, 2, length, length), LOW), vm((clips, length, width), WIDE),
            vm((clips, length, feed), LOW), vm((clips, length, width), LOW),
            vm((length, feed), LOW), vm((length, width), WIDE), vm((length, width), WIDE),
            vm((length, width), LOW), vm((length, width), LOW), vm((length, 3 * width), LOW),
            vm((clips, length, width), LOW),
            dma((4,)), dma((clips, 5)), dma((3,)), dma((5 + blocks,)), dma((clips,)),
            dma((clips, 2)), dma((clips, 2)),
        ],
        compiler_params=pltpu.CompilerParams(
            collective_id=2, has_side_effects=True, vmem_limit_bytes=60 * 2**20
        ),
    )(cotangent, *weights, x, qkv, probs, middle, slope, gains)


def run_grads(members, info, left, right, dx, features, chosen, cols, small, up_sums, stats):
    rows, width = left.shape[1:]
    clips, length, feat_width = features.shape
    embed_rows = 2 * feat_width + length
    total_rows = 12 * width
    share, embed_share = total_rows // members, embed_rows // members
    per_block = width // unit_rows(members, width, total_rows)
    dma = pltpu.SemaphoreType.DMA

    def whole(array):
        zeros = (0,) * array.ndim
        return pl.BlockSpec(array.shape, lambda b: zeros)

    def left_at(b):
        return (jnp.where(b < 3, 0, jnp.where(b == 3, 1, jnp.where(b < 8, 2, jnp.minimum(b, 11) - 5))), 0, 0)

    def right_at(b):
        return (jnp.minimum(b, 8), 0, 0)

    return pl.pallas_call(
        functools.partial(grads_kernel, members),
        grid=(13,),
        out_shape=(
            shaped(LOW, members, share + embed_share + SMALL, width),
            shaped(LOW, clips, length, feat_width),
        ),
        in_specs=[
            SMEM,
            pl.BlockSpec((1, rows, width), left_at),
            pl.BlockSpec((1, rows, width), right_at),
            whole(dx), whole(features), whole(chosen), whole(cols), whole(small), whole(up_sums),
            whole(stats),
        ],
        out_specs=(ANY, pl.BlockSpec((clips, length, feat_width), lambda b: (0, 0, 0))),
        scratch_shapes=[
            pltpu.VMEM((width, rows), LOW),
            pltpu.VMEM((2, width, width), LOW),
            pltpu.VMEM((embed_rows, width), LOW),
            pltpu.VMEM((SMALL, width), WIDE),
            pltpu.VMEM((2, SMALL, width), LOW),
            dma((2, per_block)), dma((members,)), dma((members,)),
        ],
        compiler_params=pltpu.CompilerParams(vmem_limit_bytes=56 * 2**20),
    )(info, left, right, dx, features, chosen, cols, small, up_sums, stats)


def ring_sum(stacked, tail, feature_grad):
    members, rows, width = stacked.shape
    clips, length, feat_width = feature_grad.shape
    n = members // 2
    dma = pltpu.SemaphoreType.DMA
    half = width // 2
    sems = [dma((2, 2, n)) for _ in range(9)]
    sems += [dma((2, 2)), dma((2, 2, n)), dma((2, 2, n)), dma((3,))]
    return pl.pallas_call(
        functools.partial(ring_kernel, n, rows, tail),
        out_shape=(
            shaped(LOW, members, rows, width),
            shaped(LOW, members, tail, width),
            shaped(LOW, clips, length, feat_width // 2),
        ),
        in_specs=[ANY, ANY],
        out_specs=(ANY, ANY, ANY),
        scratch_shapes=[
            pltpu.VMEM((2, n, rows, half), LOW),
            pltpu.VMEM((2, n, rows, half), LOW),
            pltpu.VMEM((2, n - 1, rows, half), LOW),
            sems,
        ],
        compiler_params=pltpu.CompilerParams(
            collective_id=0, has_side_effects=True, vmem_limit_bytes=48 * 2**20
        ),
    )(stacked, feature_grad)


def run_unpack(total, blocks):
    members, rows, width = total.shape
    unit = unit_rows(members, width, 12 * width)
    per_block, per_member = width // unit, 12 * width // members // unit

    def within(first, count):
        def at(u):
            return jnp.clip(u - first * per_block, 0, count * per_block - 1)
        return at

    attend, project, up, down = within(0, 3), within(3, 1), within(4, blocks), within(4 + blocks, blocks)

    def across(at):
        return lambda u: (at(u) % per_block, at(u) // per_block)

    return pl.pallas_call(
        functools.partial(unpack_kernel, per_block, blocks),
        grid=(12 * per_block,),
        out_shape=(
            shaped(WIDE, width, 3 * width), shaped(WIDE, width, width),
            shaped(WIDE, width, blocks * width), shaped(WIDE, blocks * width, width),
        ),
        in_specs=[pl.BlockSpec((1, unit, width), lambda u: (u // per_member, u % per_member, 0))],
        out_specs=(
            pl.BlockSpec((unit, width), across(attend)),
            pl.BlockSpec((unit, width), lambda u: (project(u), 0)),
            pl.BlockSpec((unit, width), across(up)),
            pl.BlockSpec((unit, width), lambda u: (down(u), 0)),
        ),
    )(total)


def local(
    features,
    masked,
    valid,
    kinds,
    embed_weight,
    embed_vectors,
    pos_embed,
    norm_gains,
    vectors,
    qkv_weight,
    out_weight,
    up_weight,
    up_bias,
    down_weight,
    cotangent,
):
    is_first = lax.axis_index("section") == 0
    members = lax.axis_size("wide")
    clips, length, feat_width = features.shape
    width = pos_embed.shape[1]
    weights = (qkv_weight[0], out_weight[0], up_weight[0], down_weight[0])
    blocks = up_weight.shape[2] // width
    chosen = jnp.where(kinds[:, None, None] == 0, embed_weight[0], embed_weight[1])
    kind_offset = jnp.where(kinds[:, None] == 0, embed_vectors[0], embed_vectors[1])[:, None]
    lane = jnp.arange(128)
    cols = jnp.where(
        lane == 0, masked[:, :, None], jnp.where(lane == 1, valid[:, :, None], 0)
    ).astype(WIDE)
    live_row = jnp.where(valid > 0, 0.0, NEG)[:, None]
    rows = vectors[0]
    bias_row = jnp.concatenate([rows[1], jnp.zeros((width,), WIDE), rows[2]])[None]
    left, x, qkv, probs, middle, slope, output, stats = run_forward(
        features, chosen, pos_embed, weights, cols, kind_offset, embed_vectors[2:3], bias_row,
        live_row, norm_gains[0], rows, up_bias)
    right, dx, small, up_sums = run_backward(
        cotangent, weights, x, qkv, probs, middle, slope, norm_gains[0])
    info = jnp.concatenate([kinds, is_first.astype(jnp.int32)[None]])
    stacked, feature_grad = run_grads(
        members, info, left, right, dx, features, chosen, cols, small, up_sums, stats)
    embed_share = (2 * feat_width + length) // members
    tail = embed_share + SMALL
    total, cross, feature_out = ring_sum(stacked, tail, feature_grad)
    attend_total, project_total, up_total, down_total = run_unpack(total, blocks)
    ends = jnp.where(is_first, total[:, -tail:], cross)
    embed_total = ends[:, :embed_share].reshape(-1, width).astype(WIDE)
    small_total = total[0, -SMALL:].astype(WIDE)
    stat_row = small_total[15]
    rms_out = jnp.sqrt(stat_row[0:3] / (stat_row[3] * width))[None]
    return (
        output,
        feature_out,
        embed_total[: 2 * feat_width].reshape(2, feat_width, width),
        ends[0, embed_share + 12 : embed_share + 15].astype(WIDE),
        embed_total[2 * feat_width :],
        small_total[None, 0:2],
        small_total[None, 2:8],
        attend_total[None],
        project_total[None],
        up_total[None],
        small_total[8 : 8 + blocks].reshape(1, -1),
        down_total[None],
        rms_out,
    )


def solution(mesh):
    return jax.shard_map(
        local,
        mesh=mesh,
        in_specs=(
            P("wide", None, None),
            P("wide", None),
            P("wide", None),
            P("wide"),
            P(),
            P(),
            P(),
            P("section", None, None),
            P("section", None, None),
            P("section", None, None),
            P("section", None, None),
            P("section", None, None),
            P("section", None),
            P("section", None, None),
            P("wide", None, None),
        ),
        out_specs=(
            P("wide", None, "section"),
            P("wide", None, "section"),
            P(),
            P(),
            P(),
            P("section", None, None),
            P("section", None, None),
            P("section", None, None),
            P("section", None, None),
            P("section", None, None),
            P("section", None),
            P("section", None, None),
            P("section", None),
        ),
        check_vma=False,
    )
```

time: 888 us -> 493 us (0.56)
  matrix products: 316 us -> 0 us
  Pallas kernels: 170 us -> 471 us
  other arithmetic: 163 us -> 8.04 us
  local copies, waits for them, and re-layouts: 164 us -> 11.5 us
  waiting for transfers between devices: 54.2 us -> 0 us
    dot_general x62 -> x0, matrix products: 316 us -> none  [the longest x12 85.2 us: matmul_plain(): return jnp.dot(left, right, preferred_element_type=jnp.float32)]
    pallas_call x0 -> x4, Pallas kernels: none -> 302 us  [the longest x1 116 us: run_forward(): pl.pallas_call(forward_kernel, out_shape=(shaped(LOW, 3 + blocks, clips *...]
    concatenate x9 -> x2, other arithmetic: 76.6 us -> 0.59 us  [the longest x1 0.59 us: local(): info = jnp.concatenate([kinds, is_first.astype(jnp.int32)[None]])]
    ppermute x6 -> x0, waiting for transfers between devices: 54.2 us -> none  [from_partner(): return lax.ppermute(block, axis, route)]
    convert_element_type x11 -> x4, other arithmetic: 40.2 us -> 2.81 us  [the longest x1 1.13 us: local(): cols = jnp.where(lane == 0, masked[:, :, None], jnp.where(lane == 1, vali...]
    unnamed x466 -> x18, local copies, waits for them, and re-layouts: 32.5 us -> 4.5 us
    convert_element_type x7 -> x0, local copies, waits for them, and re-layouts: 25.9 us -> none  [the longest x3 13.3 us: layer_forward(): (matmul_plain(normed, attend_weight) + in_offset).astype(jnp.bfloat16)]
    transpose x3 -> x0, local copies, waits for them, and re-layouts: 24.8 us -> none  [the longest x1 13.4 us: joined(): rows.reshape(count, width, width).transpose(1, 0, 2)]
  transfers between devices with their start and end apart: 6 -> 0, of which waited for: 5 -> 0; matrix products, arithmetic and copies ran while one was open for 20% -> 0% of each run, Pallas kernels for 0% -> 0%
where the time goes in v2:
time: 493 us; the launch traced here: 492 us
  Pallas kernels  471 us (96%)
  local copies, waits for them, and re-layouts  11.5 us (2%)
  other arithmetic  8.04 us (2%)
    pallas_call x1, Pallas kernels, ring_sum(): pl.pallas_call(functools.partial(ring_kernel, n, rows, tail), out_shape=(...  170 us
    pallas_call x1, Pallas kernels, run_forward(): pl.pallas_call(forward_kernel, out_shape=(shaped(LOW, 3 + blocks, clips *...  116 us
    pallas_call x1, Pallas kernels, run_backward(): pl.pallas_call(backward_kernel, out_shape=(shaped(LOW, 5 + blocks, clips...  111 us
    pallas_call x1, Pallas kernels, run_grads(): pl.pallas_call(functools.partial(grads_kernel, members), grid=(13,), out_...  41.3 us
    pallas_call x1, Pallas kernels, run_unpack(): pl.pallas_call(functools.partial(unpack_kernel, per_block, blocks), grid=...  32.9 us

profile of v2, /device:TPU:0, one launch (start us, length us, event | category | flops | bytes accessed | tf_op | source)
XLA Modules:
  0.0 492.1 jit_solution(17837999258111843474)
XLA Ops:
  0.6 0.0 copy-start.4
  0.7 0.0 copy-start.3
  0.7 0.0 copy-start.2
  0.7 1.4 slice_reduce_fusion.3
  2.1 0.7 broadcast_compare_fusion
  2.7 0.7 broadcast_select_fusion.1.kind_offset
  3.4 1.2 slice_bitcast_fusion.1
  4.6 1.0 broadcast_select_fusion.chosen_h.chosen
  5.6 0.0 copy-done.4
  5.6 0.0 copy-done.3
  5.6 1.1 select_convert_fusion.cols
  6.8 0.0 copy-done.2
  6.8 0.6 broadcast_in_dim.115.bias_row
  7.4 0.6 copy.32
  8.0 0.6 broadcast_in_dim.118.live_row
  8.6 116.0 %shard_map.246 = (bf16[7,1024,768]{2,1,0:T(8,128)(2,1)}, f32[2,512,768]{2,1,0:T(8,128)}, bf16[2,512,2304]{2,1,0:T(8,128)(2,1)}, bf16[2,12,512,512]{3,2,1,0:T(8,1...) custom-call(bf16[2,512,256]{2,1,0:T(8,128)(2,1)} %feat.1, ...), custom_call_target="tpu_custom_call" | custom-call | tf_op jit(solution)/shard_map/pallas_call | solution.py:895
  124.7 0.0 copy-start.5
  124.7 111.3 %shard_map.247 = (bf16[9,1024,768]{2,1,0:T(8,128)(2,1)}, bf16[2,512,768]{2,1,0:T(8,128)(2,1)}, f32[8,768]{1,0:T(8,128)}, f32[1,3072]{1,0:T(1,128)}) custom-call(bf16[2,512,768]{2,1,0:T(8,128)(2,1)} %cot_h.1, bf16[768,2304]{1,0:T(8,128)(2,1)} %bitcast.35, bf16[768,768]{1,0:T(8,128)(2,1)} %bitcast.37, bf16[768,3072]{1,0:T(8,128)(2,1)} %bitcast.31, ...), custom_call_target="tpu_custom_call" | custom-call | tf_op jit(solution)/shard_map/pallas_call | solution.py:933
  236.0 0.0 copy-done.5
  236.0 0.6 pad_add_fusion.info
  236.6 41.3 %shard_map.248 = (bf16[16,656,768]{2,1,0:T(8,128)(2,1)}, bf16[2,512,256]{2,1,0:T(8,128)(2,1)}) custom-call(s32[3]{0:T(128)} %pad_add_fusion.info, bf16[7,1024,768]{2,1,0:T(8,128)(2,1)} %get-tuple-element.35.left, bf16[9,1024,768]{2,1,0:T(8,128)(2,1)} %get-tuple-element.41.right, bf16[2,512,768]{2,1,0:T(8,128)(2,1)} %get-tuple-element.42.dx, ...), custom_call_target="tpu_custom_call" | custom-call | tf_op jit(solution)/shard_map/pallas_call | solution.py:980
  277.9 0.0 copy-start
  277.9 1.0 copy-done
  278.9 169.6 %shard_map.249 = (bf16[16,656,768]{2,1,0:T(8,128)(2,1)}, bf16[16,80,768]{2,1,0:T(8,128)(2,1)S(1)}, bf16[2,512,128]{2,1,0:T(8,128)(2,1)S(1)}) custom-call(bf16[16,656,768]{2,1,0:T(8,128)(2,1)} %get-tuple-element.46.g_ref, bf16[2,512,256]{2,1,0:T(8,128)(2,1)S(1)} %copy-done), custom_call_target="tpu_custom_call" | custom-call | tf_op jit(solution)/shard_map/pallas_call | solution.py:1015
  448.6 0.7 fusion
  449.3 0.6 slice.101
  450.6 0.5 fusion.2
  451.1 32.9 %shard_map.250 = (f32[768,2304]{1,0:T(8,128)}, f32[768,768]{1,0:T(8,128)}, f32[768,3072]{1,0:T(8,128)}, f32[3072,768]{1,0:T(8,128)}) custom-call(bf16[16,656,768]{2,1,0:T(8,128)(2,1)} %get-tuple-element.49.total), custom_call_target="tpu_custom_call" | custom-call | tf_op jit(solution)/shard_map/pallas_call | solution.py:1051
  484.0 1.8 slice_select_fusion
  485.7 0.3 slice_convert_fusion
  486.1 0.0 copy-start.1
  486.1 2.0 fusion.3
  488.1 0.6 fusion.1
  488.7 0.6 copy.28
  489.3 0.6 copy.30
  489.9 0.6 slice.97
  490.5 0.0 copy-done.1
  490.5 0.9 copy.35
  491.4 0.7 copy.36
  (7 shorter events, 0.0 us)
Async XLA Ops:
  0.6 5.0 %copy-start.4 = (s32[2,512]{1,0:T(2,128)S(1)}, s32[2,512]{1,0:T(2,128)}, u32[]{:S(2)}) copy-start(s32[2,512]{1,0:T(2,128)} %param.16) | copy-start | bytes 12292
  0.7 5.0 %copy-start.3 = (s32[2,512]{1,0:T(2,128)S(1)}, s32[2,512]{1,0:T(2,128)}, u32[]{:S(2)}) copy-start(s32[2,512]{1,0:T(2,128)} %param.17) | copy-start | bytes 12292
  0.7 6.1 %copy-start.2 = (f32[1,6,768]{2,0,1:T(1,128)S(1)}, f32[1,6,768]{2,0,1:T(1,128)}, u32[]{:S(2)}) copy-start(f32[1,6,768]{2,0,1:T(1,128)} %param.23) | copy-start | bytes 55300
  124.7 111.3 %copy-start.5 = (s32[2]{0:T(128)S(1)}, s32[2]{0:T(128)}, u32[]{:S(2)}) copy-start(s32[2]{0:T(128)} %param.18) | copy-start | bytes 28
  277.9 1.0 copy-start
  486.1 4.4 copy-start.1

commit v3 on v2

--- a/solution.py
+++ b/solution.py
@@ -12,195 +12,14 @@
 HD = 64
 EPS = 1e-06
 NEG = -1000000000.0
+
+
 MESH = pl.DeviceIdType.MESH
 SMALL = 16
 
 
-def ring_kernel(n, rows, tail, g_ref, f_ref, o_ref, e_ref, h_ref, own, part, ring, sems):
-    (own_sem, part_send, part_recv, ring_send, ring_recv, gather_send, gather_recv,
-     pair_send, pair_recv, keep_sem, cross_send, cross_recv, feat_sem) = sems
-    columns = g_ref.shape[2] // 2
-    me = lax.axis_index("wide")
-    section = lax.axis_index("section")
-    chip, core = me // 2, me % 2
-    place = jnp.where(chip % 2 == 0, chip // 2, n - 1 - chip // 2)
-
-    def member(position):
-        position = lax.rem(position + 2 * n, n)
-        return jnp.where(2 * position < n, 2 * position, 2 * (n - 1 - position) + 1) * 2 + core
-
-    right, left = member(place + 1), member(place - 1)
-    other = chip * 2 + 1 - core
-    target = (right, left)
-
-    barrier = pltpu.get_barrier_semaphore()
-    for peer in (right, left, other):
-        pl.semaphore_signal(barrier, inc=1, device_id={"wide": peer}, device_id_type=MESH)
-    pl.semaphore_signal(barrier, inc=1, device_id={"section": 1 - section}, device_id_type=MESH)
-    pl.semaphore_wait(barrier, 4)
-
-    half = -(-rows // 32) * 16
-    spans = ((0, half), (half, rows - half))
-    streams = [(q, d) for q in range(2) for d in range(2)]
-
-    def turn(position):
-        return lax.rem(position + 2 * n, n)
-
-    def reduce_at(d, step):
-        return turn(place - step) if d == 0 else turn(place + step)
-
-    def gather_at(d, index):
-        return turn(place + 1 - index) if d == 0 else turn(place - 1 + index)
-
-    def span(q):
-        return pl.ds(*spans[q])
-
-    def cols(d):
-        return pl.ds(d * columns, columns)
-
-    def remote(src, dst, send, recv, device):
-        return pltpu.make_async_remote_copy(
-            src_ref=src, dst_ref=dst, send_sem=send, recv_sem=recv,
-            device_id=device, device_id_type=MESH)
-
-    def own_copy(q, d, s):
-        return pltpu.make_async_copy(
-            g_ref.at[reduce_at(d, s) * 2 + core, span(q), cols(d)],
-            own.at[d, s, span(q)], own_sem.at[d, q, s])
-
-    def part_copy(q, d, s):
-        return remote(
-            g_ref.at[reduce_at(d, s) * 2 + 1 - core, span(q), cols(d)],
-            part.at[d, s, span(q)], part_send.at[d, q, s], part_recv.at[d, q, s],
-            {"wide": other})
-
-    def ring_copy(q, d, s):
-        return remote(
-            own.at[d, s, span(q)], ring.at[d, s, span(q)],
-            ring_send.at[d, q, s], ring_recv.at[d, q, s], {"wide": target[d]})
-
-    def spot(q, d, index, which):
-        return o_ref.at[gather_at(d, index) * 2 + which, span(q), cols(d)]
-
-    def source(q, d, index):
-        return own.at[d, n - 1, span(q)] if index == 0 else spot(q, d, index, core)
-
-    def gather_copy(q, d, index):
-        return remote(
-            source(q, d, index), spot(q, d, index, core),
-            gather_send.at[d, q, index], gather_recv.at[d, q, index], {"wide": target[d]})
-
-    def gather_landed(q, d, index):
-        return remote(
-            source(q, d, 0), spot(q, d, index + 1, core),
-            gather_send.at[d, q, index], gather_recv.at[d, q, index], {"wide": target[d]})
-
-    def pair_copy(q, d, index):
-        return remote(
-            source(q, d, index), spot(q, d, index, core),
-            pair_send.at[d, q, index], pair_recv.at[d, q, index], {"wide": other})
-
-    def pair_landed(q, d, index):
-        return remote(
-            source(q, d, 0), spot(q, d, index, 1 - core),
-            pair_send.at[d, q, index], pair_recv.at[d, q, index], {"wide": other})
-
-    def keep_copy(q, d):
-        return pltpu.make_async_copy(
-            own.at[d, n - 1, span(q)], spot(q, d, 0, core), keep_sem.at[d, q])
-
-    def cross_copy(d, index, mine):
-        which = core if mine else 1 - core
-        at = gather_at(d, index) * 2 + which
-        if mine and index == 0:
-            src = own.at[d, n - 1, pl.ds(rows - tail, tail)]
-        else:
-            src = o_ref.at[at, pl.ds(rows - tail, tail), cols(d)]
-        lane = 0 if mine else 1
-        return remote(
-            src, e_ref.at[at, :, cols(d)],
-            cross_send.at[d, lane, index], cross_recv.at[d, lane, index],
-            {"section": 1 - section})
-
-    feat_half = h_ref.shape[2]
-    feat_keep = pltpu.make_async_copy(
-        f_ref.at[:, :, pl.ds(0, feat_half)], h_ref, feat_sem.at[0])
-    feat_send = remote(
-        f_ref.at[:, :, pl.ds(feat_half, feat_half)], h_ref, feat_sem.at[1], feat_sem.at[2],
-        {"section": 1 - section})
-
-    @pl.when(section == 0)
-    def _():
-        feat_keep.start()
-        feat_send.start()
-
-    for s in range(n):
-        for q, d in streams:
-            own_copy(q, d, s).start()
-            part_copy(q, d, s).start()
-
-    for s in range(n):
-        for q, d in streams:
-            own_copy(q, d, s).wait()
-            part_copy(q, d, s).wait_recv()
-            if s:
-                ring_copy(q, d, s - 1).wait_recv()
-
-            def add(tile, carry, q=q, d=d, s=s):
-                at = pl.ds(pl.multiple_of(spans[q][0] + tile * 16, 16), 16)
-                total = own[d, s, at].astype(jnp.float32) + part[d, s, at].astype(jnp.float32)
-                if s:
-                    total = total + ring[d, s - 1, at].astype(jnp.float32)
-                own[d, s, at] = total.astype(own.dtype)
-                return carry
-
-            lax.fori_loop(0, spans[q][1] // 16, add, 0)
-            if s < n - 1:
-                ring_copy(q, d, s).start()
-            else:
-                gather_copy(q, d, 0).start()
-                pair_copy(q, d, 0).start()
-                keep_copy(q, d).start()
-                if q == 1:
-                    cross_copy(d, 0, True).start()
-
-    for t in range(n - 1):
-        for q, d in streams:
-            gather_landed(q, d, t).wait_recv()
-            if t < n - 2:
-                gather_copy(q, d, t + 1).start()
-            pair_copy(q, d, t + 1).start()
-            if q == 1:
-                cross_copy(d, t + 1, True).start()
-        for q, d in streams:
-            pair_landed(q, d, t).wait_recv()
-            if q == 1:
-                cross_copy(d, t, False).start()
-    for q, d in streams:
-        pair_landed(q, d, n - 1).wait_recv()
-        if q == 1:
-            cross_copy(d, n - 1, False).start()
-
-    @pl.when(section == 0)
-    def _():
-        feat_keep.wait()
-        feat_send.wait_send()
-
-    @pl.when(section == 1)
-    def _():
-        feat_send.wait_recv()
-
-    for q, d in streams:
-        keep_copy(q, d).wait()
-        for s in range(n):
-            part_copy(q, d, s).wait_send()
-            pair_copy(q, d, s).wait_send()
-            if s < n - 1:
-                ring_copy(q, d, s).wait_send()
-                gather_copy(q, d, s).wait_send()
-            if q == 1:
-                for mine in (True, False):
-                    cross_copy(d, s, mine).wait()
+def unit_rows(members, width):
+    return math.gcd(12 * width // members, width)
 
 
 def dot_nn(left, right):
@@ -215,6 +34,15 @@
 
 def tile_of(index, size):
     return pl.ds(pl.multiple_of(index * size, size), size)
+
+
+def loop(count, body, unroll):
+    def step(i, carry):
+        for u in range(unroll):
+            body(i * unroll + u, 0)
+        return carry
+
+    lax.fori_loop(0, count // unroll, step, 0)
 
 
 def column_sum(values):
@@ -337,7 +165,7 @@
                 x[rows, :] = jnp.where(hidden > 0.0, mask_row[...], lifted) + pos[rows, :]
                 return carry
 
-            lax.fori_loop(0, length // 128, tile, 0)
+            loop(length // 128, tile, 4)
 
         @pl.when(section == 1)
         def _():
@@ -354,7 +182,7 @@
                 x[rows, :] = landed[c, rows, :].astype(jnp.float32)
                 return carry
 
-            lax.fori_loop(0, length // 64, tile, 0)
+            loop(length // 64, tile, 4)
 
         own = saves(c)
         own[0].start()
@@ -370,7 +198,7 @@
                 target[rows, :] = (values * scale * gain + offset).astype(low)
                 return carry
 
-            lax.fori_loop(first, first + count, tile, 0)
+            loop(count, lambda i, carry: tile(first + i, carry), 4)
 
         norm_rows(x, normed, 0, 0, 0, length // 64)
         own[1].start()
@@ -385,7 +213,7 @@
             qkv[:, at] = (dot_nn(normed[...], wqkv[:, at]) + bias_row[:, at]).astype(low)
             return carry
 
-        lax.fori_loop(0, 3 * width // 256, qkv_tile, 0)
+        loop(3 * width // 256, qkv_tile, 9)
         own[2].start()
         after_first(3)
 
@@ -429,7 +257,7 @@
             stats[1:2, at] += column_sum(branch * branch * live)
             return carry
 
-        lax.fori_loop(0, width // 256, out_tile, 0)
+        loop(width // 256, out_tile, 3)
         own[4].start()
         for index in range(5, 7 + blocks):
             after_first(index)
@@ -453,7 +281,7 @@
                 slope[rows, at] = steep.astype(low)
                 return carry
 
-            lax.fori_loop(0, feed // 256, up_tile, 0)
+            loop(feed // 256, up_tile, 6)
             if h == 1:
                 for copy in own[6:]:
                     copy.start()
@@ -468,7 +296,7 @@
                 y[c, rows, at] = total.astype(low)
                 return carry
 
-            lax.fori_loop(0, width // 256, down_tile, 0)
+            loop(width // 256, down_tile, 3)
 
             @pl.when(section == 0)
             def _():
@@ -499,11 +327,11 @@
 
 
 def backward_kernel(
-    cot_h, wqkv_h, wout_h, wup_h, wdown_h, x_h, qkv_h, probs_h, middle_h, slope_h, gains,
-    right_h, dx_h, small, up_sums,
+    cot_h, wqkv_h, wout_h, wup_h, wdown_h, x_h, qkv_h, probs_h, middle_h, slope_h, left_h, gains,
+    right_h, dx_h, turned_h, small, up_sums,
     wqkv, wout, wup, wdown, x, qkv, probs, middle, slope, g,
-    d_hidden, wide_grad, d_middle, d_branch, d_context, d_qkv, d_low,
-    load_sem, state_sem, probs_sem, save_sem, dx_sem, send_sem, recv_sem,
+    d_hidden, wide_grad, d_middle, d_branch, d_context, d_qkv, d_low, upright, turned,
+    turn_sem, load_sem, state_sem, probs_sem, save_sem, dx_sem, send_sem, recv_sem,
 ):
     low = jnp.bfloat16
     f32 = jnp.float32
@@ -585,6 +413,29 @@
         grad = grad * gain
         return carried + scale * (grad - row_mean(grad) - values * row_mean(grad * values))
 
+    def turn_lefts():
+        def block(b, carry):
+            come = pltpu.make_async_copy(left_h.at[b], upright, turn_sem.at[0])
+            come.start()
+            come.wait()
+
+            def piece(i, carry):
+                at = tile_of(i, 128)
+                turned[at, :] = upright[:, at].T
+                return carry
+
+            loop(width // 128, piece, 2)
+            leave = pltpu.make_async_copy(turned, turned_h.at[b], turn_sem.at[1])
+            leave.start()
+            leave.wait()
+            return carry
+
+        lax.fori_loop(0, left_h.shape[0], block, 0)
+
+    @pl.when(section == 0)
+    def _():
+        turn_lefts()
+
     def clip(c, carry):
         def after_first(lo, hi):
             @pl.when(c > 0)
@@ -626,14 +477,14 @@
                 up_sums[:, at] += column_sum(grad.astype(f32))
                 return carry
 
-            lax.fori_loop(0, feed // 256, feed_tile, 0)
+            loop(feed // 256, feed_tile, 6)
 
             def in_tile(j, carry):
                 at = tile_of(j, 256)
                 wide_grad[rows, at] = dot_nt(d_hidden[rows, :], wup[at, :])
                 return carry
 
-            lax.fori_loop(0, width // 256, in_tile, 0)
+            loop(width // 256, in_tile, 3)
 
         after_first(3, 4)
         for copy in own[4:-1]:
@@ -650,7 +501,7 @@
             small[7:8, :] += column_sum(grad_in)
             return carry
 
-        lax.fori_loop(0, length // 64, middle_tile, 0)
+        loop(length // 64, middle_tile, 4)
         own[3].start()
 
         @pl.when(c == 0)
@@ -662,7 +513,7 @@
             d_context[:, at] = dot_nt(d_branch[...], wout[at, :]).astype(low)
             return carry
 
-        lax.fori_loop(0, width // 256, context_tile, 0)
+        loop(width // 256, context_tile, 3)
         state[2].wait()
         after_first(0, 3)
 
@@ -719,7 +570,7 @@
                 wide_grad[rows, at] = dot_nt(d_qkv[rows, :], wqkv[at, :])
                 return carry
 
-            lax.fori_loop(0, width // 256, in_tile, 0)
+            loop(width // 256, in_tile, 3)
 
             def last_tile(i, carry):
                 part = tile_of(i, 64)
@@ -727,7 +578,7 @@
                 d_low[c, part, :] = total.astype(low)
                 return carry
 
-            lax.fori_loop(h * (half // 64), (h + 1) * (half // 64), last_tile, 0)
+            loop(half // 64, lambda i, carry: last_tile(h * (half // 64) + i, carry), 4)
 
             @pl.when(section == 1)
             def _():
@@ -737,6 +588,11 @@
         return carry
 
     lax.fori_loop(0, clips, clip, 0)
+
+    @pl.when(section == 1)
+    def _():
+        turn_lefts()
+
     for copy in saves(clips - 1):
         copy.wait()
     for c in range(clips):
@@ -747,67 +603,228 @@
                 send_half(c, h).wait_send()
 
 
-def unit_rows(members, width, stack_rows):
-    return math.gcd(stack_rows // members, width)
-
-
-def grads_kernel(
-    members, info, left, right, dx, feat, chosen, cols, small_in, up_sums, stats, stack_h, feat_grad,
-    turned, result, embed, small, blank, unit_sem, embed_sem, small_sem,
+def sums_kernel(
+    members, info, turned_h, right_h, dx_h, feat_h, chosen_h, cols, small_in, up_sums, stats,
+    o_ref, t_ref, e_ref, h_ref,
+    lefts, rights, own, spare, part, ring, tails, tail_own, tail_part, tail_ring,
+    dx, feat, chosen, feat_grad, embed, small, sems,
 ):
+    (load_sem, embed_sem, part_send, part_recv, ring_send, ring_recv, gather_send, gather_recv,
+     pair_send, pair_recv, keep_sem, cross_send, cross_recv, feat_sem) = sems
     low = jnp.bfloat16
     f32 = jnp.float32
-    b = pl.program_id(0)
-    width = left.shape[2]
-    total_rows = 12 * width
-    unit = unit_rows(members, width, total_rows)
-    share = total_rows // members
+    n = members // 2
+    share, columns = own.shape[2:]
+    width = 2 * columns
+    tail = tails.shape[1]
+    unit = unit_rows(members, width)
     per_block, per_member = width // unit, share // unit
-    embed_share = embed.shape[0] // members
-
-    def unit_copy(block, u):
-        spot = block * per_block + u
-        slot = lax.rem(block, 2)
-        return pltpu.make_async_copy(
-            result.at[slot, pl.ds(u * unit, unit)],
-            stack_h.at[spot // per_member, pl.ds(pl.multiple_of(
-                lax.rem(spot, per_member) * unit, 16), unit)],
-            unit_sem.at[slot, u])
-
-    @pl.when((b == 0) | (b == 3) | (b == 4) | ((b > 7) & (b < 12)))
-    def _():
-        def turn(i, carry):
-            at = tile_of(i, 128)
-            turned[at, :] = left[0, :, at].T
+    slots = own.shape[1]
+    clips, length, feat_width = feat.shape
+    me = lax.axis_index("wide")
+    section = lax.axis_index("section")
+    chip, core = me // 2, me % 2
+    place = jnp.where(chip % 2 == 0, chip // 2, n - 1 - chip // 2)
+
+    def member_at(position):
+        position = lax.rem(position + 2 * n, n)
+        return jnp.where(2 * position < n, 2 * position, 2 * (n - 1 - position) + 1) * 2 + core
+
+    right, left = member_at(place + 1), member_at(place - 1)
+    other = chip * 2 + 1 - core
+    target = (right, left)
+
+    barrier = pltpu.get_barrier_semaphore()
+    for peer in (right, left, other):
+        pl.semaphore_signal(barrier, inc=1, device_id={"wide": peer}, device_id_type=MESH)
+    pl.semaphore_signal(barrier, inc=1, device_id={"section": 1 - section}, device_id_type=MESH)
+
+    half = -(-share // 32) * 16
+    spans = ((0, half), (half, share - half))
+    mains = [(q, d) for q in range(2) for d in range(2)]
+    streams = mains + [(2, 0), (2, 1)]
+
+    def turn(position):
+        return lax.rem(position + 2 * n, n)
+
+    def reduce_at(d, step):
+        return turn(place - step) if d == 0 else turn(place + step)
+
+    def gather_at(d, index):
+        return turn(place + 1 - index) if d == 0 else turn(place - 1 + index)
+
+    def span(q):
+        return pl.ds(*spans[q])
+
+    def cols_of(d):
+        return pl.ds(d * columns, columns)
+
+    def remote(src, dst, send, recv, device):
+        return pltpu.make_async_remote_copy(
+            src_ref=src, dst_ref=dst, send_sem=send, recv_sem=recv,
+            device_id=device, device_id_type=MESH)
+
+    def block_of(spot):
+        return spot // per_block
+
+    def operand_copies(d, s):
+        base = reduce_at(d, s) * 2 * per_member
+        first, second = block_of(base), block_of(base + 2 * per_member - 1)
+        copies = []
+        for u in range(2 * per_member):
+            block = block_of(base + u)
+            source = jnp.where(
+                block < 3, 0, jnp.where(block == 3, 1, jnp.where(block < 8, 2, block - 5)))
+            row = pl.multiple_of(lax.rem(base + u, per_block) * unit, 16)
+            copies.append(pltpu.make_async_copy(
+                turned_h.at[source, pl.ds(row, unit)], lefts.at[d, u], load_sem.at[d, u]))
+        for i, block in enumerate((first, second)):
+            copies.append(pltpu.make_async_copy(
+                right_h.at[jnp.minimum(block, 8), :, cols_of(d)], rights.at[d, i],
+                load_sem.at[d, 2 * per_member + i]))
+        return copies
+
+    def load_operands(d, s):
+        for copy in operand_copies(d, s):
+            copy.start()
+
+    def part_copy(d, s):
+        return remote(
+            spare.at[d, lax.rem(s, 2)], part.at[d, s], part_send.at[d, s], part_recv.at[d, s],
+            {"wide": other})
+
+    def ring_copy(q, d, s):
+        if q == 2:
+            src, dst = tail_own.at[d, s], tail_ring.at[d, s]
+        else:
+            src, dst = own.at[d, lax.rem(s, slots), span(q)], ring.at[d, s, span(q)]
+        return remote(src, dst, ring_send.at[d, q, s], ring_recv.at[d, q, s],
+                      {"wide": target[d]})
+
+    def products(d, s, prefetch):
+        for copy in operand_copies(d, s):
+            copy.wait()
+        base = reduce_at(d, s) * 2 * per_member
+        first = block_of(base)
+
+        def side(which, store):
+            def body(u, carry):
+                spot = which * per_member + u
+                tile = dot_nn(lefts[d, spot], rights[d, block_of(base + spot) - first])
+                store(pl.ds(pl.multiple_of(u * unit, 16), unit), tile.astype(low))
+                return carry
+
+            lax.fori_loop(0, per_member, body, 0)
+
+        def store_spare(rows, tile):
+            spare[d, lax.rem(s, 2), rows, :] = tile
+
+        def store_own(rows, tile):
+            own[d, lax.rem(s, slots), rows, :] = tile
+
+        side(1 - core, store_spare)
+        part_copy(d, s).start()
+        side(core, store_own)
+        prefetch()
+
+    def final_of(q, d):
+        return tail_own.at[d, n - 1] if q == 2 else own.at[d, (n - 1) % slots, span(q)]
+
+    def spot_of(q, d, index, which):
+        member = gather_at(d, index) * 2 + which
+        if q == 2:
+            return t_ref.at[member, :, cols_of(d)]
+        return o_ref.at[member, span(q), cols_of(d)]
+
+    def gather_copy(q, d, index, first=False):
+        src = final_of(q, d) if first else spot_of(q, d, index, core)
+        return remote(
+            src, spot_of(q, d, index, core),
+            gather_send.at[d, q, index], gather_recv.at[d, q, index], {"wide": target[d]})
+
+    def gather_landed(q, d, index):
+        return remote(
+            final_of(q, d), spot_of(q, d, index + 1, core),
+            gather_send.at[d, q, index], gather_recv.at[d, q, index], {"wide": target[d]})
+
+    def pair_copy(q, d, index, first=False):
+        src = final_of(q, d) if first else spot_of(q, d, index, core)
+        return remote(
+            src, spot_of(q, d, index, core),
+            pair_send.at[d, q, index], pair_recv.at[d, q, index], {"wide": other})
+
+    def pair_landed(q, d, index):
+        return remote(
+            final_of(q, d), spot_of(q, d, index, 1 - core),
+            pair_send.at[d, q, index], pair_recv.at[d, q, index], {"wide": other})
+
+    def keep_copy(q, d):
+        return pltpu.make_async_copy(final_of(q, d), spot_of(q, d, 0, core), keep_sem.at[d, q])
+
+    def cross_copy(d, index, mine, first=False):
+        member = gather_at(d, index) * 2 + (core if mine else 1 - core)
+        src = final_of(2, d) if first else t_ref.at[member, :, cols_of(d)]
+        lane = 0 if mine else 1
+        return remote(
+            src, e_ref.at[member, :, cols_of(d)],
+            cross_send.at[d, lane, index], cross_recv.at[d, lane, index],
+            {"section": 1 - section})
+
+    def hand_over(q, d):
+        gather_copy(q, d, 0, True).start()
+        pair_copy(q, d, 0, True).start()
+        keep_copy(q, d).start()
+        if q == 2:
+            @pl.when(section == 0)
+            def _():
+                cross_copy(d, 0, True, True).start()
+
+    def reduce_main(q, d, s, begin=False, end=False):
+        if not begin:
+            ring_copy(q, d, s - 1).wait_recv()
+
+        def add(tile, carry):
+            at = pl.ds(pl.multiple_of(spans[q][0] + tile * 16, 16), 16)
+            slot = lax.rem(s, slots)
+            total = own[d, slot, at].astype(f32) + part[d, s, at].astype(f32)
+            if not begin:
+                total = total + ring[d, s - 1, at].astype(f32)
+            own[d, slot, at] = total.astype(low)
             return carry
 
-        lax.fori_loop(0, width // 128, turn, 0)
-
-    @pl.when(b < 12)
-    def _():
-        @pl.when(b > 1)
-        def _():
-            for u in range(per_block):
-                unit_copy(b - 2, u).wait()
-
-        def part(i, carry):
-            at = tile_of(i, 128)
-            result[lax.rem(b, 2), at, :] = dot_nn(turned[at, :], right[0]).astype(low)
-            return carry
-
-        lax.fori_loop(0, width // 128, part, 0)
-        for u in range(per_block):
-            unit_copy(b, u).start()
-
-    @pl.when(b == 12)
-    def _():
-        for block in (10, 11):
-            for u in range(per_block):
-                unit_copy(block, u).wait()
-        feat_width = feat.shape[2]
-        first = info[2].astype(f32)
-        clips = feat.shape[0]
-        blank[...] = jnp.zeros_like(blank)
+        loop(spans[q][1] // 16, add, 1)
+        if end:
+            hand_over(q, d)
+        else:
+            ring_copy(q, d, s).start()
+
+    def tail_part_copy(d, s):
+        return remote(
+            tails.at[reduce_at(d, s) * 2 + 1 - core, :, cols_of(d)], tail_part.at[d, s],
+            part_send.at[d, n + s], part_recv.at[d, n + s], {"wide": other})
+
+    def reduce_tail(d, s, begin=False, end=False):
+        tail_part_copy(d, s).wait_recv()
+        total = tails[reduce_at(d, s) * 2 + core, :, cols_of(d)].astype(f32)
+        total = total + tail_part[d, s].astype(f32)
+        if not begin:
+            ring_copy(2, d, s - 1).wait_recv()
+            total = total + tail_ring[d, s - 1].astype(f32)
+        tail_own[d, s] = total.astype(low)
+        if end:
+            hand_over(2, d)
+        else:
+            ring_copy(2, d, s).start()
+
+    feat_half = h_ref.shape[2]
+    feat_keep = pltpu.make_async_copy(
+        feat_grad.at[:, :, pl.ds(0, feat_half)], h_ref, feat_sem.at[0])
+    feat_send = remote(
+        feat_grad.at[:, :, pl.ds(feat_half, feat_half)], h_ref, feat_sem.at[1], feat_sem.at[2],
+        {"section": 1 - section})
+
+    def embed_back():
+        first = (1 - section).astype(f32)
         small[...] = jnp.zeros_like(small)
         small[0:8, :] = small_in[...]
         for i in range(up_sums.shape[1] // width):
@@ -820,58 +837,257 @@
         for c in range(clips):
             count = count + jnp.sum(cols[c][:, 1:2], axis=0, keepdims=True)
         small[15:16, :] = jnp.where(lane == 3, count, row)
-        weight_sum = [jnp.zeros((feat_width, width), f32)] * 2
-        place_sum = jnp.zeros(dx.shape[1:], f32)
-        for c in range(clips):
-            grad = dx[c]
-            kept = jnp.where(cols[c][:, 0:1] > 0.0, jnp.zeros_like(grad), grad)
-            feat_grad[c] = dot_nt(kept, chosen[c]).astype(low)
-            second = info[c].astype(f32)
-            flags = ((1.0 - second) * first, second * first)
-            wide = dot_nn(feat[c].T, kept)
-            sums = column_sum(kept.astype(f32))
-            for kind in range(2):
-                weight_sum[kind] = weight_sum[kind] + flags[kind] * wide
-                small[12 + kind : 13 + kind, :] += flags[kind] * sums
-            small[14:15, :] += first * (column_sum(grad.astype(f32)) - sums)
-            place_sum = place_sum + grad.astype(f32)
-        embed[0:feat_width, :] = weight_sum[0].astype(low)
-        embed[feat_width : 2 * feat_width, :] = weight_sum[1].astype(low)
-        embed[2 * feat_width :, :] = (place_sum * first).astype(low)
-        blank[0] = small[...].astype(low)
-        copies = []
+        embed[...] = jnp.zeros_like(embed)
+
+        @pl.when(section == 0)
+        def _():
+            weight_sum = [jnp.zeros((feat_width, width), f32)] * 2
+            place_sum = jnp.zeros((length, width), f32)
+            for c in range(clips):
+                grad = dx[c]
+                kept = jnp.where(cols[c][:, 0:1] > 0.0, jnp.zeros_like(grad), grad)
+                feat_grad[c] = dot_nt(kept, chosen[c]).astype(low)
+                second = info[c].astype(f32)
+                flags = (1.0 - second, second)
+                wide = dot_nn(feat[c].T, kept)
+                sums = column_sum(kept.astype(f32))
+                for kind in range(2):
+                    weight_sum[kind] = weight_sum[kind] + flags[kind] * wide
+                    small[12 + kind : 13 + kind, :] += flags[kind] * sums
+                small[14:15, :] += column_sum(grad.astype(f32)) - sums
+                place_sum = place_sum + grad.astype(f32)
+            embed[0:feat_width, :] = weight_sum[0].astype(low)
+            embed[feat_width : 2 * feat_width, :] = weight_sum[1].astype(low)
+            embed[2 * feat_width :, :] = place_sum.astype(low)
+            feat_keep.start()
+            feat_send.start()
+
+        embed_share = tail - SMALL
         for w in range(members):
-            copies.append(pltpu.make_async_copy(
-                embed.at[pl.ds(w * embed_share, embed_share)],
-                stack_h.at[w, pl.ds(share, embed_share)], embed_sem.at[w]))
-            copies.append(pltpu.make_async_copy(
-                blank.at[min(w, 1)],
-                stack_h.at[w, pl.ds(share + embed_share, SMALL)], small_sem.at[w]))
-        for copy in copies:
-            copy.start()
-        for copy in copies:
-            copy.wait()
-
-
-def unpack_kernel(per_block, blocks, total, attend, project, up, down):
-    b = pl.program_id(0) // per_block
-    values = total[0].astype(jnp.float32)
-
-    @pl.when(b < 3)
+            tails[w, 0:embed_share, :] = embed[w * embed_share : (w + 1) * embed_share, :]
+            if w == 0:
+                tails[w, embed_share:, :] = small[...].astype(low)
+            else:
+                tails[w, embed_share:, :] = jnp.zeros((SMALL, width), low)
+
+    embed_loads = [
+        pltpu.make_async_copy(src, dst, embed_sem.at[i])
+        for i, (src, dst) in enumerate(((dx_h, dx), (feat_h, feat), (chosen_h, chosen)))
+    ]
+
+    for d in range(2):
+        load_operands(d, 0)
+    for copy in embed_loads:
+        copy.start()
+    pl.semaphore_wait(barrier, 4)
+    for d in range(2):
+        products(d, 0, functools.partial(load_operands, d, 1))
+    for d in range(2):
+        part_copy(d, 0).wait_recv()
+        for q in range(2):
+            reduce_main(q, d, 0, begin=True)
+
+    def prefetch_after(d, s):
+        @pl.when(s < n)
+        def _():
+            load_operands(d, s)
+
+    for d in range(2):
+        products(d, 1, functools.partial(prefetch_after, d, 2))
+    for copy in embed_loads:
+        copy.wait()
+    embed_back()
+
+    def send_tails(s, carry):
+        for d in range(2):
+            tail_part_copy(d, s).start()
+        return carry
+
+    lax.fori_loop(0, n, send_tails, 0)
+
+    def scatter_step(s, carry):
+        for q in range(2):
+            for d in range(2):
+                if q == 0:
+                    part_copy(d, s).wait_recv()
+                reduce_main(q, d, s)
+
+        for d in range(2):
+            @pl.when(s > 0)
+            def _():
+                part_copy(d, s - 1).wait_send()
+
+            @pl.when(s > 1)
+            def _():
+                for q in range(2):
+                    ring_copy(q, d, s - 2).wait_send()
+
+            products(d, s + 1, functools.partial(prefetch_after, d, s + 2))
+
+        for d in range(2):
+            @pl.when(s == 1)
+            def _():
+                reduce_tail(d, 0, begin=True)
+
+            @pl.when(s > 1)
+            def _():
+                reduce_tail(d, s - 1)
+        return carry
+
+    lax.fori_loop(1, n - 1, scatter_step, 0)
+    for q in range(2):
+        for d in range(2):
+            if q == 0:
+                part_copy(d, n - 1).wait_recv()
+            reduce_main(q, d, n - 1, end=True)
+    for d in range(2):
+        reduce_tail(d, n - 2, begin=n == 2)
+
+    def gather_step(q, d, t):
+        gather_landed(q, d, t).wait_recv()
+
+        @pl.when(t < n - 2)
+        def _():
+            gather_copy(q, d, t + 1).start()
+
+        pair_copy(q, d, t + 1).start()
+        if q == 2:
+            @pl.when(section == 0)
+            def _():
+                cross_copy(d, t + 1, True).start()
+
+    def pass_pair(d, t):
+        pair_landed(2, d, t).wait_recv()
+
+        @pl.when(section == 0)
+        def _():
+            cross_copy(d, t, False).start()
+
+    for q, d in mains:
+        gather_step(q, d, 0)
+    for d in range(2):
+        reduce_tail(d, n - 1, end=True)
+
+    def spread(t, carry):
+        for q, d in mains:
+            gather_step(q, d, t)
+        for d in range(2):
+            gather_step(2, d, t - 1)
+            pass_pair(d, t - 1)
+        return carry
+
+    lax.fori_loop(1, n - 1, spread, 0)
+    for d in range(2):
+        gather_step(2, d, n - 2)
+        pass_pair(d, n - 2)
+    for d in range(2):
+        pass_pair(d, n - 1)
+
+    @pl.when(section == 0)
     def _():
-        attend[...] = values
-
-    @pl.when(b == 3)
+        feat_keep.wait()
+        feat_send.wait_send()
+
+    @pl.when(section == 1)
     def _():
-        project[...] = values
-
-    @pl.when((b > 3) & (b < 4 + blocks))
-    def _():
-        up[...] = values
-
-    @pl.when(b > 3 + blocks)
-    def _():
-        down[...] = values
+        feat_send.wait_recv()
+
+    for q, d in streams:
+        keep_copy(q, d).wait()
+    for d in range(2):
+        for s in range(max(n - 2, 0), n):
+            part_copy(d, s).wait_send()
+        for s in range(max(n - 3, 0), n - 1):
+            for q in range(2):
+                ring_copy(q, d, s).wait_send()
+
+    def finish(s, carry):
+        for d in range(2):
+            tail_part_copy(d, s).wait_send()
+            for q in range(3):
+                pair_copy(q, d, s).wait_send()
+                if q < 2:
+                    pair_landed(q, d, s).wait_recv()
+
+            @pl.when(s < n - 1)
+            def _():
+                ring_copy(2, d, s).wait_send()
+                for q in range(3):
+                    gather_copy(q, d, s).wait_send()
+
+            for mine in (True, False):
+                @pl.when(section == 0)
+                def _():
+                    cross_copy(d, s, mine).wait_send()
+
+                @pl.when(section == 1)
+                def _():
+                    cross_copy(d, s, mine).wait_recv()
+        return carry
+
+    lax.fori_loop(0, n, finish, 0)
+
+
+def unpack_kernel(
+    blocks, total, attend, project, up, down, coming, going, in_sem, out_sem
+):
+    members, share, width = total.shape
+    slots, unit = coming.shape[:2]
+    per_block, per_member = width // unit, share // unit
+    count = members * per_member
+
+    def in_copy(u):
+        slot = lax.rem(u, slots)
+        row = pl.multiple_of(lax.rem(u, per_member) * unit, 16)
+        return pltpu.make_async_copy(
+            total.at[u // per_member, pl.ds(row, unit)], coming.at[slot], in_sem.at[slot])
+
+    def out_copy(u, dst, row, column):
+        slot = lax.rem(u, slots)
+        return pltpu.make_async_copy(
+            going.at[slot],
+            dst.at[pl.ds(pl.multiple_of(row, 16), unit), pl.ds(pl.multiple_of(column, 128), width)],
+            out_sem.at[slot])
+
+    for u in range(slots):
+        in_copy(u).start()
+
+    def step(u, carry):
+        slot = lax.rem(u, slots)
+        in_copy(u).wait()
+
+        @pl.when(u >= slots)
+        def _():
+            out_copy(u, project, 0, 0).wait()
+
+        going[slot] = coming[slot].astype(jnp.float32)
+        block, row = u // per_block, lax.rem(u, per_block) * unit
+
+        @pl.when(block < 3)
+        def _():
+            out_copy(u, attend, row, block * width).start()
+
+        @pl.when(block == 3)
+        def _():
+            out_copy(u, project, row, 0).start()
+
+        @pl.when((block > 3) & (block < 4 + blocks))
+        def _():
+            out_copy(u, up, row, (block - 4) * width).start()
+
+        @pl.when(block > 3 + blocks)
+        def _():
+            out_copy(u, down, (u - (4 + blocks) * per_block) * unit, 0).start()
+
+        @pl.when(u + slots < count)
+        def _():
+            in_copy(u + slots).start()
+
+        return carry
+
+    lax.fori_loop(0, count, step, 0)
+    for u in range(count - slots, count):
+        out_copy(u, project, 0, 0).wait()
 
 
 ANY = pl.BlockSpec(memory_space=pl.ANY)
@@ -924,7 +1140,7 @@
       gains, vectors, up_bias)
 
 
-def run_backward(cotangent, weights, x, qkv, probs, middle, slope, gains):
+def run_backward(cotangent, weights, x, qkv, probs, middle, slope, left, gains):
     clips, length, width = cotangent.shape
     feed = weights[2].shape[1]
     blocks = feed // width
@@ -935,11 +1151,12 @@
         out_shape=(
             shaped(LOW, 5 + blocks, clips * length, width),
             shaped(LOW, clips, length, width),
+            shaped(LOW, left.shape[0], width, clips * length),
             shaped(WIDE, 8, width),
             shaped(WIDE, 1, feed),
         ),
-        in_specs=[ANY] * 10 + [VMEM],
-        out_specs=(ANY, ANY, VMEM, VMEM),
+        in_specs=[ANY] * 11 + [VMEM],
+        out_specs=(ANY, ANY, ANY, VMEM, VMEM),
         scratch_shapes=[
             vm((width, 3 * width), LOW), vm((width, width), LOW), vm((width, feed), LOW),
             vm((feed, width), LOW),
@@ -949,119 +1166,75 @@
             vm((length, feed), LOW), vm((length, width), WIDE), vm((length, width), WIDE),
             vm((length, width), LOW), vm((length, width), LOW), vm((length, 3 * width), LOW),
             vm((clips, length, width), LOW),
-            dma((4,)), dma((clips, 5)), dma((3,)), dma((5 + blocks,)), dma((clips,)),
+            vm((clips * length, width), LOW), vm((width, clips * length), LOW),
+            dma((2,)), dma((4,)), dma((clips, 5)), dma((3,)), dma((5 + blocks,)), dma((clips,)),
             dma((clips, 2)), dma((clips, 2)),
         ],
         compiler_params=pltpu.CompilerParams(
             collective_id=2, has_side_effects=True, vmem_limit_bytes=60 * 2**20
         ),
-    )(cotangent, *weights, x, qkv, probs, middle, slope, gains)
-
-
-def run_grads(members, info, left, right, dx, features, chosen, cols, small, up_sums, stats):
-    rows, width = left.shape[1:]
+    )(cotangent, *weights, x, qkv, probs, middle, slope, left, gains)
+
+
+def run_sums(members, info, turned, right, dx, features, chosen, cols, small, up_sums, stats):
+    width, rows = turned.shape[1:]
     clips, length, feat_width = features.shape
+    n = members // 2
+    share = 12 * width // members
     embed_rows = 2 * feat_width + length
-    total_rows = 12 * width
-    share, embed_share = total_rows // members, embed_rows // members
-    per_block = width // unit_rows(members, width, total_rows)
+    tail = embed_rows // members + SMALL
+    unit = unit_rows(members, width)
+    per_member = share // unit
+    half = width // 2
     dma = pltpu.SemaphoreType.DMA
-
-    def whole(array):
-        zeros = (0,) * array.ndim
-        return pl.BlockSpec(array.shape, lambda b: zeros)
-
-    def left_at(b):
-        return (jnp.where(b < 3, 0, jnp.where(b == 3, 1, jnp.where(b < 8, 2, jnp.minimum(b, 11) - 5))), 0, 0)
-
-    def right_at(b):
-        return (jnp.minimum(b, 8), 0, 0)
-
+    vm = pltpu.VMEM
+    sems = [dma((2, 2 * per_member + 2)), dma((3,)), dma((2, 2 * n)), dma((2, 2 * n))]
+    sems += [dma((2, 3, n)) for _ in range(6)]
+    sems += [dma((2, 3)), dma((2, 2, n)), dma((2, 2, n)), dma((3,))]
     return pl.pallas_call(
-        functools.partial(grads_kernel, members),
-        grid=(13,),
+        functools.partial(sums_kernel, members),
         out_shape=(
-            shaped(LOW, members, share + embed_share + SMALL, width),
-            shaped(LOW, clips, length, feat_width),
-        ),
-        in_specs=[
-            SMEM,
-            pl.BlockSpec((1, rows, width), left_at),
-            pl.BlockSpec((1, rows, width), right_at),
-            whole(dx), whole(features), whole(chosen), whole(cols), whole(small), whole(up_sums),
-            whole(stats),
-        ],
-        out_specs=(ANY, pl.BlockSpec((clips, length, feat_width), lambda b: (0, 0, 0))),
-        scratch_shapes=[
-            pltpu.VMEM((width, rows), LOW),
-            pltpu.VMEM((2, width, width), LOW),
-            pltpu.VMEM((embed_rows, width), LOW),
-            pltpu.VMEM((SMALL, width), WIDE),
-            pltpu.VMEM((2, SMALL, width), LOW),
-            dma((2, per_block)), dma((members,)), dma((members,)),
-        ],
-        compiler_params=pltpu.CompilerParams(vmem_limit_bytes=56 * 2**20),
-    )(info, left, right, dx, features, chosen, cols, small, up_sums, stats)
-
-
-def ring_sum(stacked, tail, feature_grad):
-    members, rows, width = stacked.shape
-    clips, length, feat_width = feature_grad.shape
-    n = members // 2
-    dma = pltpu.SemaphoreType.DMA
-    half = width // 2
-    sems = [dma((2, 2, n)) for _ in range(9)]
-    sems += [dma((2, 2)), dma((2, 2, n)), dma((2, 2, n)), dma((3,))]
-    return pl.pallas_call(
-        functools.partial(ring_kernel, n, rows, tail),
-        out_shape=(
-            shaped(LOW, members, rows, width),
+            shaped(LOW, members, share, width),
+            shaped(LOW, members, tail, width),
             shaped(LOW, members, tail, width),
             shaped(LOW, clips, length, feat_width // 2),
         ),
-        in_specs=[ANY, ANY],
-        out_specs=(ANY, ANY, ANY),
+        in_specs=[SMEM] + [ANY] * 5 + [VMEM] * 4,
+        out_specs=(ANY,) * 4,
         scratch_shapes=[
-            pltpu.VMEM((2, n, rows, half), LOW),
-            pltpu.VMEM((2, n, rows, half), LOW),
-            pltpu.VMEM((2, n - 1, rows, half), LOW),
+            vm((2, 2 * per_member, unit, rows), LOW), vm((2, 2, rows, half), LOW),
+            vm((2, 3, share, half), LOW), vm((2, 2, share, half), LOW),
+            vm((2, n, share, half), LOW), vm((2, n - 1, share, half), LOW),
+            vm((members, tail, width), LOW), vm((2, n, tail, half), LOW),
+            vm((2, n, tail, half), LOW), vm((2, n - 1, tail, half), LOW),
+            vm((clips, length, width), LOW), vm(features.shape, LOW), vm(chosen.shape, LOW),
+            vm(features.shape, LOW), vm((embed_rows, width), LOW), vm((SMALL, width), WIDE),
             sems,
         ],
         compiler_params=pltpu.CompilerParams(
-            collective_id=0, has_side_effects=True, vmem_limit_bytes=48 * 2**20
+            collective_id=0, has_side_effects=True, vmem_limit_bytes=60 * 2**20
         ),
-    )(stacked, feature_grad)
+    )(info, turned, right, dx, features, chosen, cols, small, up_sums, stats)
 
 
 def run_unpack(total, blocks):
-    members, rows, width = total.shape
-    unit = unit_rows(members, width, 12 * width)
-    per_block, per_member = width // unit, 12 * width // members // unit
-
-    def within(first, count):
-        def at(u):
-            return jnp.clip(u - first * per_block, 0, count * per_block - 1)
-        return at
-
-    attend, project, up, down = within(0, 3), within(3, 1), within(4, blocks), within(4 + blocks, blocks)
-
-    def across(at):
-        return lambda u: (at(u) % per_block, at(u) // per_block)
-
+    members, share, width = total.shape
+    unit = unit_rows(members, width)
+    slots = 6
+    dma = pltpu.SemaphoreType.DMA
     return pl.pallas_call(
-        functools.partial(unpack_kernel, per_block, blocks),
-        grid=(12 * per_block,),
+        functools.partial(unpack_kernel, blocks),
         out_shape=(
             shaped(WIDE, width, 3 * width), shaped(WIDE, width, width),
             shaped(WIDE, width, blocks * width), shaped(WIDE, blocks * width, width),
         ),
-        in_specs=[pl.BlockSpec((1, unit, width), lambda u: (u // per_member, u % per_member, 0))],
-        out_specs=(
-            pl.BlockSpec((unit, width), across(attend)),
-            pl.BlockSpec((unit, width), lambda u: (project(u), 0)),
-            pl.BlockSpec((unit, width), across(up)),
-            pl.BlockSpec((unit, width), lambda u: (down(u), 0)),
-        ),
+        in_specs=[ANY],
+        out_specs=(ANY,) * 4,
+        scratch_shapes=[
+            pltpu.VMEM((slots, unit, width), LOW), pltpu.VMEM((slots, unit, width), WIDE),
+            dma((slots,)), dma((slots,)),
+        ],
+        compiler_params=pltpu.CompilerParams(vmem_limit_bytes=32 * 2**20),
     )(total)
 
 
@@ -1100,18 +1273,15 @@
     left, x, qkv, probs, middle, slope, output, stats = run_forward(
         features, chosen, pos_embed, weights, cols, kind_offset, embed_vectors[2:3], bias_row,
         live_row, norm_gains[0], rows, up_bias)
-    right, dx, small, up_sums = run_backward(
-        cotangent, weights, x, qkv, probs, middle, slope, norm_gains[0])
-    info = jnp.concatenate([kinds, is_first.astype(jnp.int32)[None]])
-    stacked, feature_grad = run_grads(
-        members, info, left, right, dx, features, chosen, cols, small, up_sums, stats)
+    right, dx, turned, small, up_sums = run_backward(
+        cotangent, weights, x, qkv, probs, middle, slope, left, norm_gains[0])
+    total, tails, cross, feature_out = run_sums(
+        members, kinds, turned, right, dx, features, chosen, cols, small, up_sums, stats)
+    attend_total, project_total, up_total, down_total = run_unpack(total, blocks)
     embed_share = (2 * feat_width + length) // members
-    tail = embed_share + SMALL
-    total, cross, feature_out = ring_sum(stacked, tail, feature_grad)
-    attend_total, project_total, up_total, down_total = run_unpack(total, blocks)
-    ends = jnp.where(is_first, total[:, -tail:], cross)
+    ends = jnp.where(is_first, tails, cross)
     embed_total = ends[:, :embed_share].reshape(-1, width).astype(WIDE)
-    small_total = total[0, -SMALL:].astype(WIDE)
+    small_total = tails[0, -SMALL:].astype(WIDE)
     stat_row = small_total[15]
     rms_out = jnp.sqrt(stat_row[0:3] / (stat_row[3] * width))[None]
     return (

time: 493 us -> 397 us (0.81)
  Pallas kernels: 471 us -> 373 us
    pallas_call x3 -> x2, Pallas kernels: 244 us -> 187 us  [the longest x1 177 us: run_sums(): pl.pallas_call(functools.partial(sums_kernel, members), out_shape=(shaped...]
    pallas_call x1, Pallas kernels: 111 us -> 89.6 us  [run_backward(): pl.pallas_call(backward_kernel, out_shape=(shaped(LOW, 5 + blocks, clips...]
    pallas_call x1, Pallas kernels: 116 us -> 95.7 us  [run_forward(): pl.pallas_call(forward_kernel, out_shape=(shaped(LOW, 3 + blocks, clips *...]
where the time goes in v3:
time: 397 us; the launch traced here: 395 us
  Pallas kernels  373 us (94%)
  local copies, waits for them, and re-layouts  15.4 us (4%)
  other arithmetic  5.92 us (1%)
    pallas_call x1, Pallas kernels, run_sums(): pl.pallas_call(functools.partial(sums_kernel, members), out_shape=(shaped...  177 us
    pallas_call x1, Pallas kernels, run_forward(): pl.pallas_call(forward_kernel, out_shape=(shaped(LOW, 3 + blocks, clips *...  95.7 us
    pallas_call x1, Pallas kernels, run_backward(): pl.pallas_call(backward_kernel, out_shape=(shaped(LOW, 5 + blocks, clips...  89.6 us
    pallas_call x1, Pallas kernels, run_unpack(): pl.pallas_call(functools.partial(unpack_kernel, blocks), out_shape=(shape...  9.79 us
    unnamed x20, local copies, waits for them, and re-layouts  8.48 us

profile of v3, /device:TPU:0, one launch (start us, length us, event | category | flops | bytes accessed | tf_op | source)
XLA Modules:
  0.0 395.4 jit_solution(6715239585563129758)
XLA Ops:
  0.6 0.0 copy-start.6
  0.7 0.0 copy-start.5
  0.7 0.0 copy-start.4
  0.7 1.4 slice_reduce_fusion.3
  2.1 0.7 broadcast_compare_fusion
  2.7 0.7 broadcast_select_fusion.2.kind_offset
  3.4 1.2 slice_bitcast_fusion.1
  4.6 1.0 broadcast_select_fusion.1.chosen_h
  5.6 0.0 copy-done.6
  5.6 0.0 copy-done.5
  5.6 1.1 select_convert_fusion.cols
  6.8 0.0 copy-done.4
  6.8 0.6 broadcast_in_dim.109.bias_row
  7.4 0.6 copy.32
  8.0 0.6 broadcast_in_dim.112.live_row
  8.6 95.7 %shard_map.246 = (bf16[7,1024,768]{2,1,0:T(8,128)(2,1)}, f32[2,512,768]{2,1,0:T(8,128)}, bf16[2,512,2304]{2,1,0:T(8,128)(2,1)}, bf16[2,12,512,512]{3,2,1,0:T(8,1...) custom-call(bf16[2,512,256]{2,1,0:T(8,128)(2,1)} %feat_h.3, ...), custom_call_target="tpu_custom_call" | custom-call | tf_op jit(solution)/shard_map/pallas_call | solution.py:1111
  104.3 89.6 %shard_map.247 = (bf16[9,1024,768]{2,1,0:T(8,128)(2,1)}, bf16[2,512,768]{2,1,0:T(8,128)(2,1)}, bf16[7,768,1024]{2,1,0:T(8,128)(2,1)}, f32[8,768]{1,0:T(8,128)}, f32[1,3072]{1,0:T(1,128)}) custom-call(bf16[2,512,768]{2,1,0:T(8,128)(2,1)} %cot_h.1, bf16[768,2304]{1,0:T(8,128)(2,1)} %bitcast.34, bf16[768,768]{1,0:T(8,128)(2,1)} %bitcast.36, ...), custom_call_target="tpu_custom_call" | custom-call | tf_op jit(solution)/shard_map/pallas_call | solution.py:1149
  194.0 177.4 %shard_map.248 = (bf16[16,576,768]{2,1,0:T(8,128)(2,1)}, bf16[16,80,768]{2,1,0:T(8,128)(2,1)}, bf16[16,80,768]{2,1,0:T(8,128)(2,1)}, bf16[2,512,128]{2,1,0:T(8,128)(2,1)}) custom-call(s32[2]{0:T(128)} %info.1, bf16[7,768,1024]{2,1,0:T(8,128)(2,1)} %get-tuple-element.41.turned_h, bf16[9,1024,768]{2,1,0:T(8,128)(2,1)} %get-tuple-element.42.right_h, ...), custom_call_target="tpu_custom_call" | custom-call | tf_op jit(solution)/shard_map/pallas_call | solution.py:1194
  371.4 0.7 fusion
  372.2 0.6 slice.97
  373.4 0.5 fusion.2
  373.9 0.0 copy-start
  373.9 5.0 %copy-done = bf16[16,576,768]{2,1,0:T(8,128)(2,1)S(1)} copy-done((bf16[16,576,768]{2,1,0:T(8,128)(2,1)S(1)}, bf16[16,576,768]{2,1,0:T(8,128)(2,1)}, u32[]{:S(2)}) %copy-start) | copy-done | bytes 14155800
  378.9 0.0 copy-start.1
  379.0 9.8 %shard_map.249 = (f32[768,2304]{1,0:T(8,128)}, f32[768,768]{1,0:T(8,128)}, f32[768,3072]{1,0:T(8,128)}, f32[3072,768]{1,0:T(8,128)}) custom-call(bf16[16,576,768]{2,1,0:T(8,128)(2,1)S(1)} %copy-done), custom_call_target="tpu_custom_call" | custom-call | tf_op jit(solution)/shard_map/pallas_call | solution.py:1225
  388.8 0.0 copy-done.1
  388.8 0.2 broadcast_select_fusion
  389.0 0.3 slice_convert_fusion
  389.3 0.0 copy-start.2
  389.3 0.0 copy-start.3
  389.3 2.0 fusion.3
  391.3 0.6 fusion.1
  391.9 0.6 copy.28
  392.6 0.6 copy.30
  393.2 0.6 slice.93
  393.8 0.0 copy-done.2
  393.8 0.9 copy.35
  394.7 0.0 copy-done.3
  394.7 0.7 copy.36
  (7 shorter events, 0.0 us)
Async XLA Ops:
  0.6 5.0 %copy-start.6 = (s32[2,512]{1,0:T(2,128)S(1)}, s32[2,512]{1,0:T(2,128)}, u32[]{:S(2)}) copy-start(s32[2,512]{1,0:T(2,128)} %param.16) | copy-start | bytes 12292
  0.7 5.0 %copy-start.5 = (s32[2,512]{1,0:T(2,128)S(1)}, s32[2,512]{1,0:T(2,128)}, u32[]{:S(2)}) copy-start(s32[2,512]{1,0:T(2,128)} %param.17) | copy-start | bytes 12292
  0.7 6.1 %copy-start.4 = (f32[1,6,768]{2,0,1:T(1,128)S(1)}, f32[1,6,768]{2,0,1:T(1,128)}, u32[]{:S(2)}) copy-start(f32[1,6,768]{2,0,1:T(1,128)} %param.23) | copy-start | bytes 55300
  373.9 5.0 %copy-start = (bf16[16,576,768]{2,1,0:T(8,128)(2,1)S(1)}, bf16[16,576,768]{2,1,0:T(8,128)(2,1)}, u32[]{:S(2)}) copy-start(bf16[16,576,768]{2,1,0:T(8,128)(2,1)} %get-tuple-element.50.total) | copy-start | bytes 42467332
  378.9 9.8 %copy-start.1 = (bf16[16,80,768]{2,1,0:T(8,128)(2,1)S(1)}, bf16[16,80,768]{2,1,0:T(8,128)(2,1)}, u32[]{:S(2)}) copy-start(bf16[16,80,768]{2,1,0:T(8,128)(2,1)} %get-tuple-element.48) | copy-start | bytes 5898244
  389.3 4.5 %copy-start.2 = (bf16[2,512,384]{2,1,0:T(8,128)(2,1)S(1)}, bf16[2,512,384]{2,1,0:T(8,128)(2,1)}, u32[]{:S(2)}) copy-start(bf16[2,512,384]{2,1,0:T(8,128)(2,1)} %get-tuple-element.94) | copy-start | bytes 2359300
  389.3 5.3 %copy-start.3 = (bf16[2,512,128]{2,1,0:T(8,128)(2,1)S(1)}, bf16[2,512,128]{2,1,0:T(8,128)(2,1)}, u32[]{:S(2)}) copy-start(bf16[2,512,128]{2,1,0:T(8,128)(2,1)} %get-tuple-element.95) | copy-start | bytes 786436

commit v4 on v3

--- a/solution.py
+++ b/solution.py
@@ -33,10 +33,17 @@
 
 
 def tile_of(index, size):
+    if isinstance(index, int):
+        return pl.ds(index * size, size)
     return pl.ds(pl.multiple_of(index * size, size), size)
 
 
 def loop(count, body, unroll):
+    if count == unroll:
+        for i in range(count):
+            body(i, 0)
+        return
+
     def step(i, carry):
         for u in range(unroll):
             body(i * unroll + u, 0)
@@ -51,6 +58,11 @@
 
 def row_mean(values):
     return jnp.mean(values, axis=-1, keepdims=True)
+
+
+def pick_kind(kind, first, second):
+    keep = (kind == 0).astype(jnp.float32)
+    return first.astype(jnp.float32) * keep + second.astype(jnp.float32) * (1.0 - keep)
 
 
 def gelu_pair(hidden):
@@ -86,10 +98,11 @@
 
 
 def forward_kernel(
-    feat_h, chosen_h, pos_h, wqkv_h, wout_h, wup_h, wdown_h,
-    cols, kind_offset, mask_row, bias_row, live_row, gains, vectors, up_bias,
-    left_h, x_h, qkv_h, probs_h, middle_h, slope_h, out_h, stats,
-    feat, chosen, pos, wqkv, wout, wup, wdown,
+    kinds, feat_h, masked_h, valid_h, embw_h, embv_h, pos_h, gains_h, vectors_h, wqkv_h, wout_h,
+    wup_h, upb_h, wdown_h,
+    left_h, x_h, qkv_h, probs_h, middle_h, slope_h, out_h, cols, stats,
+    feat, masked, valid, embw, embv, pos, gains, vectors, wqkv, wout, wup, up_bias, wdown,
+    chosen, live_row,
     x, normed, qkv, probs, context, middle, hidden_in, active, slope, y, landed,
     load_sem, save_sem, probs_sem, send_sem, recv_sem, back_send, back_recv, keep_sem,
 ):
@@ -100,11 +113,22 @@
     feed = wup.shape[1]
     heads2 = width // 128
     blocks = feed // width
+    loads = fetch(
+        [(masked_h, masked), (valid_h, valid), (gains_h.at[0], gains),
+         (vectors_h.at[0], vectors), (upb_h, up_bias),
+         (feat_h, feat), (embw_h, embw), (embv_h, embv), (pos_h, pos),
+         (wqkv_h.at[0], wqkv), (wout_h.at[0], wout), (wup_h.at[0], wup), (wdown_h.at[0], wdown)],
+        load_sem)
     greet_partner()
-    loads = fetch(
-        [(feat_h, feat), (chosen_h, chosen), (pos_h, pos), (wqkv_h, wqkv), (wout_h, wout),
-         (wup_h, wup), (wdown_h, wdown)], load_sem)
     stats[...] = jnp.zeros_like(stats)
+    for copy in loads[:9]:
+        copy.wait()
+    sublane = lax.broadcasted_iota(jnp.int32, (128, length), 0)
+    for c in range(clips):
+        flags = jnp.where(sublane == 0, masked[c : c + 1, :], 0)
+        flags = jnp.where(sublane == 1, valid[c : c + 1, :], flags)
+        cols[c] = flags.astype(jnp.float32).T
+        live_row[c] = jnp.where(valid[c : c + 1, :] > 0, 0.0, NEG)
     low_lanes = lax.broadcasted_iota(jnp.int32, (1, 128), 1) < HD
 
     def save(index, src, dst):
@@ -153,27 +177,20 @@
 
         @pl.when(section == 0)
         def _():
-            @pl.when(c == 0)
-            def _():
-                for copy in loads[:3]:
-                    copy.wait()
+            chosen[...] = pick_kind(kinds[c], embw[0], embw[1]).astype(low)
+            offset = pick_kind(kinds[c], embv[0:1, :], embv[1:2, :])
 
             def tile(i, carry):
                 rows = tile_of(i, 128)
-                lifted = dot_nn(feat[c, rows, :], chosen[c]) + kind_offset[c]
+                lifted = dot_nn(feat[c, rows, :], chosen[...]) + offset
                 hidden = cols[c, rows, :][:, 0:1]
-                x[rows, :] = jnp.where(hidden > 0.0, mask_row[...], lifted) + pos[rows, :]
+                x[rows, :] = jnp.where(hidden > 0.0, embv[2:3, :], lifted) + pos[rows, :]
                 return carry
 
             loop(length // 128, tile, 4)
 
         @pl.when(section == 1)
         def _():
-            @pl.when(c == 0)
-            def _():
-                for copy in loads[:3]:
-                    copy.wait()
-
             for h in range(2):
                 send_half(c, h).wait_recv()
 
@@ -206,11 +223,16 @@
 
         @pl.when(c == 0)
         def _():
-            loads[3].wait()
+            loads[9].wait()
 
         def qkv_tile(j, carry):
             at = tile_of(j, 256)
-            qkv[:, at] = (dot_nn(normed[...], wqkv[:, at]) + bias_row[:, at]).astype(low)
+            part = dot_nn(normed[...], wqkv[:, at])
+            if j < width // 256:
+                part = part + vectors[1:2, at]
+            elif j >= 2 * width // 256:
+                part = part + vectors[2:3, tile_of(j - 2 * width // 256, 256)]
+            qkv[:, at] = part.astype(low)
             return carry
 
         loop(3 * width // 256, qkv_tile, 9)
@@ -246,7 +268,7 @@
 
         @pl.when(c == 0)
         def _():
-            loads[4].wait()
+            loads[10].wait()
 
         live = cols[c][:, 1:2]
 
@@ -264,8 +286,8 @@
 
         @pl.when(c == 0)
         def _():
-            loads[5].wait()
-            loads[6].wait()
+            loads[11].wait()
+            loads[12].wait()
 
         for h in range(2):
             rows = pl.ds(h * half, half)
@@ -327,9 +349,9 @@
 
 
 def backward_kernel(
-    cot_h, wqkv_h, wout_h, wup_h, wdown_h, x_h, qkv_h, probs_h, middle_h, slope_h, left_h, gains,
+    cot_h, wqkv_h, wout_h, wup_h, wdown_h, x_h, qkv_h, probs_h, middle_h, slope_h, left_h, gains_h,
     right_h, dx_h, turned_h, small, up_sums,
-    wqkv, wout, wup, wdown, x, qkv, probs, middle, slope, g,
+    wqkv, wout, wup, wdown, gains, x, qkv, probs, middle, slope, g,
     d_hidden, wide_grad, d_middle, d_branch, d_context, d_qkv, d_low, upright, turned,
     turn_sem, load_sem, state_sem, probs_sem, save_sem, dx_sem, send_sem, recv_sem,
 ):
@@ -357,7 +379,9 @@
     def _():
         cot_load(0).start()
 
-    loads = fetch([(wdown_h, wdown), (wup_h, wup), (wout_h, wout), (wqkv_h, wqkv)], load_sem)
+    loads = fetch(
+        [(gains_h.at[0], gains), (wdown_h.at[0], wdown), (wup_h.at[0], wup), (wout_h.at[0], wout),
+         (wqkv_h.at[0], wqkv)], load_sem)
     for c in range(clips):
         for copy in state_loads(c):
             copy.start()
@@ -454,8 +478,8 @@
 
         @pl.when(c == 0)
         def _():
-            loads[0].wait()
-            loads[1].wait()
+            for copy in loads[:3]:
+                copy.wait()
 
         state[0].wait()
         state[1].wait()
@@ -506,7 +530,7 @@
 
         @pl.when(c == 0)
         def _():
-            loads[2].wait()
+            loads[3].wait()
 
         def context_tile(j, carry):
             at = tile_of(j, 256)
@@ -559,7 +583,7 @@
 
         @pl.when(c == 0)
         def _():
-            loads[3].wait()
+            loads[4].wait()
 
         state[3].wait()
         for h in range(2):
@@ -604,22 +628,22 @@
 
 
 def sums_kernel(
-    members, info, turned_h, right_h, dx_h, feat_h, chosen_h, cols, small_in, up_sums, stats,
+    members, kinds, turned_h, right_h, dx_h, feat_h, embw_h, cols, small_in, up_sums, stats,
     o_ref, t_ref, e_ref, h_ref,
-    lefts, rights, own, spare, part, ring, tails, tail_own, tail_part, tail_ring,
-    dx, feat, chosen, feat_grad, embed, small, sems,
+    lefts, rights, chunk, part, ring, tails, tail_own, tail_part, tail_ring,
+    dx, feat, embw, feat_grad, embed, small, sems,
 ):
     (load_sem, embed_sem, part_send, part_recv, ring_send, ring_recv, gather_send, gather_recv,
      pair_send, pair_recv, keep_sem, cross_send, cross_recv, feat_sem) = sems
     low = jnp.bfloat16
     f32 = jnp.float32
     n = members // 2
-    share, columns = own.shape[2:]
+    share, columns = chunk.shape[3:]
     width = 2 * columns
     tail = tails.shape[1]
     unit = unit_rows(members, width)
     per_block, per_member = width // unit, share // unit
-    slots = own.shape[1]
+    slots = chunk.shape[1]
     clips, length, feat_width = feat.shape
     me = lax.axis_index("wide")
     section = lax.axis_index("section")
@@ -637,12 +661,15 @@
     barrier = pltpu.get_barrier_semaphore()
     for peer in (right, left, other):
         pl.semaphore_signal(barrier, inc=1, device_id={"wide": peer}, device_id_type=MESH)
-    pl.semaphore_signal(barrier, inc=1, device_id={"section": 1 - section}, device_id_type=MESH)
-
-    half = -(-share // 32) * 16
-    spans = ((0, half), (half, share - half))
-    mains = [(q, d) for q in range(2) for d in range(2)]
-    streams = mains + [(2, 0), (2, 1)]
+    @pl.when(section == 1)
+    def _():
+        pl.semaphore_signal(barrier, inc=1, device_id={"section": 0}, device_id_type=MESH)
+
+    pieces = ring_send.shape[1] - 1
+    piece = -(-share // (16 * pieces)) * 16
+    spans = [(q * piece, min(piece, share - q * piece)) for q in range(pieces)]
+    mains = [(q, d) for q in range(pieces) for d in range(2)]
+    streams = mains + [(pieces, 0), (pieces, 1)]
 
     def turn(position):
         return lax.rem(position + 2 * n, n)
@@ -690,14 +717,14 @@
 
     def part_copy(d, s):
         return remote(
-            spare.at[d, lax.rem(s, 2)], part.at[d, s], part_send.at[d, s], part_recv.at[d, s],
+            chunk.at[d, lax.rem(s, slots), 1 - core], part.at[d, s], part_send.at[d, s], part_recv.at[d, s],
             {"wide": other})
 
     def ring_copy(q, d, s):
-        if q == 2:
+        if q == pieces:
             src, dst = tail_own.at[d, s], tail_ring.at[d, s]
         else:
-            src, dst = own.at[d, lax.rem(s, slots), span(q)], ring.at[d, s, span(q)]
+            src, dst = chunk.at[d, lax.rem(s, slots), core, span(q)], ring.at[d, s, span(q)]
         return remote(src, dst, ring_send.at[d, q, s], ring_recv.at[d, q, s],
                       {"wide": target[d]})
 
@@ -707,32 +734,22 @@
         base = reduce_at(d, s) * 2 * per_member
         first = block_of(base)
 
-        def side(which, store):
-            def body(u, carry):
-                spot = which * per_member + u
-                tile = dot_nn(lefts[d, spot], rights[d, block_of(base + spot) - first])
-                store(pl.ds(pl.multiple_of(u * unit, 16), unit), tile.astype(low))
-                return carry
-
-            lax.fori_loop(0, per_member, body, 0)
-
-        def store_spare(rows, tile):
-            spare[d, lax.rem(s, 2), rows, :] = tile
-
-        def store_own(rows, tile):
-            own[d, lax.rem(s, slots), rows, :] = tile
-
-        side(1 - core, store_spare)
+        for u in range(0, 2 * per_member, 2):
+            rows = lefts[d, u : u + 2].reshape(2 * unit, lefts.shape[3])
+            tile = dot_nn(rows, rights[d, block_of(base + u) - first]).astype(low)
+            for i in range(2):
+                which, row = (u + i) // per_member, (u + i) % per_member * unit
+                chunk[d, lax.rem(s, slots), which, pl.ds(row, unit), :] = (
+                    tile[i * unit : (i + 1) * unit])
         part_copy(d, s).start()
-        side(core, store_own)
         prefetch()
 
     def final_of(q, d):
-        return tail_own.at[d, n - 1] if q == 2 else own.at[d, (n - 1) % slots, span(q)]
+        return tail_own.at[d, n - 1] if q == pieces else chunk.at[d, (n - 1) % slots, core, span(q)]
 
     def spot_of(q, d, index, which):
         member = gather_at(d, index) * 2 + which
-        if q == 2:
+        if q == pieces:
             return t_ref.at[member, :, cols_of(d)]
         return o_ref.at[member, span(q), cols_of(d)]
 
@@ -763,7 +780,7 @@
 
     def cross_copy(d, index, mine, first=False):
         member = gather_at(d, index) * 2 + (core if mine else 1 - core)
-        src = final_of(2, d) if first else t_ref.at[member, :, cols_of(d)]
+        src = final_of(pieces, d) if first else t_ref.at[member, :, cols_of(d)]
         lane = 0 if mine else 1
         return remote(
             src, e_ref.at[member, :, cols_of(d)],
@@ -774,7 +791,7 @@
         gather_copy(q, d, 0, True).start()
         pair_copy(q, d, 0, True).start()
         keep_copy(q, d).start()
-        if q == 2:
+        if q == pieces:
             @pl.when(section == 0)
             def _():
                 cross_copy(d, 0, True, True).start()
@@ -786,10 +803,10 @@
         def add(tile, carry):
             at = pl.ds(pl.multiple_of(spans[q][0] + tile * 16, 16), 16)
             slot = lax.rem(s, slots)
-            total = own[d, slot, at].astype(f32) + part[d, s, at].astype(f32)
+            total = chunk[d, slot, core, at].astype(f32) + part[d, s, at].astype(f32)
             if not begin:
                 total = total + ring[d, s - 1, at].astype(f32)
-            own[d, slot, at] = total.astype(low)
+            chunk[d, slot, core, at] = total.astype(low)
             return carry
 
         loop(spans[q][1] // 16, add, 1)
@@ -808,13 +825,13 @@
         total = tails[reduce_at(d, s) * 2 + core, :, cols_of(d)].astype(f32)
         total = total + tail_part[d, s].astype(f32)
         if not begin:
-            ring_copy(2, d, s - 1).wait_recv()
+            ring_copy(pieces, d, s - 1).wait_recv()
             total = total + tail_ring[d, s - 1].astype(f32)
         tail_own[d, s] = total.astype(low)
         if end:
-            hand_over(2, d)
+            hand_over(pieces, d)
         else:
-            ring_copy(2, d, s).start()
+            ring_copy(pieces, d, s).start()
 
     feat_half = h_ref.shape[2]
     feat_keep = pltpu.make_async_copy(
@@ -846,8 +863,9 @@
             for c in range(clips):
                 grad = dx[c]
                 kept = jnp.where(cols[c][:, 0:1] > 0.0, jnp.zeros_like(grad), grad)
-                feat_grad[c] = dot_nt(kept, chosen[c]).astype(low)
-                second = info[c].astype(f32)
+                chosen = pick_kind(kinds[c], embw[0], embw[1]).astype(low)
+                feat_grad[c] = dot_nt(kept, chosen).astype(low)
+                second = kinds[c].astype(f32)
                 flags = (1.0 - second, second)
                 wide = dot_nn(feat[c].T, kept)
                 sums = column_sum(kept.astype(f32))
@@ -872,19 +890,19 @@
 
     embed_loads = [
         pltpu.make_async_copy(src, dst, embed_sem.at[i])
-        for i, (src, dst) in enumerate(((dx_h, dx), (feat_h, feat), (chosen_h, chosen)))
+        for i, (src, dst) in enumerate(((dx_h, dx), (feat_h, feat), (embw_h, embw)))
     ]
 
     for d in range(2):
         load_operands(d, 0)
     for copy in embed_loads:
         copy.start()
-    pl.semaphore_wait(barrier, 4)
+    pl.semaphore_wait(barrier, jnp.where(section == 0, 4, 3))
     for d in range(2):
         products(d, 0, functools.partial(load_operands, d, 1))
     for d in range(2):
         part_copy(d, 0).wait_recv()
-        for q in range(2):
+        for q in range(pieces):
             reduce_main(q, d, 0, begin=True)
 
     def prefetch_after(d, s):
@@ -906,20 +924,17 @@
     lax.fori_loop(0, n, send_tails, 0)
 
     def scatter_step(s, carry):
-        for q in range(2):
+        for q in range(pieces):
             for d in range(2):
                 if q == 0:
                     part_copy(d, s).wait_recv()
                 reduce_main(q, d, s)
 
         for d in range(2):
-            @pl.when(s > 0)
-            def _():
-                part_copy(d, s - 1).wait_send()
-
             @pl.when(s > 1)
             def _():
-                for q in range(2):
+                part_copy(d, s - 2).wait_send()
+                for q in range(pieces):
                     ring_copy(q, d, s - 2).wait_send()
 
             products(d, s + 1, functools.partial(prefetch_after, d, s + 2))
@@ -935,7 +950,7 @@
         return carry
 
     lax.fori_loop(1, n - 1, scatter_step, 0)
-    for q in range(2):
+    for q in range(pieces):
         for d in range(2):
             if q == 0:
                 part_copy(d, n - 1).wait_recv()
@@ -951,13 +966,13 @@
             gather_copy(q, d, t + 1).start()
 
         pair_copy(q, d, t + 1).start()
-        if q == 2:
+        if q == pieces:
             @pl.when(section == 0)
             def _():
                 cross_copy(d, t + 1, True).start()
 
     def pass_pair(d, t):
-        pair_landed(2, d, t).wait_recv()
+        pair_landed(pieces, d, t).wait_recv()
 
         @pl.when(section == 0)
         def _():
@@ -972,13 +987,13 @@
         for q, d in mains:
             gather_step(q, d, t)
         for d in range(2):
-            gather_step(2, d, t - 1)
+            gather_step(pieces, d, t - 1)
             pass_pair(d, t - 1)
         return carry
 
     lax.fori_loop(1, n - 1, spread, 0)
     for d in range(2):
-        gather_step(2, d, n - 2)
+        gather_step(pieces, d, n - 2)
         pass_pair(d, n - 2)
     for d in range(2):
         pass_pair(d, n - 1)
@@ -995,24 +1010,24 @@
     for q, d in streams:
         keep_copy(q, d).wait()
     for d in range(2):
-        for s in range(max(n - 2, 0), n):
+        for s in range(max(n - 3, 0), n):
             part_copy(d, s).wait_send()
         for s in range(max(n - 3, 0), n - 1):
-            for q in range(2):
+            for q in range(pieces):
                 ring_copy(q, d, s).wait_send()
 
     def finish(s, carry):
         for d in range(2):
             tail_part_copy(d, s).wait_send()
-            for q in range(3):
+            for q in range(pieces + 1):
                 pair_copy(q, d, s).wait_send()
-                if q < 2:
+                if q < pieces:
                     pair_landed(q, d, s).wait_recv()
 
             @pl.when(s < n - 1)
             def _():
-                ring_copy(2, d, s).wait_send()
-                for q in range(3):
+                ring_copy(pieces, d, s).wait_send()
+                for q in range(pieces + 1):
                     gather_copy(q, d, s).wait_send()
 
             for mine in (True, False):
@@ -1028,10 +1043,24 @@
     lax.fori_loop(0, n, finish, 0)
 
 
-def unpack_kernel(
-    blocks, total, attend, project, up, down, coming, going, in_sem, out_sem
+def finish_kernel(
+    blocks, total, tails, cross, out_in, feat_in,
+    out, feat, embed, places, attend, project, up, down, embed_vectors, gains, vectors, up_bias, rms,
+    coming, going, ends, wide_ends, out_hold, feat_hold, in_sem, out_sem, ends_sem, plain_sem,
+    embed_sem,
 ):
     members, share, width = total.shape
+    section = lax.axis_index("section")
+    tail = tails.shape[1]
+    embed_share = tail - SMALL
+    held = [(out_in, out_hold, out), (feat_in, feat_hold, feat)]
+    plain_in = [
+        pltpu.make_async_copy(src, hold, plain_sem.at[i]) for i, (src, hold, _) in enumerate(held)
+    ]
+    plain_out = [
+        pltpu.make_async_copy(hold, dst, plain_sem.at[2 + i])
+        for i, (_, hold, dst) in enumerate(held)
+    ]
     slots, unit = coming.shape[:2]
     per_block, per_member = width // unit, share // unit
     count = members * per_member
@@ -1049,8 +1078,14 @@
             dst.at[pl.ds(pl.multiple_of(row, 16), unit), pl.ds(pl.multiple_of(column, 128), width)],
             out_sem.at[slot])
 
+    own_ends = pltpu.make_async_copy(tails, ends.at[0], ends_sem.at[0])
+    far_ends = pltpu.make_async_copy(cross, ends.at[1], ends_sem.at[1])
     for u in range(slots):
         in_copy(u).start()
+    own_ends.start()
+    far_ends.start()
+    for copy in plain_in:
+        copy.start()
 
     def step(u, carry):
         slot = lax.rem(u, slots)
@@ -1086,6 +1121,37 @@
         return carry
 
     lax.fori_loop(0, count, step, 0)
+    for copy in plain_in:
+        copy.wait()
+    for copy in plain_out:
+        copy.start()
+    own_ends.wait()
+    far_ends.wait()
+    small = ends[0, 0, embed_share:, :].astype(jnp.float32)
+    gains[...] = small[0:2, :]
+    vectors[...] = small[2:8, :]
+    for i in range(blocks):
+        up_bias[:, i * width : (i + 1) * width] = small[8 + i : 9 + i, :]
+    stat = small[15:16, :]
+    rms[...] = jnp.sqrt(stat[:, 0:3] / (stat[:, 3:4] * width))
+    embed_vectors[...] = ends[section, 0, embed_share:, :].astype(jnp.float32)[12:15, :]
+
+    def widen(w, carry):
+        wide_ends[w] = ends[section, w, 0:embed_share, :].astype(jnp.float32)
+        return carry
+
+    lax.fori_loop(0, members, widen, 0)
+    per_weight = embed.shape[0] // embed_share
+    leave = []
+    for w in range(members):
+        at = w if w < per_weight else w - per_weight
+        dst = embed if w < per_weight else places
+        leave.append(pltpu.make_async_copy(
+            wide_ends.at[w], dst.at[pl.ds(at * embed_share, embed_share)], embed_sem.at[w]))
+    for copy in leave:
+        copy.start()
+    for copy in leave + plain_out:
+        copy.wait()
     for u in range(count - slots, count):
         out_copy(u, project, 0, 0).wait()
 
@@ -1095,16 +1161,17 @@
 SMEM = pl.BlockSpec(memory_space=pltpu.SMEM)
 LOW = jnp.bfloat16
 WIDE = jnp.float32
+PIECES = 2
 
 
 def shaped(kind, *dims):
     return jax.ShapeDtypeStruct(dims, kind)
 
 
-def run_forward(features, chosen, pos_embed, weights, cols, kind_offset, mask_row, bias_row,
-                live_row, gains, vectors, up_bias):
+def run_forward(features, masked, valid, kinds, embed_weight, embed_vectors, pos_embed, norm_gains,
+                vectors, qkv_weight, out_weight, up_weight, up_bias, down_weight):
     clips, length, feat_width = features.shape
-    width, feed = weights[2].shape
+    width, feed = up_weight.shape[1:]
     blocks = feed // width
     dma = pltpu.SemaphoreType.DMA
     vm = pltpu.VMEM
@@ -1118,31 +1185,35 @@
             shaped(WIDE, clips, length, width),
             shaped(LOW, clips, length, feed),
             shaped(LOW, clips, length, width // 2),
+            shaped(WIDE, clips, length, 128),
             shaped(WIDE, 8, width),
         ),
-        in_specs=[ANY] * 7 + [VMEM] * 8,
-        out_specs=(ANY,) * 7 + (VMEM,),
+        in_specs=[SMEM] + [ANY] * 13,
+        out_specs=(ANY,) * 7 + (VMEM,) * 2,
         scratch_shapes=[
-            vm(features.shape, LOW), vm(chosen.shape, LOW), vm(pos_embed.shape, WIDE),
+            vm(features.shape, LOW), vm(masked.shape, jnp.int32), vm(valid.shape, jnp.int32),
+            vm(embed_weight.shape, LOW), vm(embed_vectors.shape, WIDE), vm(pos_embed.shape, WIDE),
+            vm(norm_gains.shape[1:], WIDE), vm(vectors.shape[1:], WIDE),
             vm((width, 3 * width), LOW), vm((width, width), LOW), vm((width, feed), LOW),
-            vm((feed, width), LOW),
+            vm(up_bias.shape, WIDE), vm((feed, width), LOW),
+            vm((feat_width, width), LOW), vm((clips, 1, length), WIDE),
             vm((length, width), WIDE), vm((length, width), LOW), vm((length, 3 * width), LOW),
             vm((2, 2, length, length), LOW), vm((length, width), LOW), vm((length, width), WIDE),
             vm((length, width), LOW), vm((length, feed), LOW), vm((length, feed), LOW),
             vm((clips, length, width), LOW), vm((clips, length, width), LOW),
-            dma((7,)), dma((7 + blocks,)), dma((2,)), dma((clips, 2)), dma((clips, 2)),
+            dma((13,)), dma((7 + blocks,)), dma((2,)), dma((clips, 2)), dma((clips, 2)),
             dma((clips, 2)), dma((clips, 2)), dma((clips, 2)),
         ],
         compiler_params=pltpu.CompilerParams(
             collective_id=1, has_side_effects=True, vmem_limit_bytes=56 * 2**20
         ),
-    )(features, chosen, pos_embed, *weights, cols, kind_offset, mask_row, bias_row, live_row,
-      gains, vectors, up_bias)
+    )(kinds, features, masked, valid, embed_weight, embed_vectors, pos_embed, norm_gains, vectors,
+      qkv_weight, out_weight, up_weight, up_bias, down_weight)
 
 
 def run_backward(cotangent, weights, x, qkv, probs, middle, slope, left, gains):
     clips, length, width = cotangent.shape
-    feed = weights[2].shape[1]
+    feed = weights[2].shape[2]
     blocks = feed // width
     dma = pltpu.SemaphoreType.DMA
     vm = pltpu.VMEM
@@ -1155,11 +1226,11 @@
             shaped(WIDE, 8, width),
             shaped(WIDE, 1, feed),
         ),
-        in_specs=[ANY] * 11 + [VMEM],
+        in_specs=[ANY] * 12,
         out_specs=(ANY, ANY, ANY, VMEM, VMEM),
         scratch_shapes=[
             vm((width, 3 * width), LOW), vm((width, width), LOW), vm((width, feed), LOW),
-            vm((feed, width), LOW),
+            vm((feed, width), LOW), vm(gains.shape[1:], WIDE),
             vm((clips, length, width), WIDE), vm((clips, length, 3 * width), LOW),
             vm((3, 2, length, length), LOW), vm((clips, length, width), WIDE),
             vm((clips, length, feed), LOW), vm((clips, length, width), LOW),
@@ -1167,7 +1238,7 @@
             vm((length, width), LOW), vm((length, width), LOW), vm((length, 3 * width), LOW),
             vm((clips, length, width), LOW),
             vm((clips * length, width), LOW), vm((width, clips * length), LOW),
-            dma((2,)), dma((4,)), dma((clips, 5)), dma((3,)), dma((5 + blocks,)), dma((clips,)),
+            dma((2,)), dma((5,)), dma((clips, 5)), dma((3,)), dma((5 + blocks,)), dma((clips,)),
             dma((clips, 2)), dma((clips, 2)),
         ],
         compiler_params=pltpu.CompilerParams(
@@ -1176,7 +1247,7 @@
     )(cotangent, *weights, x, qkv, probs, middle, slope, left, gains)
 
 
-def run_sums(members, info, turned, right, dx, features, chosen, cols, small, up_sums, stats):
+def run_sums(members, kinds, turned, right, dx, features, embed_weight, cols, small, up_sums, stats):
     width, rows = turned.shape[1:]
     clips, length, feat_width = features.shape
     n = members // 2
@@ -1189,8 +1260,8 @@
     dma = pltpu.SemaphoreType.DMA
     vm = pltpu.VMEM
     sems = [dma((2, 2 * per_member + 2)), dma((3,)), dma((2, 2 * n)), dma((2, 2 * n))]
-    sems += [dma((2, 3, n)) for _ in range(6)]
-    sems += [dma((2, 3)), dma((2, 2, n)), dma((2, 2, n)), dma((3,))]
+    sems += [dma((2, PIECES + 1, n)) for _ in range(6)]
+    sems += [dma((2, PIECES + 1)), dma((2, 2, n)), dma((2, 2, n)), dma((3,))]
     return pl.pallas_call(
         functools.partial(sums_kernel, members),
         out_shape=(
@@ -1203,39 +1274,49 @@
         out_specs=(ANY,) * 4,
         scratch_shapes=[
             vm((2, 2 * per_member, unit, rows), LOW), vm((2, 2, rows, half), LOW),
-            vm((2, 3, share, half), LOW), vm((2, 2, share, half), LOW),
+            vm((2, 3, 2, share, half), LOW),
             vm((2, n, share, half), LOW), vm((2, n - 1, share, half), LOW),
             vm((members, tail, width), LOW), vm((2, n, tail, half), LOW),
             vm((2, n, tail, half), LOW), vm((2, n - 1, tail, half), LOW),
-            vm((clips, length, width), LOW), vm(features.shape, LOW), vm(chosen.shape, LOW),
+            vm((clips, length, width), LOW), vm(features.shape, LOW), vm(embed_weight.shape, LOW),
             vm(features.shape, LOW), vm((embed_rows, width), LOW), vm((SMALL, width), WIDE),
             sems,
         ],
         compiler_params=pltpu.CompilerParams(
             collective_id=0, has_side_effects=True, vmem_limit_bytes=60 * 2**20
         ),
-    )(info, turned, right, dx, features, chosen, cols, small, up_sums, stats)
-
-
-def run_unpack(total, blocks):
+    )(kinds, turned, right, dx, features, embed_weight, cols, small, up_sums, stats)
+
+
+def run_finish(total, tails, cross, output, feature_out, feed, feat_width):
     members, share, width = total.shape
     unit = unit_rows(members, width)
-    slots = 6
+    blocks = feed // width
+    embed_share = tails.shape[1] - SMALL
+    places = members * embed_share - 2 * feat_width
+    slots = 12
     dma = pltpu.SemaphoreType.DMA
+    vm = pltpu.VMEM
     return pl.pallas_call(
-        functools.partial(unpack_kernel, blocks),
+        functools.partial(finish_kernel, blocks),
         out_shape=(
+            shaped(LOW, *output.shape), shaped(LOW, *feature_out.shape),
+            shaped(WIDE, 2 * feat_width, width), shaped(WIDE, places, width),
             shaped(WIDE, width, 3 * width), shaped(WIDE, width, width),
-            shaped(WIDE, width, blocks * width), shaped(WIDE, blocks * width, width),
+            shaped(WIDE, width, feed), shaped(WIDE, feed, width),
+            shaped(WIDE, 3, width), shaped(WIDE, 2, width), shaped(WIDE, 6, width),
+            shaped(WIDE, 1, feed), shaped(WIDE, 1, 3),
         ),
-        in_specs=[ANY],
-        out_specs=(ANY,) * 4,
+        in_specs=[ANY] * 5,
+        out_specs=(ANY,) * 8 + (VMEM,) * 5,
         scratch_shapes=[
-            pltpu.VMEM((slots, unit, width), LOW), pltpu.VMEM((slots, unit, width), WIDE),
-            dma((slots,)), dma((slots,)),
+            vm((slots, unit, width), LOW), vm((slots, unit, width), WIDE),
+            vm((2, *tails.shape), LOW), vm((members, embed_share, width), WIDE),
+            vm(output.shape, LOW), vm(feature_out.shape, LOW),
+            dma((slots,)), dma((slots,)), dma((2,)), dma((4,)), dma((members,)),
         ],
-        compiler_params=pltpu.CompilerParams(vmem_limit_bytes=32 * 2**20),
-    )(total)
+        compiler_params=pltpu.CompilerParams(vmem_limit_bytes=56 * 2**20),
+    )(total, tails, cross, output, feature_out)
 
 
 def local(
@@ -1255,49 +1336,35 @@
     down_weight,
     cotangent,
 ):
-    is_first = lax.axis_index("section") == 0
     members = lax.axis_size("wide")
     clips, length, feat_width = features.shape
     width = pos_embed.shape[1]
-    weights = (qkv_weight[0], out_weight[0], up_weight[0], down_weight[0])
-    blocks = up_weight.shape[2] // width
-    chosen = jnp.where(kinds[:, None, None] == 0, embed_weight[0], embed_weight[1])
-    kind_offset = jnp.where(kinds[:, None] == 0, embed_vectors[0], embed_vectors[1])[:, None]
-    lane = jnp.arange(128)
-    cols = jnp.where(
-        lane == 0, masked[:, :, None], jnp.where(lane == 1, valid[:, :, None], 0)
-    ).astype(WIDE)
-    live_row = jnp.where(valid > 0, 0.0, NEG)[:, None]
-    rows = vectors[0]
-    bias_row = jnp.concatenate([rows[1], jnp.zeros((width,), WIDE), rows[2]])[None]
-    left, x, qkv, probs, middle, slope, output, stats = run_forward(
-        features, chosen, pos_embed, weights, cols, kind_offset, embed_vectors[2:3], bias_row,
-        live_row, norm_gains[0], rows, up_bias)
+    feed = up_weight.shape[2]
+    left, x, qkv, probs, middle, slope, output, cols, stats = run_forward(
+        features, masked, valid, kinds, embed_weight, embed_vectors, pos_embed, norm_gains, vectors,
+        qkv_weight, out_weight, up_weight, up_bias, down_weight)
+    weights = (qkv_weight, out_weight, up_weight, down_weight)
     right, dx, turned, small, up_sums = run_backward(
-        cotangent, weights, x, qkv, probs, middle, slope, left, norm_gains[0])
+        cotangent, weights, x, qkv, probs, middle, slope, left, norm_gains)
     total, tails, cross, feature_out = run_sums(
-        members, kinds, turned, right, dx, features, chosen, cols, small, up_sums, stats)
-    attend_total, project_total, up_total, down_total = run_unpack(total, blocks)
-    embed_share = (2 * feat_width + length) // members
-    ends = jnp.where(is_first, tails, cross)
-    embed_total = ends[:, :embed_share].reshape(-1, width).astype(WIDE)
-    small_total = tails[0, -SMALL:].astype(WIDE)
-    stat_row = small_total[15]
-    rms_out = jnp.sqrt(stat_row[0:3] / (stat_row[3] * width))[None]
+        members, kinds, turned, right, dx, features, embed_weight, cols, small, up_sums, stats)
+    (output, feature_out, embed, places, attend, project, up, down, embed_rows, gain_rows,
+     vector_rows, up_rows, rms) = run_finish(
+        total, tails, cross, output, feature_out, feed, feat_width)
     return (
         output,
         feature_out,
-        embed_total[: 2 * feat_width].reshape(2, feat_width, width),
-        ends[0, embed_share + 12 : embed_share + 15].astype(WIDE),
-        embed_total[2 * feat_width :],
-        small_total[None, 0:2],
-        small_total[None, 2:8],
-        attend_total[None],
-        project_total[None],
-        up_total[None],
-        small_total[8 : 8 + blocks].reshape(1, -1),
-        down_total[None],
-        rms_out,
+        embed.reshape(2, feat_width, width),
+        embed_rows,
+        places,
+        gain_rows[None],
+        vector_rows[None],
+        attend[None],
+        project[None],
+        up[None],
+        up_rows,
+        down[None],
+        rms,
     )
 
 

time: 397 us -> 384 us (0.967)
  local copies, waits for them, and re-layouts: 15.4 us -> 2.7 us
  Pallas kernels: 373 us -> 380 us
  other arithmetic: 5.92 us -> 0 us
    pallas_call x1, Pallas kernels: 9.79 us -> 17.4 us  [run_finish(): pl.pallas_call(functools.partial(finish_kernel, blocks), out_shape=(shape...]
    unnamed x20 -> x2, local copies, waits for them, and re-layouts: 8.48 us -> 2.7 us
    slice x6 -> x0, local copies, waits for them, and re-layouts: 4.59 us -> none  [the longest x1 1.98 us: local(): embed_total[2 * feat_width:]]
where the time goes in v4:
time: 384 us; the launch traced here: 383 us
  Pallas kernels  380 us (99%)
    pallas_call x1, Pallas kernels, run_sums(): pl.pallas_call(functools.partial(sums_kernel, members), out_shape=(shaped...  179 us
    pallas_call x1, Pallas kernels, run_forward(): pl.pallas_call(forward_kernel, out_shape=(shaped(LOW, 3 + blocks, clips *...  94.2 us
    pallas_call x1, Pallas kernels, run_backward(): pl.pallas_call(backward_kernel, out_shape=(shaped(LOW, 5 + blocks, clips...  89.9 us
    pallas_call x1, Pallas kernels, run_finish(): pl.pallas_call(functools.partial(finish_kernel, blocks), out_shape=(shape...  17.4 us

profile of v4, /device:TPU:0, one launch (start us, length us, event | category | flops | bytes accessed | tf_op | source)
XLA Modules:
  0.0 383.5 jit_solution(7421283986379964129)
XLA Ops:
  0.6 1.3 copy.28.vectors_h
  2.0 94.2 %shard_map.246 = (bf16[7,1024,768]{2,1,0:T(8,128)(2,1)}, f32[2,512,768]{2,1,0:T(8,128)}, bf16[2,512,2304]{2,1,0:T(8,128)(2,1)}, bf16[2,12,512,512]{3,2,1,0:T(8,1...) custom-call(s32[2]{0:T(128)} %kinds.3, ...), custom_call_target="tpu_custom_call" | custom-call | tf_op jit(solution)/shard_map/pallas_call | solution.py:1178
  96.2 89.9 %shard_map.247 = (bf16[9,1024,768]{2,1,0:T(8,128)(2,1)}, bf16[2,512,768]{2,1,0:T(8,128)(2,1)}, bf16[7,768,1024]{2,1,0:T(8,128)(2,1)}, f32[8,768]{1,0:T(8,128)}, f32[1,3072]{1,0:T(1,128)}) custom-call(bf16[2,512,768]{2,1,0:T(8,128)(2,1)} %cot_h.1, bf16[1,768,2304]{2,1,0:T(8,128)(2,1)} %wqkv_h.3, bf16[1,768,768]{2,1,0:T(8,128)(2,1)} %wout_h.3, ...), custom_call_target="tpu_custom_call" | custom-call | tf_op jit(solution)/shard_map/pallas_call | solution.py:1220
  186.1 178.6 %shard_map.248 = (bf16[16,576,768]{2,1,0:T(8,128)(2,1)}, bf16[16,80,768]{2,1,0:T(8,128)(2,1)}, bf16[16,80,768]{2,1,0:T(8,128)(2,1)}, bf16[2,512,128]{2,1,0:T(8,128)(2,1)}) custom-call(s32[2]{0:T(128)} %kinds.3, bf16[7,768,1024]{2,1,0:T(8,128)(2,1)} %get-tuple-element.50.turned_h, bf16[9,1024,768]{2,1,0:T(8,128)(2,1)} %get-tuple-element.51.right_h, ...), custom_call_target="tpu_custom_call" | custom-call | tf_op jit(solution)/shard_map/pallas_call | solution.py:1265
  364.7 17.4 %shard_map.249 = (bf16[2,512,384]{2,1,0:T(8,128)(2,1)}, bf16[2,512,128]{2,1,0:T(8,128)(2,1)}, f32[512,768]{1,0:T(8,128)}, f32[512,768]{1,0:T(8,128)}, f32[768,23...) custom-call(bf16[16,576,768]{2,1,0:T(8,128)(2,1)} %get-tuple-element, ...), custom_call_target="tpu_custom_call" | custom-call | tf_op jit(solution)/shard_map/pallas_call | solution.py:1300
  382.1 1.4 copy.29

commit v5 on v4

--- a/solution.py
+++ b/solution.py
@@ -67,12 +67,7 @@
 
 def gelu_pair(hidden):
     decay = jnp.exp(-0.5 * hidden * hidden)
-    t = 1.0 / (1.0 + (0.3275911 * 0.5**0.5) * jnp.abs(hidden))
-    poly = 1.061405429 * 0.5
-    for term in (-1.453152027, 1.421413741, -0.284496736, 0.254829592):
-        poly = poly * t + 0.5 * term
-    upper = poly * t * decay
-    cdf = jnp.where(hidden > 0.0, 1.0 - upper, upper)
+    cdf = 0.5 + 0.5 * lax.erf(hidden * 0.5**0.5)
     return hidden * cdf, cdf + hidden * decay * 0.3989422804014327
 
 
@@ -100,9 +95,9 @@
 def forward_kernel(
     kinds, feat_h, masked_h, valid_h, embw_h, embv_h, pos_h, gains_h, vectors_h, wqkv_h, wout_h,
     wup_h, upb_h, wdown_h,
-    left_h, x_h, qkv_h, probs_h, middle_h, slope_h, out_h, cols, stats,
+    left_h, x_h, qkv_h, probs_h, inverse_h, exact_h, middle_h, slope_h, out_h, cols, stats,
     feat, masked, valid, embw, embv, pos, gains, vectors, wqkv, wout, wup, up_bias, wdown,
-    chosen, live_row,
+    chosen, dead_keys, inverse, exact,
     x, normed, qkv, probs, context, middle, hidden_in, active, slope, y, landed,
     load_sem, save_sem, probs_sem, send_sem, recv_sem, back_send, back_recv, keep_sem,
 ):
@@ -115,7 +110,7 @@
     blocks = feed // width
     loads = fetch(
         [(masked_h, masked), (valid_h, valid), (gains_h.at[0], gains),
-         (vectors_h.at[0], vectors), (upb_h, up_bias),
+         (vectors_h, vectors), (upb_h, up_bias),
          (feat_h, feat), (embw_h, embw), (embv_h, embv), (pos_h, pos),
          (wqkv_h.at[0], wqkv), (wout_h.at[0], wout), (wup_h.at[0], wup), (wdown_h.at[0], wdown)],
         load_sem)
@@ -128,7 +123,6 @@
         flags = jnp.where(sublane == 0, masked[c : c + 1, :], 0)
         flags = jnp.where(sublane == 1, valid[c : c + 1, :], flags)
         cols[c] = flags.astype(jnp.float32).T
-        live_row[c] = jnp.where(valid[c : c + 1, :] > 0, 0.0, NEG)
     low_lanes = lax.broadcasted_iota(jnp.int32, (1, 128), 1) < HD
 
     def save(index, src, dst):
@@ -142,7 +136,7 @@
             (hidden_in, left_h.at[2, rows]), (slope, slope_h.at[c]),
         ] + [
             (active.at[:, pl.ds(b * width, width)], left_h.at[3 + b, rows]) for b in range(blocks)
-        ]
+        ] + [(inverse, inverse_h.at[c]), (exact, exact_h.at[c])]
         return [save(i, src, dst) for i, (src, dst) in enumerate(pairs)]
 
     def probs_save(c, pair):
@@ -205,7 +199,7 @@
         own[0].start()
 
         def norm_rows(source, target, which, shift, first, count):
-            gain, offset = gains[which : which + 1, :], vectors[shift : shift + 1, :]
+            gain, offset = gains[which : which + 1, :], vectors[shift]
 
             def tile(i, carry):
                 rows = tile_of(i, 64)
@@ -229,15 +223,22 @@
             at = tile_of(j, 256)
             part = dot_nn(normed[...], wqkv[:, at])
             if j < width // 256:
-                part = part + vectors[1:2, at]
+                part = part + vectors[1, :, at]
             elif j >= 2 * width // 256:
-                part = part + vectors[2:3, tile_of(j - 2 * width // 256, 256)]
+                part = part + vectors[2, :, tile_of(j - 2 * width // 256, 256)]
             qkv[:, at] = part.astype(low)
             return carry
 
         loop(3 * width // 256, qkv_tile, 9)
         own[2].start()
         after_first(3)
+        after_first(7 + blocks)
+        after_first(8 + blocks)
+
+        lane = lax.broadcasted_iota(jnp.int32, (1, 128), 1)
+        scale, one, zero = (jnp.full((1, 128), v, low) for v in (HD**-0.5, 1.0, 0.0))
+        dead_keys[...] = jnp.broadcast_to(
+            jnp.where(cols[c][:, 1:2] > 0.0, 0.0, NEG), dead_keys.shape).astype(low)
 
         def attend(pair, carry):
             @pl.when((pair > 1) | (c > 0))
@@ -250,20 +251,27 @@
             values_in = qkv[:, tile_of(pair + 2 * heads2, 128)]
             outs = []
             for h in range(2):
-                pick = jnp.where(low_lanes == (h == 0), HD**-0.5, 0.0).astype(low)
-                scores = dot_nt(queries * pick, keys_in) + live_row[c]
+                mine = low_lanes == (h == 0)
+                extra = lane == (64 if h == 0 else 0)
+                scaled = jnp.where(mine, queries * scale, jnp.where(extra, one, zero))
+                scores = dot_nt(scaled, jnp.where(extra, dead_keys[...], keys_in))
                 top = jnp.max(scores, axis=-1, keepdims=True)
-                scores = jnp.exp(scores - top)
-                total = jnp.sum(scores, axis=-1, keepdims=True)
-                soft = (scores * (1.0 / total)).astype(low)
+                soft = jnp.exp(scores - top).astype(low)
                 probs[lax.rem(pair, 2), h] = soft
-                outs.append(dot_nn(soft, values_in))
-            context[:, at] = jnp.where(low_lanes, outs[0], outs[1]).astype(low)
+                outs.append(dot_nn(soft, jnp.where(mine, values_in, one)))
+            total = pltpu.roll(jnp.where(low_lanes, outs[1], outs[0]), 64, 1)
+            scale_back = 1.0 / total
+            inverse[:, at] = scale_back
+            mixed = jnp.where(low_lanes, outs[0], outs[1]) * scale_back
+            exact[:, at] = mixed
+            context[:, at] = mixed.astype(low)
             probs_save(c, pair).start()
             return carry
 
         lax.fori_loop(0, heads2, attend, 0)
         own[3].start()
+        own[7 + blocks].start()
+        own[8 + blocks].start()
         after_first(4)
 
         @pl.when(c == 0)
@@ -274,7 +282,7 @@
 
         def out_tile(j, carry):
             at = tile_of(j, 256)
-            branch = dot_nn(context[...], wout[:, at]) + vectors[3:4, at]
+            branch = dot_nn(context[...], wout[:, at]) + vectors[3, :, at]
             middle[:, at] = x[:, at] + branch
             stats[1:2, at] += column_sum(branch * branch * live)
             return carry
@@ -303,14 +311,14 @@
                 slope[rows, at] = steep.astype(low)
                 return carry
 
-            loop(feed // 256, up_tile, 6)
+            loop(feed // 256, up_tile, 12)
             if h == 1:
-                for copy in own[6:]:
+                for copy in own[6 : 7 + blocks]:
                     copy.start()
 
             def down_tile(j, carry):
                 at = tile_of(j, 256)
-                mixer = dot_nn(active[rows, :], wdown[:, at]) + vectors[5:6, at]
+                mixer = dot_nn(active[rows, :], wdown[:, at]) + vectors[5, :, at]
                 total = middle[rows, at] + mixer
                 flags = cols[c, rows, :][:, 1:2]
                 stats[0:1, at] += column_sum(total * total * flags)
@@ -349,9 +357,9 @@
 
 
 def backward_kernel(
-    cot_h, wqkv_h, wout_h, wup_h, wdown_h, x_h, qkv_h, probs_h, middle_h, slope_h, left_h, gains_h,
+    cot_h, wqkv_h, wout_h, wup_h, wdown_h, x_h, qkv_h, probs_h, inverse_h, exact_h, middle_h, slope_h, left_h, gains_h,
     right_h, dx_h, turned_h, small, up_sums,
-    wqkv, wout, wup, wdown, gains, x, qkv, probs, middle, slope, g,
+    wqkv, wout, wup, wdown, gains, x, qkv, probs, inverse, context, middle, slope, g,
     d_hidden, wide_grad, d_middle, d_branch, d_context, d_qkv, d_low, upright, turned,
     turn_sem, load_sem, state_sem, probs_sem, save_sem, dx_sem, send_sem, recv_sem,
 ):
@@ -369,7 +377,8 @@
         return pltpu.make_async_copy(cot_h.at[c], g.at[c], state_sem.at[c, 0])
 
     def state_loads(c):
-        pairs = [(slope_h, slope), (middle_h, middle), (qkv_h, qkv), (x_h, x)]
+        pairs = [(slope_h, slope), (middle_h, middle), (qkv_h, qkv), (x_h, x), (inverse_h, inverse),
+                 (exact_h, context)]
         return [
             pltpu.make_async_copy(src.at[c], dst.at[c], state_sem.at[c, 1 + i])
             for i, (src, dst) in enumerate(pairs)
@@ -501,7 +510,7 @@
                 up_sums[:, at] += column_sum(grad.astype(f32))
                 return carry
 
-            loop(feed // 256, feed_tile, 6)
+            loop(feed // 256, feed_tile, 12)
 
             def in_tile(j, carry):
                 at = tile_of(j, 256)
@@ -539,6 +548,8 @@
 
         loop(width // 256, context_tile, 3)
         state[2].wait()
+        state[4].wait()
+        state[5].wait()
         after_first(0, 3)
 
         def attend(pair, carry):
@@ -548,16 +559,17 @@
             at, key_at = tile_of(pair, 128), tile_of(pair + heads2, 128)
             value_at = tile_of(pair + 2 * heads2, 128)
             queries, keys_in, values_in = qkv[c, :, at], qkv[c, :, key_at], qkv[c, :, value_at]
-            grad = d_context[:, at]
+            grad_wide = d_context[:, at].astype(f32) * inverse[c, :, at]
+            grad = grad_wide.astype(low)
+            along = grad.astype(f32) * context[c, :, at]
             queries_t, grad_t = queries.T, grad.T
             d_queries, keys_t, values_t = [], [], []
             for h in range(2):
-                pick = jnp.where(low_lanes == (h == 0), 1.0, 0.0).astype(low)
+                mine = low_lanes == (h == 0)
                 soft = probs[slot, h]
-                soft_wide = soft.astype(f32)
-                d_soft = dot_nt(grad * pick, values_in)
-                delta = jnp.sum(soft_wide * d_soft, axis=-1, keepdims=True)
-                d_scores = (soft_wide * (d_soft - delta)).astype(low)
+                delta = jnp.sum(jnp.where(mine, along, 0.0), axis=-1, keepdims=True)
+                d_soft = dot_nt(jnp.where(mine, grad, jnp.zeros_like(grad)), values_in)
+                d_scores = (soft.astype(f32) * (d_soft - delta)).astype(low)
                 part = slice(h * HD, (h + 1) * HD)
                 values_t.append(dot_nn(grad_t[part], soft))
                 keys_t.append(dot_nn(queries_t[part], d_scores))
@@ -1129,7 +1141,8 @@
     far_ends.wait()
     small = ends[0, 0, embed_share:, :].astype(jnp.float32)
     gains[...] = small[0:2, :]
-    vectors[...] = small[2:8, :]
+    for i in range(6):
+        vectors[i] = small[2 + i : 3 + i, :]
     for i in range(blocks):
         up_bias[:, i * width : (i + 1) * width] = small[8 + i : 9 + i, :]
     stat = small[15:16, :]
@@ -1183,25 +1196,28 @@
             shaped(LOW, clips, length, 3 * width),
             shaped(LOW, clips, H, length, length),
             shaped(WIDE, clips, length, width),
+            shaped(WIDE, clips, length, width),
+            shaped(WIDE, clips, length, width),
             shaped(LOW, clips, length, feed),
             shaped(LOW, clips, length, width // 2),
             shaped(WIDE, clips, length, 128),
             shaped(WIDE, 8, width),
         ),
         in_specs=[SMEM] + [ANY] * 13,
-        out_specs=(ANY,) * 7 + (VMEM,) * 2,
+        out_specs=(ANY,) * 9 + (VMEM,) * 2,
         scratch_shapes=[
             vm(features.shape, LOW), vm(masked.shape, jnp.int32), vm(valid.shape, jnp.int32),
             vm(embed_weight.shape, LOW), vm(embed_vectors.shape, WIDE), vm(pos_embed.shape, WIDE),
-            vm(norm_gains.shape[1:], WIDE), vm(vectors.shape[1:], WIDE),
+            vm(norm_gains.shape[1:], WIDE), vm(vectors.shape, WIDE),
             vm((width, 3 * width), LOW), vm((width, width), LOW), vm((width, feed), LOW),
             vm(up_bias.shape, WIDE), vm((feed, width), LOW),
-            vm((feat_width, width), LOW), vm((clips, 1, length), WIDE),
+            vm((feat_width, width), LOW), vm((length, 128), LOW), vm((length, width), WIDE),
+            vm((length, width), WIDE),
             vm((length, width), WIDE), vm((length, width), LOW), vm((length, 3 * width), LOW),
             vm((2, 2, length, length), LOW), vm((length, width), LOW), vm((length, width), WIDE),
             vm((length, width), LOW), vm((length, feed), LOW), vm((length, feed), LOW),
             vm((clips, length, width), LOW), vm((clips, length, width), LOW),
-            dma((13,)), dma((7 + blocks,)), dma((2,)), dma((clips, 2)), dma((clips, 2)),
+            dma((13,)), dma((9 + blocks,)), dma((2,)), dma((clips, 2)), dma((clips, 2)),
             dma((clips, 2)), dma((clips, 2)), dma((clips, 2)),
         ],
         compiler_params=pltpu.CompilerParams(
@@ -1211,7 +1227,7 @@
       qkv_weight, out_weight, up_weight, up_bias, down_weight)
 
 
-def run_backward(cotangent, weights, x, qkv, probs, middle, slope, left, gains):
+def run_backward(cotangent, weights, x, qkv, probs, inverse, exact, middle, slope, left, gains):
     clips, length, width = cotangent.shape
     feed = weights[2].shape[2]
     blocks = feed // width
@@ -1226,25 +1242,26 @@
             shaped(WIDE, 8, width),
             shaped(WIDE, 1, feed),
         ),
-        in_specs=[ANY] * 12,
+        in_specs=[ANY] * 14,
         out_specs=(ANY, ANY, ANY, VMEM, VMEM),
         scratch_shapes=[
             vm((width, 3 * width), LOW), vm((width, width), LOW), vm((width, feed), LOW),
             vm((feed, width), LOW), vm(gains.shape[1:], WIDE),
             vm((clips, length, width), WIDE), vm((clips, length, 3 * width), LOW),
-            vm((3, 2, length, length), LOW), vm((clips, length, width), WIDE),
+            vm((2, 2, length, length), LOW), vm((clips, length, width), WIDE),
+            vm((clips, length, width), WIDE), vm((clips, length, width), WIDE),
             vm((clips, length, feed), LOW), vm((clips, length, width), LOW),
             vm((length, feed), LOW), vm((length, width), WIDE), vm((length, width), WIDE),
             vm((length, width), LOW), vm((length, width), LOW), vm((length, 3 * width), LOW),
             vm((clips, length, width), LOW),
             vm((clips * length, width), LOW), vm((width, clips * length), LOW),
-            dma((2,)), dma((5,)), dma((clips, 5)), dma((3,)), dma((5 + blocks,)), dma((clips,)),
+            dma((2,)), dma((5,)), dma((clips, 7)), dma((3,)), dma((5 + blocks,)), dma((clips,)),
             dma((clips, 2)), dma((clips, 2)),
         ],
         compiler_params=pltpu.CompilerParams(
-            collective_id=2, has_side_effects=True, vmem_limit_bytes=60 * 2**20
+            collective_id=2, has_side_effects=True, vmem_limit_bytes=62 * 2**20
         ),
-    )(cotangent, *weights, x, qkv, probs, middle, slope, left, gains)
+    )(cotangent, *weights, x, qkv, probs, inverse, exact, middle, slope, left, gains)
 
 
 def run_sums(members, kinds, turned, right, dx, features, embed_weight, cols, small, up_sums, stats):
@@ -1304,7 +1321,7 @@
             shaped(WIDE, 2 * feat_width, width), shaped(WIDE, places, width),
             shaped(WIDE, width, 3 * width), shaped(WIDE, width, width),
             shaped(WIDE, width, feed), shaped(WIDE, feed, width),
-            shaped(WIDE, 3, width), shaped(WIDE, 2, width), shaped(WIDE, 6, width),
+            shaped(WIDE, 3, width), shaped(WIDE, 2, width), shaped(WIDE, 6, 1, width),
             shaped(WIDE, 1, feed), shaped(WIDE, 1, 3),
         ),
         in_specs=[ANY] * 5,
@@ -1340,12 +1357,12 @@
     clips, length, feat_width = features.shape
     width = pos_embed.shape[1]
     feed = up_weight.shape[2]
-    left, x, qkv, probs, middle, slope, output, cols, stats = run_forward(
-        features, masked, valid, kinds, embed_weight, embed_vectors, pos_embed, norm_gains, vectors,
-        qkv_weight, out_weight, up_weight, up_bias, down_weight)
+    left, x, qkv, probs, inverse, exact, middle, slope, output, cols, stats = run_forward(
+        features, masked, valid, kinds, embed_weight, embed_vectors, pos_embed, norm_gains,
+        vectors.transpose(1, 0, 2), qkv_weight, out_weight, up_weight, up_bias, down_weight)
     weights = (qkv_weight, out_weight, up_weight, down_weight)
     right, dx, turned, small, up_sums = run_backward(
-        cotangent, weights, x, qkv, probs, middle, slope, left, norm_gains)
+        cotangent, weights, x, qkv, probs, inverse, exact, middle, slope, left, norm_gains)
     total, tails, cross, feature_out = run_sums(
         members, kinds, turned, right, dx, features, embed_weight, cols, small, up_sums, stats)
     (output, feature_out, embed, places, attend, project, up, down, embed_rows, gain_rows,
@@ -1358,7 +1375,7 @@
         embed_rows,
         places,
         gain_rows[None],
-        vector_rows[None],
+        vector_rows.transpose(1, 0, 2),
         attend[None],
         project[None],
         up[None],

time: 384 us -> 363 us (0.945)
  Pallas kernels: 380 us -> 361 us
    pallas_call x1, Pallas kernels: 94.2 us -> 81.3 us  [run_forward(): pl.pallas_call(forward_kernel, out_shape=(shaped(LOW, 3 + blocks, clips *...]
    pallas_call x1, Pallas kernels: 89.9 us -> 84 us  [run_backward(): pl.pallas_call(backward_kernel, out_shape=(shaped(LOW, 5 + blocks, clips...]
where the time goes in v5:
time: 363 us; the launch traced here: 362 us
  Pallas kernels  361 us (99%)
    pallas_call x1, Pallas kernels, run_sums(): pl.pallas_call(functools.partial(sums_kernel, members), out_shape=(shaped...  179 us
    pallas_call x1, Pallas kernels, run_backward(): pl.pallas_call(backward_kernel, out_shape=(shaped(LOW, 5 + blocks, clips...  84 us
    pallas_call x1, Pallas kernels, run_forward(): pl.pallas_call(forward_kernel, out_shape=(shaped(LOW, 3 + blocks, clips *...  81.3 us
    pallas_call x1, Pallas kernels, run_finish(): pl.pallas_call(functools.partial(finish_kernel, blocks), out_shape=(shape...  17.4 us

profile of v5, /device:TPU:0, one launch (start us, length us, event | category | flops | bytes accessed | tf_op | source)
XLA Modules:
  0.0 362.3 jit_solution(6463717022906511491)
XLA Ops:
  0.6 81.3 %shard_map.246 = (bf16[7,1024,768]{2,1,0:T(8,128)(2,1)}, f32[2,512,768]{2,1,0:T(8,128)}, bf16[2,512,2304]{2,1,0:T(8,128)(2,1)}, bf16[2,12,512,512]{3,2,1,0:T(8,1...) custom-call(s32[2]{0:T(128)} %kinds.3, ...), custom_call_target="tpu_custom_call" | custom-call | tf_op jit(solution)/shard_map/pallas_call | solution.py:1191
  82.0 84.0 %shard_map.247 = (bf16[9,1024,768]{2,1,0:T(8,128)(2,1)}, bf16[2,512,768]{2,1,0:T(8,128)(2,1)}, bf16[7,768,1024]{2,1,0:T(8,128)(2,1)}, f32[8,768]{1,0:T(8,128)}, f32[1,3072]{1,0:T(1,128)}) custom-call(bf16[2,512,768]{2,1,0:T(8,128)(2,1)} %cot_h.1, bf16[1,768,2304]{2,1,0:T(8,128)(2,1)} %wqkv_h.3, bf16[1,768,768]{2,1,0:T(8,128)(2,1)} %wout_h.3, ...), custom_call_target="tpu_custom_call" | custom-call | tf_op jit(solution)/shard_map/pallas_call | solution.py:1236
  166.0 178.6 %shard_map.248 = (bf16[16,576,768]{2,1,0:T(8,128)(2,1)}, bf16[16,80,768]{2,1,0:T(8,128)(2,1)}, bf16[16,80,768]{2,1,0:T(8,128)(2,1)}, bf16[2,512,128]{2,1,0:T(8,128)(2,1)}) custom-call(s32[2]{0:T(128)} %kinds.3, bf16[7,768,1024]{2,1,0:T(8,128)(2,1)} %get-tuple-element.54.turned_h, bf16[9,1024,768]{2,1,0:T(8,128)(2,1)} %get-tuple-element.55.right_h, ...), custom_call_target="tpu_custom_call" | custom-call | tf_op jit(solution)/shard_map/pallas_call | solution.py:1282
  344.6 17.4 %shard_map.249 = (bf16[2,512,384]{2,1,0:T(8,128)(2,1)}, bf16[2,512,128]{2,1,0:T(8,128)(2,1)}, f32[512,768]{1,0:T(8,128)}, f32[512,768]{1,0:T(8,128)}, f32[768,23...) custom-call(bf16[16,576,768]{2,1,0:T(8,128)(2,1)} %get-tuple-element, ...), custom_call_target="tpu_custom_call" | custom-call | tf_op jit(solution)/shard_map/pallas_call | solution.py:1317

commit v6 on v5

--- a/solution.py
+++ b/solution.py
@@ -71,11 +71,8 @@
     return hidden * cdf, cdf + hidden * decay * 0.3989422804014327
 
 
-def fetch(pairs, sems):
-    copies = [pltpu.make_async_copy(src, dst, sems.at[i]) for i, (src, dst) in enumerate(pairs)]
-    for copy in copies:
-        copy.start()
-    return copies
+def fetches(pairs, sems):
+    return [pltpu.make_async_copy(src, dst, sems.at[i]) for i, (src, dst) in enumerate(pairs)]
 
 
 def greet_partner():
@@ -108,12 +105,14 @@
     feed = wup.shape[1]
     heads2 = width // 128
     blocks = feed // width
-    loads = fetch(
+    loads = fetches(
         [(masked_h, masked), (valid_h, valid), (gains_h.at[0], gains),
          (vectors_h, vectors), (upb_h, up_bias),
          (feat_h, feat), (embw_h, embw), (embv_h, embv), (pos_h, pos),
          (wqkv_h.at[0], wqkv), (wout_h.at[0], wout), (wup_h.at[0], wup), (wdown_h.at[0], wdown)],
         load_sem)
+    for copy in loads:
+        copy.start()
     greet_partner()
     stats[...] = jnp.zeros_like(stats)
     for copy in loads[:9]:
@@ -249,16 +248,21 @@
             queries = qkv[:, at]
             keys_in = qkv[:, tile_of(pair + heads2, 128)]
             values_in = qkv[:, tile_of(pair + 2 * heads2, 128)]
-            outs = []
+            raw, softs = [], []
             for h in range(2):
-                mine = low_lanes == (h == 0)
                 extra = lane == (64 if h == 0 else 0)
-                scaled = jnp.where(mine, queries * scale, jnp.where(extra, one, zero))
-                scores = dot_nt(scaled, jnp.where(extra, dead_keys[...], keys_in))
-                top = jnp.max(scores, axis=-1, keepdims=True)
-                soft = jnp.exp(scores - top).astype(low)
+                scaled = jnp.where(
+                    low_lanes == (h == 0), queries * scale, jnp.where(extra, one, zero))
+                raw.append(dot_nt(scaled, jnp.where(extra, dead_keys[...], keys_in)))
+            for h in range(2):
+                top = jnp.max(raw[h], axis=-1, keepdims=True)
+                soft = jnp.exp(raw[h] - top).astype(low)
                 probs[lax.rem(pair, 2), h] = soft
-                outs.append(dot_nn(soft, jnp.where(mine, values_in, one)))
+                softs.append(soft)
+            outs = [
+                dot_nn(softs[h], jnp.where(low_lanes == (h == 0), values_in, one))
+                for h in range(2)
+            ]
             total = pltpu.roll(jnp.where(low_lanes, outs[1], outs[0]), 64, 1)
             scale_back = 1.0 / total
             inverse[:, at] = scale_back
@@ -384,21 +388,20 @@
             for i, (src, dst) in enumerate(pairs)
         ]
 
-    @pl.when(section == 1)
-    def _():
-        cot_load(0).start()
-
-    loads = fetch(
+    loads = fetches(
         [(gains_h.at[0], gains), (wdown_h.at[0], wdown), (wup_h.at[0], wup), (wout_h.at[0], wout),
          (wqkv_h.at[0], wqkv)], load_sem)
-    for c in range(clips):
-        for copy in state_loads(c):
-            copy.start()
-
-    @pl.when(section == 1)
-    def _():
-        for c in range(1, clips):
+
+    def start_cot(c):
+        @pl.when(section == 1)
+        def _():
             cot_load(c).start()
+
+    first = state_loads(0)
+    start_cot(0)
+    for copy in (loads[1], first[0], loads[0], loads[2], first[1], loads[3], first[2], first[4],
+                 first[5], loads[4], first[3]):
+        copy.start()
 
     small[...] = jnp.zeros_like(small)
     up_sums[...] = jnp.zeros_like(up_sums)
@@ -522,6 +525,12 @@
         after_first(3, 4)
         for copy in own[4:-1]:
             copy.start()
+
+        @pl.when(c + 1 < clips)
+        def _():
+            start_cot(c + 1)
+            for copy in state_loads(c + 1):
+                copy.start()
 
         def middle_tile(i, carry):
             rows = tile_of(i, 64)
@@ -907,11 +916,11 @@
 
     for d in range(2):
         load_operands(d, 0)
-    for copy in embed_loads:
-        copy.start()
     pl.semaphore_wait(barrier, jnp.where(section == 0, 4, 3))
     for d in range(2):
         products(d, 0, functools.partial(load_operands, d, 1))
+    for copy in embed_loads:
+        copy.start()
     for d in range(2):
         part_copy(d, 0).wait_recv()
         for q in range(pieces):

time: 363 us -> 359 us (0.989)
  Pallas kernels: 361 us -> 357 us
where the time goes in v6:
time: 359 us; the launch traced here: 358 us
  Pallas kernels  357 us (99%)
    pallas_call x1, Pallas kernels, run_sums(): pl.pallas_call(functools.partial(sums_kernel, members), out_shape=(shaped...  178 us
    pallas_call x1, Pallas kernels, run_backward(): pl.pallas_call(backward_kernel, out_shape=(shaped(LOW, 5 + blocks, clips...  82.7 us
    pallas_call x1, Pallas kernels, run_forward(): pl.pallas_call(forward_kernel, out_shape=(shaped(LOW, 3 + blocks, clips *...  78.8 us
    pallas_call x1, Pallas kernels, run_finish(): pl.pallas_call(functools.partial(finish_kernel, blocks), out_shape=(shape...  17.4 us

profile of v6, /device:TPU:0, one launch (start us, length us, event | category | flops | bytes accessed | tf_op | source)
XLA Modules:
  0.0 358.2 jit_solution(1483700708129126411)
XLA Ops:
  0.6 78.8 %shard_map.246 = (bf16[7,1024,768]{2,1,0:T(8,128)(2,1)}, f32[2,512,768]{2,1,0:T(8,128)}, bf16[2,512,2304]{2,1,0:T(8,128)(2,1)}, bf16[2,12,512,512]{3,2,1,0:T(8,1...) custom-call(s32[2]{0:T(128)} %kinds.3, ...), custom_call_target="tpu_custom_call" | custom-call | tf_op jit(solution)/shard_map/pallas_call | solution.py:1200
  79.4 82.7 %shard_map.247 = (bf16[9,1024,768]{2,1,0:T(8,128)(2,1)}, bf16[2,512,768]{2,1,0:T(8,128)(2,1)}, bf16[7,768,1024]{2,1,0:T(8,128)(2,1)}, f32[8,768]{1,0:T(8,128)}, f32[1,3072]{1,0:T(1,128)}) custom-call(bf16[2,512,768]{2,1,0:T(8,128)(2,1)} %cot_h.1, bf16[1,768,2304]{2,1,0:T(8,128)(2,1)} %wqkv_h.3, bf16[1,768,768]{2,1,0:T(8,128)(2,1)} %wout_h.3, ...), custom_call_target="tpu_custom_call" | custom-call | tf_op jit(solution)/shard_map/pallas_call | solution.py:1245
  162.1 178.5 %shard_map.248 = (bf16[16,576,768]{2,1,0:T(8,128)(2,1)}, bf16[16,80,768]{2,1,0:T(8,128)(2,1)}, bf16[16,80,768]{2,1,0:T(8,128)(2,1)}, bf16[2,512,128]{2,1,0:T(8,128)(2,1)}) custom-call(s32[2]{0:T(128)} %kinds.3, bf16[7,768,1024]{2,1,0:T(8,128)(2,1)} %get-tuple-element.54.turned_h, bf16[9,1024,768]{2,1,0:T(8,128)(2,1)} %get-tuple-element.55.right_h, ...), custom_call_target="tpu_custom_call" | custom-call | tf_op jit(solution)/shard_map/pallas_call | solution.py:1291
  340.6 17.4 %shard_map.249 = (bf16[2,512,384]{2,1,0:T(8,128)(2,1)}, bf16[2,512,128]{2,1,0:T(8,128)(2,1)}, f32[512,768]{1,0:T(8,128)}, f32[512,768]{1,0:T(8,128)}, f32[768,23...) custom-call(bf16[16,576,768]{2,1,0:T(8,128)(2,1)} %get-tuple-element, ...), custom_call_target="tpu_custom_call" | custom-call | tf_op jit(solution)/shard_map/pallas_call | solution.py:1326

commit v7 on v6

--- a/solution.py
+++ b/solution.py
@@ -168,35 +168,6 @@
         after_first(0)
         after_first(1)
 
-        @pl.when(section == 0)
-        def _():
-            chosen[...] = pick_kind(kinds[c], embw[0], embw[1]).astype(low)
-            offset = pick_kind(kinds[c], embv[0:1, :], embv[1:2, :])
-
-            def tile(i, carry):
-                rows = tile_of(i, 128)
-                lifted = dot_nn(feat[c, rows, :], chosen[...]) + offset
-                hidden = cols[c, rows, :][:, 0:1]
-                x[rows, :] = jnp.where(hidden > 0.0, embv[2:3, :], lifted) + pos[rows, :]
-                return carry
-
-            loop(length // 128, tile, 4)
-
-        @pl.when(section == 1)
-        def _():
-            for h in range(2):
-                send_half(c, h).wait_recv()
-
-            def tile(i, carry):
-                rows = tile_of(i, 64)
-                x[rows, :] = landed[c, rows, :].astype(jnp.float32)
-                return carry
-
-            loop(length // 64, tile, 4)
-
-        own = saves(c)
-        own[0].start()
-
         def norm_rows(source, target, which, shift, first, count):
             gain, offset = gains[which : which + 1, :], vectors[shift]
 
@@ -210,7 +181,37 @@
 
             loop(count, lambda i, carry: tile(first + i, carry), 4)
 
-        norm_rows(x, normed, 0, 0, 0, length // 64)
+        @pl.when(section == 0)
+        def _():
+            chosen[...] = pick_kind(kinds[c], embw[0], embw[1]).astype(low)
+            offset = pick_kind(kinds[c], embv[0:1, :], embv[1:2, :])
+
+            def tile(i, carry):
+                rows = tile_of(i, 128)
+                lifted = dot_nn(feat[c, rows, :], chosen[...]) + offset
+                hidden = cols[c, rows, :][:, 0:1]
+                x[rows, :] = jnp.where(hidden > 0.0, embv[2:3, :], lifted) + pos[rows, :]
+                return carry
+
+            loop(length // 128, tile, 4)
+            norm_rows(x, normed, 0, 0, 0, length // 64)
+
+        @pl.when(section == 1)
+        def _():
+            def tile(i, carry):
+                rows = tile_of(i, 64)
+                x[rows, :] = landed[c, rows, :].astype(jnp.float32)
+                return carry
+
+            for h in range(2):
+                send_half(c, h).wait_recv()
+                first = h * (half // 64)
+                loop(half // 64, lambda i, carry, first=first: tile(first + i, carry), 4)
+                norm_rows(x, normed, 0, 0, first, half // 64)
+
+        own = saves(c)
+        own[0].start()
+
         own[1].start()
         after_first(2)
 
@@ -543,7 +544,7 @@
             small[7:8, :] += column_sum(grad_in)
             return carry
 
-        loop(length // 64, middle_tile, 4)
+        loop(length // 64, middle_tile, 8)
         own[3].start()
 
         @pl.when(c == 0)
@@ -830,7 +831,7 @@
             chunk[d, slot, core, at] = total.astype(low)
             return carry
 
-        loop(spans[q][1] // 16, add, 1)
+        loop(spans[q][1] // 16, add, 6 if spans[q][1] % 96 == 0 else 1)
         if end:
             hand_over(q, d)
         else:
@@ -919,12 +920,11 @@
     pl.semaphore_wait(barrier, jnp.where(section == 0, 4, 3))
     for d in range(2):
         products(d, 0, functools.partial(load_operands, d, 1))
-    for copy in embed_loads:
-        copy.start()
-    for d in range(2):
         part_copy(d, 0).wait_recv()
         for q in range(pieces):
             reduce_main(q, d, 0, begin=True)
+    for copy in embed_loads:
+        copy.start()
 
     def prefetch_after(d, s):
         @pl.when(s < n)

time: 359 us -> 357 us (level)
  no operation moved by 1% of the time
where the time goes in v7:
time: 357 us
  Pallas kernels  356 us (100%)
    pallas_call x1, Pallas kernels, run_sums(): pl.pallas_call(functools.partial(sums_kernel, members), out_shape=(shaped...  177 us
    pallas_call x1, Pallas kernels, run_backward(): pl.pallas_call(backward_kernel, out_shape=(shaped(LOW, 5 + blocks, clips...  82.6 us
    pallas_call x1, Pallas kernels, run_forward(): pl.pallas_call(forward_kernel, out_shape=(shaped(LOW, 3 + blocks, clips *...  78.3 us
    pallas_call x1, Pallas kernels, run_finish(): pl.pallas_call(functools.partial(finish_kernel, blocks), out_shape=(shape...  17.4 us

profile of v7, /device:TPU:0, one launch (start us, length us, event | category | flops | bytes accessed | tf_op | source)
XLA Modules:
  0.0 356.7 jit_solution(16694153379023650061)
XLA Ops:
  0.6 78.3 %shard_map.246 = (bf16[7,1024,768]{2,1,0:T(8,128)(2,1)}, f32[2,512,768]{2,1,0:T(8,128)}, bf16[2,512,2304]{2,1,0:T(8,128)(2,1)}, bf16[2,12,512,512]{3,2,1,0:T(8,1...) custom-call(s32[2]{0:T(128)} %kinds.3, ...), custom_call_target="tpu_custom_call" | custom-call | tf_op jit(solution)/shard_map/pallas_call | solution.py:1200
  78.9 82.6 %shard_map.247 = (bf16[9,1024,768]{2,1,0:T(8,128)(2,1)}, bf16[2,512,768]{2,1,0:T(8,128)(2,1)}, bf16[7,768,1024]{2,1,0:T(8,128)(2,1)}, f32[8,768]{1,0:T(8,128)}, f32[1,3072]{1,0:T(1,128)}) custom-call(bf16[2,512,768]{2,1,0:T(8,128)(2,1)} %cot_h.1, bf16[1,768,2304]{2,1,0:T(8,128)(2,1)} %wqkv_h.3, bf16[1,768,768]{2,1,0:T(8,128)(2,1)} %wout_h.3, ...), custom_call_target="tpu_custom_call" | custom-call | tf_op jit(solution)/shard_map/pallas_call | solution.py:1245
  161.6 177.5 %shard_map.248 = (bf16[16,576,768]{2,1,0:T(8,128)(2,1)}, bf16[16,80,768]{2,1,0:T(8,128)(2,1)}, bf16[16,80,768]{2,1,0:T(8,128)(2,1)}, bf16[2,512,128]{2,1,0:T(8,128)(2,1)}) custom-call(s32[2]{0:T(128)} %kinds.3, bf16[7,768,1024]{2,1,0:T(8,128)(2,1)} %get-tuple-element.54.turned_h, bf16[9,1024,768]{2,1,0:T(8,128)(2,1)} %get-tuple-element.55.right_h, ...), custom_call_target="tpu_custom_call" | custom-call | tf_op jit(solution)/shard_map/pallas_call | solution.py:1291
  339.0 17.4 %shard_map.249 = (bf16[2,512,384]{2,1,0:T(8,128)(2,1)}, bf16[2,512,128]{2,1,0:T(8,128)(2,1)}, f32[512,768]{1,0:T(8,128)}, f32[512,768]{1,0:T(8,128)}, f32[768,23...) custom-call(bf16[16,576,768]{2,1,0:T(8,128)(2,1)} %get-tuple-element, ...), custom_call_target="tpu_custom_call" | custom-call | tf_op jit(solution)/shard_map/pallas_call | solution.py:1326
